TPU v7x, 32 devices: a whole 2x2x4 slice. The times are simulated.
32 devices in a mesh: seq: 8 (over z, core), batch: 4 (over y, x).
Axes of the slice: x: 2, y: 2, z: 4, core: 2. Of those that a mesh axis runs over, the one named last changes fastest.
Arguments:
- tokens: bfloat16 [2, 8, 1024, 640], P(None, 'batch', 'seq'), may hold values from -6 to 6
- mask: int32 [2, 8, 1024], P(None, 'batch', 'seq'), may hold values from 0 to 1, as said below
- cotangent: bfloat16 [2, 8, 1024, 640], P(None, 'batch', 'seq'), may hold values from -6 to 6
- ln1_gain: float32 [640], replicated, may hold values from 0.1 to 1.9
- ln1_bias: float32 [640], replicated, may hold values from -1.75 to 1.75
- qkv_weight: bfloat16 [640, 1920], replicated, may hold values from -0.25 to 0.25
- q_bias: float32 [640], replicated, may hold values from -3 to 3
- v_bias: float32 [640], replicated, may hold values from -3 to 3
- out_weight: bfloat16 [640, 640], replicated, may hold values from -4 to 4
- out_bias: float32 [640], replicated, may hold values from -1.75 to 1.75
- ln2_gain: float32 [640], replicated, may hold values from 0.1 to 1.9
- ln2_bias: float32 [640], replicated, may hold values from -1.75 to 1.75
- up_weight: bfloat16 [640, 5120], replicated, may hold values from -0.25 to 0.25
- up_bias: float32 [5120], replicated, may hold values from -3 to 3
- down_weight: bfloat16 [5120, 640], replicated, may hold values from -0.078125 to 0.078125
- down_bias: float32 [640], replicated, may hold values from -1.75 to 1.75
Outputs:
- out: bfloat16 [2, 8, 1024, 640], P(None, 'batch', 'seq')
- grad_in: bfloat16 [2, 8, 1024, 640], P(None, 'batch', 'seq')
- ln1_gain_grad: float32 [640], replicated
- ln1_bias_grad: float32 [640], replicated
- qkv_weight_grad: float32 [640, 1920], P('seq', 'batch')
- q_bias_grad: float32 [640], replicated
- v_bias_grad: float32 [640], replicated
- out_weight_grad: float32 [640, 640], P('seq', 'batch')
- out_bias_grad: float32 [640], replicated
- ln2_gain_grad: float32 [640], replicated
- ln2_bias_grad: float32 [640], replicated
- up_weight_grad: float32 [640, 5120], P('seq', 'batch')
- up_bias_grad: float32 [5120], replicated
- down_weight_grad: float32 [5120, 640], P('seq', 'batch')
- down_bias_grad: float32 [640], replicated
Inputs may be any that keep to these rules, and one draw needn't show every extreme that they name: `mask`: 1 marks a masked position; every sequence has one or more.
All inputs are finite; a program needn't handle non-finite values.
Results may differ from a plain program's by a relative error of at most 0.017.
Values may be sent and summed in bfloat16 or wider, within the bound.
No kernel may reach another device: no remote copies, remote signals or barrier semaphores. Data moves between devices by JAX's collectives and lax.ppermute only.
A program may use at most 192 MiB of HBM per device.

v0:
```python
import jax
import jax.numpy as jnp
from jax import lax
from jax.experimental import pallas as pl
from jax.experimental.pallas import tpu as pltpu
from jax.sharding import PartitionSpec as P

HEADS = 20
EPS = 1e-05
LOG2E = 1.4426950408889634
ROWS = 256
F32 = jnp.float32
BF16 = jnp.bfloat16
LANES = 128


def dot(left, right):
    return jnp.dot(left, right, preferred_element_type=F32)


def dot_nt(left, right):
    return lax.dot_general(left, right, (((1,), (1,)), ((), ())), preferred_element_type=F32)


def norm_rows(rows_in):
    mean_val = jnp.mean(rows_in, axis=-1, keepdims=True)
    centered = rows_in - mean_val
    inv_std = lax.rsqrt(jnp.mean(centered * centered, axis=-1, keepdims=True) + EPS)
    return centered * inv_std, inv_std


def norm_back(scaled, normed, inv_std):
    inner = (
        scaled
        - jnp.mean(scaled, axis=-1, keepdims=True)
        - normed * jnp.mean(scaled * normed, axis=-1, keepdims=True)
    )
    return inner * inv_std


def params_of(mib):
    return pltpu.CompilerParams(vmem_limit_bytes=mib * 1024 * 1024)


def cost(flops, moved, trans=0, part=1):
    return pl.CostEstimate(
        flops=flops // part, bytes_accessed=moved // part, transcendentals=trans // part
    )


def sds(shape, dtype):
    return jax.ShapeDtypeStruct(shape, dtype)


VMEM = pl.BlockSpec(memory_space=pltpu.VMEM)
ANY = pl.BlockSpec(memory_space=pl.ANY)
HBM = pl.BlockSpec(memory_space=pltpu.HBM)


def run(body, operands, after=(), in_specs=None, out_specs=None, vmem=32, **more):
    count, extra = len(operands), len(after)

    def inner(*refs):
        body(*refs[:count], *refs[count + extra :])

    specs = [VMEM] * count if in_specs is None else list(in_specs)
    shapes = more["out_shape"]
    if out_specs is None:
        out_specs = [VMEM] * len(shapes) if isinstance(shapes, (list, tuple)) else VMEM
    return pl.pallas_call(
        inner,
        in_specs=specs + [ANY] * extra,
        out_specs=out_specs,
        compiler_params=params_of(vmem),
        **more,
    )(*operands, *after)


def far(item):
    return pltpu.with_memory_space_constraint(item, pltpu.HBM)


def gate(items, after):
    def body(*refs):
        del refs

    return pl.pallas_call(
        body,
        in_specs=[ANY] * (len(items) + len(after)),
        out_specs=[ANY] * len(items),
        out_shape=[sds(item.shape, item.dtype) for item in items],
        input_output_aliases={n: n for n in range(len(items))},
        cost_estimate=cost(0, 0),
        name="gate",
    )(*items, *after)


def place(group):
    spot = lax.axis_index("seq")
    return spot, lax.rem(spot, group), lax.div(spot, group)


def deal(item, group, after=()):
    count, rows, width = item.shape

    def body(in_ref, *out_refs):
        _, _, quad = place(group)
        for d in range(count):
            out_refs[d][...] = in_ref[quad ^ d]

    return run(
        body,
        [item],
        after,
        out_shape=[sds((rows, width), item.dtype)] * count,
        vmem=6,
        cost_estimate=cost(0, 4 * count * rows * width),
        name="deal",
    )


def collect(pieces, group, after):
    count = len(pieces)
    rows, width = pieces[0].shape

    def body(*refs):
        _, _, quad = place(group)
        for d in range(count):
            refs[count][quad ^ d] = refs[d][...]

    return run(
        body,
        pieces,
        after,
        out_shape=sds((count, rows, width), pieces[0].dtype),
        vmem=6,
        cost_estimate=cost(0, 4 * count * rows * width),
        name="collect",
    )


def stack(pieces, after):
    count = len(pieces)

    def body(*refs):
        for d in range(count):
            refs[count][d] = refs[d][...]

    return run(
        body,
        pieces,
        after,
        out_shape=sds((count,) + pieces[0].shape, pieces[0].dtype),
        vmem=12,
        cost_estimate=cost(0, 4 * count * pieces[0].size),
        name="stack",
    )


def swap(item, axis, size, distance):
    return lax.ppermute(item, axis, [(i, i ^ distance) for i in range(size)])


def over_quads(pieces, group):
    return [
        piece if d == 0 else swap(piece, "seq", len(pieces) * group, d * group)
        for d, piece in enumerate(pieces)
    ]


def pick_weights(qkv_weight, qkv_bias, out_weight, group, real, wide):
    width = qkv_weight.shape[0]
    tiles = wide // LANES

    def body(w_ref, b_ref, o_ref, wo_ref, bo_ref, *out_refs):
        _, part, _ = place(group)
        wo_ref[...] = jnp.zeros_like(wo_ref)
        bo_ref[...] = jnp.zeros_like(bo_ref)
        for ref in out_refs:
            ref[...] = jnp.zeros_like(ref)
        for c in range(group):

            @pl.when(part == c)
            def _(c=c):
                for p in range(3):
                    for t in range(tiles):
                        some = min(LANES, real - t * LANES)
                        src = p * width + c * real + t * LANES
                        dst = (3 * t + p) * LANES
                        wo_ref[:, dst : dst + some] = w_ref[:, src : src + some]
                        bo_ref[:, dst : dst + some] = b_ref[:, src : src + some]
                for n in range(group):
                    src = (c + n) % group * real
                    out_refs[n][0:real, :] = o_ref[src : src + real, :]

    return pl.pallas_call(
        body,
        out_shape=[sds((width, 3 * wide), BF16), sds((1, 3 * wide), F32)]
        + [sds((wide, width), BF16)] * group,
        compiler_params=params_of(24),
        cost_estimate=cost(0, 8 * 1024 * 1024),
        name="pick_weights",
    )(qkv_weight, qkv_bias, out_weight)


def by_pairs(live, visit):
    size = 2 if live % 2 == 0 else 1

    @pl.loop(0, live // size)
    def _(i):
        visit([i * size + e for e in range(size)])


def attend_tiles(query_at, keys_at, vals_at, att_ref, lse_ref, keys, vals, acc, tiles, heads, head_dim):
    per_tile = LANES // head_dim
    total = att_ref.shape[0]
    exp_scale = head_dim ** (-0.5) * LOG2E
    lane = lax.broadcasted_iota(jnp.int32, (1, LANES), 1)
    row = lax.broadcasted_iota(jnp.int32, (LANES, 1), 0)
    lse_ref[...] = jnp.zeros_like(lse_ref)
    vals[:, :, LANES:] = jnp.ones((per_tile, total, LANES), BF16)
    for n, t in enumerate(tiles):
        live = min(per_tile, heads - t * per_tile)
        key_t = keys_at(n).astype(F32).T
        val_f = vals_at(n).astype(F32)
        for j in range(live):
            keys[j] = jnp.where(row // head_dim == j, key_t, 0.0).astype(BF16)
            vals[j, :, :LANES] = jnp.where(lane // head_dim == j, val_f, 0.0).astype(BF16)
        acc[...] = jnp.zeros_like(acc)

        def visit(some, n=n):
            scores = [dot(query_at(n), keys[j]) for j in some]
            for item, j in zip(scores, some):
                row_max = jnp.max(item, axis=-1, keepdims=True) * exp_scale
                expd = jnp.exp2(item * exp_scale - row_max).astype(BF16)
                mixed = dot(expd, vals[j])
                den = mixed[:, LANES:]
                acc[...] += mixed[:, :LANES] / den
                lse_ref[...] = jnp.where(
                    lane == n * per_tile + j, row_max + jnp.log2(den), lse_ref[...]
                )

        by_pairs(live, visit)
        att_ref[:, n * LANES : (n + 1) * LANES] = acc[...].astype(BF16)


def attend_scratch(total, head_dim):
    per_tile = LANES // head_dim
    return [
        pltpu.VMEM((per_tile, LANES, total), BF16),
        pltpu.VMEM((per_tile, total, 2 * LANES), BF16),
        pltpu.VMEM((total, LANES), F32),
    ]


def attend_first(x_pieces, gain, shift, weight, bias, tiles, heads, head_dim):
    count = len(x_pieces)
    piece_rows, width = x_pieces[0].shape
    total = count * piece_rows
    cols_all = weight.shape[1]

    def body(*refs):
        x_refs = refs[:count]
        gain_ref, shift_ref, w_ref, bias_ref = refs[count : count + 4]
        x_ref, qkv_ref, att_ref, lse_ref, keys, vals, acc = refs[count + 4 :]
        for n in range(count):
            x_ref[n * piece_rows : (n + 1) * piece_rows, :] = x_refs[n][...]

        @pl.loop(0, total // ROWS)
        def _(i):
            rows = pl.ds(pl.multiple_of(i * ROWS, ROWS), ROWS)
            normed, _ = norm_rows(x_ref[rows, :].astype(F32))
            low = (normed * gain_ref[...] + shift_ref[...]).astype(BF16)
            qkv_ref[rows, :] = (dot(low, w_ref[...]) + bias_ref[...]).astype(BF16)

        def columns(at):
            return slice(at * LANES, (at + 1) * LANES)

        attend_tiles(
            lambda n: qkv_ref[:, columns(3 * n)],
            lambda n: qkv_ref[:, columns(3 * n + 1)],
            lambda n: qkv_ref[:, columns(3 * n + 2)],
            att_ref,
            lse_ref,
            keys,
            vals,
            acc,
            range(tiles),
            heads,
            head_dim,
        )

    return run(
        body,
        [*x_pieces, gain, shift, weight, bias],
        out_shape=[
            sds((total, width), BF16),
            sds((total, cols_all), BF16),
            sds((total, tiles * LANES), BF16),
            sds((total, LANES), F32),
        ],
        scratch_shapes=attend_scratch(total, head_dim),
        vmem=23,
        cost_estimate=cost(
            2 * total * width * cols_all + 4 * heads * total * total * 256,
            8 * 1024 * 1024,
            heads * total * total,
        ),
        name="attend_first",
    )


def attend_last(qkv, tile, heads, head_dim, after):
    total = qkv.shape[0]

    def body(qkv_ref, att_ref, lse_ref, keys, vals, acc):
        attend_tiles(
            lambda n: qkv_ref[:, 0:LANES],
            lambda n: qkv_ref[:, LANES : 2 * LANES],
            lambda n: qkv_ref[:, 2 * LANES : 3 * LANES],
            att_ref,
            lse_ref,
            keys,
            vals,
            acc,
            [tile],
            heads,
            head_dim,
        )

    live = heads - tile * (LANES // head_dim)
    return run(
        body,
        [qkv],
        after,
        grid=(1,),
        in_specs=[pl.BlockSpec((total, 3 * LANES), lambda i: (0, tile))],
        out_specs=[pl.BlockSpec((total, LANES), lambda i: (0, 0))] * 2,
        out_shape=[sds((total, LANES), BF16), sds((total, LANES), F32)],
        scratch_shapes=attend_scratch(total, head_dim),
        vmem=14,
        cost_estimate=cost(4 * live * total * total * 256, 2 * 1024 * 1024, live * total * total),
        name="attend_last",
    )


def gelu_parts(value):
    size = jnp.abs(value)
    near = pl.reciprocal(1.0 + (0.3275911 * 0.7071067811865476) * size, approx=True)
    bell = jnp.exp2(value * value * (-0.5 * LOG2E))
    poly = near * (
        0.5 * 0.254829592
        + near
        * (
            0.5 * -0.284496736
            + near * (0.5 * 1.421413741 + near * (0.5 * -1.453152027 + near * (0.5 * 1.061405429)))
        )
    )
    tail = poly * bell
    area = jnp.where(value < 0.0, tail, 1.0 - tail)
    return value * area, area + value * bell * 0.3989422804014327


class Units:
    def __init__(self, block, blocks, start, size, stride, quads, high):
        self.block, self.blocks, self.start, self.size = block, blocks, start, size
        self.stride, self.quads, self.high = stride, quads, high
        self.count = blocks * size
        self.chunk = 512 if self.count % 512 == 0 else 256
        self.packed = quads is not None

    def loads(self, part, hbm_up, hbm_down, hbm_bias, up_ref, down_ref, bias_ref, sem):
        copies = []
        for b in range(self.blocks):
            src = self.start
            if self.packed:
                src = pl.multiple_of((b * self.stride + part) * self.block, LANES) + self.start
            src = pl.ds(src, self.size)
            dst = pl.ds(b * self.size, self.size)
            copies.append(
                pltpu.make_async_copy(hbm_up.at[:, src], up_ref.at[:, dst], sem.at[2 * b])
            )
            copies.append(
                pltpu.make_async_copy(hbm_down.at[src, :], down_ref.at[dst, :], sem.at[2 * b + 1])
            )
            bias_ref[0:1, dst] = hbm_bias[:, src]
        return copies

    def grad_shapes(self, width):
        if self.packed:
            return [pltpu.HBM((2, self.quads, self.high, self.size), BF16)] * 4
        return [sds((width, self.count), BF16)] * 2

    def scratch(self, total, width):
        grads = (self.blocks, self.quads, self.high, self.size) if self.packed else (8, LANES)
        return [
            pltpu.VMEM(grads, BF16),
            pltpu.VMEM(grads, BF16),
            pltpu.SemaphoreType.DMA((8,)),
            pltpu.VMEM((total, self.count), BF16),
            pltpu.VMEM((total, self.count), BF16),
            pltpu.VMEM((width, self.count), BF16),
            pltpu.VMEM((self.count, width), BF16),
            pltpu.VMEM((8, self.count), F32),
            pltpu.SemaphoreType.DMA((2 * self.blocks,)),
        ]

    def compute(self, part, second, second_t, grad, grad_t, acc, gs, ubg, scratch, outs):
        up_slots, down_slots, out_sem, acts, grad_pres, up_ref, down_ref, bias_ref, _ = scratch
        if not self.packed:
            up_slots, down_slots = outs
        quad = lax.div(lax.axis_index("seq"), self.stride)
        mine = lax.axis_index("batch")

        def enter(i):
            rows = slice(i * ROWS, (i + 1) * ROWS)
            pre = dot(second[rows, :], up_ref[...]) + bias_ref[0:1, :]
            return pre, dot_nt(grad[rows, :], down_ref[...])

        def weights(n):
            first, last = n * self.chunk, (n + 1) * self.chunk
            up_grad = dot(second_t[...], grad_pres[:, first:last]).astype(BF16)
            down_grad = dot(grad_t[...], acts[:, first:last]).astype(BF16)
            if not self.packed:
                up_slots[:, first:last] = up_grad
                down_slots[:, first:last] = down_grad
                return
            at = first
            while at < last:
                block = at // self.size
                stop = min(last, (block + 1) * self.size)
                src = slice(at - first, stop - first)
                dst = slice(at - block * self.size, stop - block * self.size)
                for m in range(self.blocks):
                    rows = slice(m * self.high, (m + 1) * self.high)
                    up_slots[block ^ mine, m ^ quad, :, dst] = up_grad[rows, src]
                    down_slots[m ^ mine, block ^ quad, :, dst] = down_grad[rows, src]
                at = stop

        ready = enter(0)
        chunks = second.shape[0] // ROWS
        for i in range(chunks):
            ahead = enter(i + 1) if i + 1 < chunks else None
            rows = slice(i * ROWS, (i + 1) * ROWS)
            pre, grad_act = ready
            value, slope = gelu_parts(pre)
            act = value.astype(BF16)
            grad_pre = (grad_act * slope).astype(BF16)
            acts[rows, :] = act
            grad_pres[rows, :] = grad_pre
            ubg[0:1, :] += jnp.sum(grad_pre.astype(F32), axis=0, keepdims=True)
            acc[rows, :] += dot(act, down_ref[...])
            gs[rows, :] += dot_nt(grad_pre, up_ref[...])
            ready = ahead
        for n in range(self.count // self.chunk):
            weights(n)
        stores = []
        if self.packed:
            order = ((up_slots, (0, 2)), (up_slots, (1, 3)), (down_slots, (0, 1)), (down_slots, (2, 3)))
            for m, (source, slots) in enumerate(order):
                for n in range(2):
                    stores.append(
                        pltpu.make_async_copy(
                            source.at[slots[n]], outs[m].at[n], out_sem.at[2 * m + n]
                        )
                    )
        return stores


def feed_first(
    rows_all, att_first, att_last, cot_pieces, out_w, out_b, gain, shift, up, up_b, down, down_b, units
):
    pieces = len(att_first)
    total, width = rows_all.shape
    piece_rows = total // pieces
    count = len(cot_pieces)
    cot_rows = total // count
    split = att_first[0].shape[1]
    grads = units.grad_shapes(width)

    def body(*refs):
        x_ref, refs = refs[0], refs[1:]
        att_refs, refs = refs[: 2 * pieces], refs[2 * pieces :]
        cot_refs, refs = refs[:count], refs[count:]
        wo_refs, refs = refs[:pieces], refs[pieces:]
        ob_ref, gain_ref, shift_ref, up_hbm, ub_ref, down_hbm, db_ref = refs[:7]
        mid_ref, second, second_t, grad, grad_t, own_ref, low_ref, ubg, refs = *refs[7:15], refs[15:]
        send_refs, refs = refs[: pieces - 1], refs[pieces - 1 :]
        outs, refs = refs[: len(grads)], refs[len(grads) :]
        acc, gs, mid_rows, mid_sem, *scratch = refs
        _, part, _ = place(pieces)
        loads = units.loads(part, up_hbm, down_hbm, ub_ref, *scratch[5:])
        for load in loads:
            load.start()
        ubg[...] = jnp.zeros_like(ubg)
        masked = jnp.zeros((1, width), F32)
        for ref in cot_refs:
            masked = masked + ref[cot_rows : cot_rows + 1, :].astype(F32)
        factor = total / (4.0 * masked)
        for n in range(count):
            scaled = cot_refs[n][0:cot_rows, :].astype(F32) * factor
            dst = slice(n * cot_rows, (n + 1) * cot_rows)
            grad[dst, :] = scaled.astype(BF16)

        for h in range(pieces):

            @pl.loop(0, piece_rows // ROWS)
            def _(i, h=h):
                at = pl.multiple_of(i * ROWS, ROWS)
                dst = pl.ds(h * piece_rows + at, ROWS)
                mid = x_ref[dst, :].astype(F32) + ob_ref[...]
                for n in range(pieces):
                    src = pl.ds(((h - n) % pieces) * piece_rows + at, ROWS)
                    mid = mid + dot(att_refs[2 * n][src, :], wo_refs[n][0:split, :])
                    mid = mid + dot(att_refs[2 * n + 1][src, :], wo_refs[n][split:, :])
                mid_rows[dst, :] = mid
                normed, _ = norm_rows(mid)
                low = normed * gain_ref[...] + shift_ref[...]
                second[dst, :] = low.astype(BF16)
                second_t[:, dst] = low.T.astype(BF16)
                grad_t[:, dst] = grad[dst, :].astype(F32).T.astype(BF16)
                acc[dst, :] = mid + db_ref[...] if h == 0 else jnp.zeros((ROWS, width), F32)
                gs[dst, :] = jnp.zeros((ROWS, width), F32)

        keep_mid = pltpu.make_async_copy(mid_rows, mid_ref, mid_sem)
        keep_mid.start()
        for load in loads:
            load.wait()
        stores = units.compute(
            part, second, second_t, grad, grad_t, acc, gs, ubg, scratch, outs
        )
        for store in stores:
            store.start()
        keep_mid.wait()
        own_ref[...] = acc[0:piece_rows, :]
        low_ref[...] = gs[...].astype(BF16)
        for h in range(1, pieces):
            send_refs[h - 1][...] = acc[h * piece_rows : (h + 1) * piece_rows, :].astype(BF16)
        for store in stores:
            store.wait()

    att_all = [item for pair in zip(att_first, att_last) for item in pair]
    turned = sds((width, total), BF16)
    flat = sds((total, width), BF16)
    half = sds((piece_rows, width), F32)
    return run(
        body,
        [
            rows_all,
            *att_all,
            *cot_pieces,
            *out_w,
            out_b,
            gain,
            shift,
            far(up),
            up_b,
            far(down),
            down_b,
        ],
        in_specs=[VMEM] * (1 + 3 * pieces + count) + [VMEM, VMEM, VMEM, HBM, VMEM, HBM, VMEM],
        out_specs=[HBM] + [VMEM] * (6 + pieces) + [HBM if units.packed else VMEM] * len(grads),
        out_shape=[pltpu.HBM((total, width), F32), flat, turned, flat, turned, half, flat, sds((8, units.count), F32)]
        + [sds((piece_rows, width), BF16)] * (pieces - 1)
        + grads,
        scratch_shapes=[pltpu.VMEM((total, width), F32)] * 3
        + [pltpu.SemaphoreType.DMA]
        + units.scratch(total, width),
        vmem=26,
        cost_estimate=cost(12 * total * width * units.count, 24 * 1024 * 1024, total * units.count),
        name="feed_first",
    )


def feed_second(second, second_t, grad, grad_t, own_first, low_first, sends, up, up_b, down, units):
    pieces = 1 + len(sends)
    total, width = second.shape
    piece_rows = total // pieces
    grads = units.grad_shapes(width)

    def body(*refs):
        second, second_t, grad, grad_t, own_in, low_in, up_hbm, ub_ref, down_hbm, refs = (
            *refs[:9],
            refs[9:],
        )
        send_ins, refs = refs[: pieces - 1], refs[pieces - 1 :]
        own_ref, low_ref, ubg, refs = refs[0], refs[1], refs[2], refs[3:]
        send_refs, refs = refs[: pieces - 1], refs[pieces - 1 :]
        outs, (acc, gs), scratch = refs[: len(grads)], refs[len(grads) :][:2], refs[len(grads) + 2 :]
        _, part, _ = place(pieces)
        loads = units.loads(part, up_hbm, down_hbm, ub_ref, *scratch[5:])
        for load in loads:
            load.start()
        ubg[...] = jnp.zeros_like(ubg)
        acc[...] = jnp.zeros_like(acc)
        gs[...] = jnp.zeros_like(gs)
        for load in loads:
            load.wait()
        stores = units.compute(
            part, second, second_t, grad, grad_t, acc, gs, ubg, scratch, outs
        )
        for store in stores:
            store.start()
        low_ref[...] = (gs[...] + low_in[...].astype(F32)).astype(BF16)
        own_ref[...] = acc[0:piece_rows, :] + own_in[...]
        for h in range(1, pieces):
            item = acc[h * piece_rows : (h + 1) * piece_rows, :] + send_ins[h - 1][...].astype(F32)
            send_refs[h - 1][...] = item.astype(BF16)
        for store in stores:
            store.wait()

    return run(
        body,
        [
            second,
            second_t,
            grad,
            grad_t,
            own_first,
            low_first,
            far(up),
            up_b,
            far(down),
            *sends,
        ],
        in_specs=[VMEM] * 6 + [HBM, VMEM, HBM] + [VMEM] * (pieces - 1),
        out_specs=[VMEM] * (2 + pieces) + [HBM if units.packed else VMEM] * len(grads),
        out_shape=[
            sds((piece_rows, width), F32),
            sds((total, width), BF16),
            sds((8, units.count), F32),
        ]
        + [sds((piece_rows, width), BF16)] * (pieces - 1)
        + grads,
        scratch_shapes=[pltpu.VMEM((total, width), F32)] * 2 + units.scratch(total, width),
        vmem=30,
        cost_estimate=cost(12 * total * width * units.count, 24 * 1024 * 1024, total * units.count),
        name="feed_second",
    )


def mid_back(mid, grad_second, received, grad_rows, gain, out_w, att_first, att_last, chunk):
    pieces = 1 + len(received)
    total, width = mid.shape
    per_piece = total // pieces // ROWS
    split = att_first.shape[1]
    wide = split + att_last.shape[1]
    steps = total // ROWS

    def body(*refs):
        mid_ref, gs_ref, refs = refs[0], refs[1], refs[2:]
        recv_refs, refs = refs[: pieces - 1], refs[pieces - 1 :]
        go_ref, gain_ref, wo_ref, att_ref, last_ref = refs[:5]
        gm_ref, do_ref, sums_ref, *dwo_refs, acc = refs[5:]
        i = pl.program_id(0)

        @pl.when(i == 0)
        def _():
            sums_ref[...] = jnp.zeros_like(sums_ref)
            acc[...] = jnp.zeros_like(acc)

        normed, inv_std = norm_rows(mid_ref[...])
        grad = gs_ref[...].astype(F32)
        for ref in recv_refs:
            grad = grad + ref[...].astype(F32)
        go = go_ref[...].astype(F32)
        grad_mid = go + norm_back(grad * gain_ref[...], normed, inv_std)
        low = grad_mid.astype(BF16)
        do_ref[...] = dot_nt(low, wo_ref[...]).astype(BF16)
        acc[0:split, :] += dot(att_ref[...].astype(F32).T.astype(BF16), low)
        acc[split:, :] += dot(last_ref[...].astype(F32).T.astype(BF16), low)

        @pl.when(i < per_piece)
        def _():
            gm_ref[...] = grad_mid
            for n, item in enumerate((grad * normed, grad, low.astype(F32), go)):
                sums_ref[n : n + 1, :] += jnp.sum(item, axis=0, keepdims=True)

        @pl.when(i == steps - 1)
        def _():
            if chunk == 0:
                dwo_refs[0][...] = acc[...].astype(BF16)
                return
            _, part, _ = place(pieces)
            for c in range(pieces):

                @pl.when(part == c)
                def _(c=c):
                    for n in range(dwo_refs[0].shape[0]):
                        for e in range(pieces):
                            at = (n * pieces + (c + e) % pieces) * chunk
                            dwo_refs[e][n] = acc[at : at + chunk, :].astype(BF16)

    def rows_of(columns):
        return pl.BlockSpec((ROWS, columns), lambda i: (i, 0))

    def theirs(n):
        def index(i):
            piece = lax.rem(lax.div(i, per_piece) + pieces - n, pieces)
            return piece * per_piece + lax.rem(i, per_piece), 0

        return pl.BlockSpec((ROWS, width), index)

    def whole(*shape):
        return pl.BlockSpec(shape, lambda i: (0,) * len(shape))

    if chunk == 0:
        grads = [((wide, width), sds((wide, width), BF16))]
    else:
        shape = (width // (pieces * pieces * chunk), chunk, width)
        grads = [(shape, pltpu.HBM(shape, BF16))] * pieces
    return run(
        body,
        [
            far(mid),
            far(grad_second),
            *received,
            far(grad_rows),
            gain,
            out_w,
            far(att_first),
            far(att_last),
        ],
        grid=(steps,),
        in_specs=[rows_of(width), rows_of(width)]
        + [theirs(n) for n in range(1, pieces)]
        + [rows_of(width), whole(1, width), whole(wide, width), rows_of(split), rows_of(wide - split)],
        out_specs=[
            pl.BlockSpec((ROWS, width), lambda i: (jnp.minimum(i, per_piece - 1), 0)),
            rows_of(wide),
            whole(8, width),
        ]
        + [whole(*shape) for shape, _ in grads],
        out_shape=[
            sds((per_piece * ROWS, width), F32),
            sds((total, wide), BF16),
            sds((8, width), F32),
        ]
        + [item for _, item in grads],
        scratch_shapes=[pltpu.VMEM((wide, width), F32)],
        vmem=16,
        cost_estimate=cost(4 * total * width * wide, 14 * 1024 * 1024),
        name="mid_back",
    )


def attend_backward(
    qkv, grad_att, att, att_tile, logs, lane_first, tile, heads, head_dim, after=(), part=1
):
    total = qkv.shape[0]
    per_tile = LANES // head_dim
    live = min(per_tile, heads - tile * per_tile)
    scale = head_dim ** (-0.5)
    exp_scale = scale * LOG2E

    def body(qkv_ref, do_ref, att_ref, lse_ref, out_ref, *scratch):
        km, vm, qm, dm, key_t, query_t, do_t, dq_t, lse_t, mean_t = scratch
        lane = lax.broadcasted_iota(jnp.int32, (1, LANES), 1)
        lse_t[...] = lse_ref[...].T
        query = qkv_ref[:, 0:LANES].astype(F32)
        key = qkv_ref[:, LANES : 2 * LANES].astype(F32)
        val = qkv_ref[:, 2 * LANES : 3 * LANES].astype(F32)
        upstream = do_ref[...].astype(F32)
        both_t = (upstream * att_ref[...].astype(F32)).T
        for j in range(live):
            mean_t[j : j + 1, :] = jnp.sum(
                both_t[j * head_dim : (j + 1) * head_dim, :], axis=0, keepdims=True
            )
        query_t[...] = query.T.astype(BF16)
        do_t[...] = upstream.T.astype(BF16)
        key_t[...] = key.T.astype(BF16)
        for j in range(live):
            mine = lane // head_dim == j
            km[j] = jnp.where(mine, key, 0.0).astype(BF16)
            vm[j] = jnp.where(mine, val, 0.0).astype(BF16)
            qm[j] = jnp.where(mine, query, 0.0).astype(BF16)
            dm[j] = jnp.where(mine, upstream, 0.0).astype(BF16)
        dq_t[...] = jnp.zeros_like(dq_t)

        @pl.loop(0, total // ROWS)
        def _(i):
            rows = pl.ds(pl.multiple_of(i * ROWS, ROWS), ROWS)
            grad_key = jnp.zeros((ROWS, LANES), F32)
            grad_val = jnp.zeros((ROWS, LANES), F32)

            def enter(j):
                return dot(km[j, rows, :], query_t[...]), dot(vm[j, rows, :], do_t[...])

            ready = enter(0)
            for j in range(live):
                ahead = enter(j + 1) if j + 1 < live else None
                scores, grad_prob = ready
                head = lane_first + j
                own = slice(j * head_dim, (j + 1) * head_dim)
                probs = jnp.exp2(scores * exp_scale - lse_t[head : head + 1, :])
                grad_scores = (probs * (grad_prob - mean_t[j : j + 1, :])).astype(BF16)
                grad_val = grad_val + dot(probs.astype(BF16), dm[j])
                grad_key = grad_key + dot(grad_scores, qm[j])
                dq_t[own, :] += dot(key_t[own, rows], grad_scores)
                ready = ahead
            out_ref[rows, LANES : 2 * LANES] = (grad_key * scale).astype(BF16)
            out_ref[rows, 2 * LANES : 3 * LANES] = grad_val.astype(BF16)

        out_ref[:, 0:LANES] = (dq_t[...].T * scale).astype(BF16)

    masked = pltpu.VMEM((live, total, LANES), BF16)
    turned = pltpu.VMEM((LANES, total), BF16)
    turned_f = pltpu.VMEM((LANES, total), F32)
    return run(
        body,
        [qkv, grad_att, att, logs],
        after,
        grid=(1,),
        in_specs=[
            pl.BlockSpec((total, 3 * LANES), lambda i: (0, tile)),
            pl.BlockSpec((total, LANES), lambda i: (0, tile)),
            pl.BlockSpec((total, LANES), lambda i: (0, att_tile)),
            pl.BlockSpec((total, LANES), lambda i: (0, 0)),
        ],
        out_specs=pl.BlockSpec((total, 3 * LANES), lambda i: (0, 0)),
        out_shape=sds((total, 3 * LANES), BF16),
        scratch_shapes=[masked] * 4
        + [turned] * 3
        + [turned_f] * 2
        + [pltpu.VMEM((8, total), F32)],
        vmem=17,
        cost_estimate=cost(
            2 * live * total * total * 256 * 5, 3 * 1024 * 1024, live * total * total, part
        ),
        name="attend_backward",
    )


def project_weights(rows_all, gain, shift, grad_tiles, pieces, quads, packed, after):
    total, width = rows_all.shape
    tiles = len(grad_tiles)
    tile_cols = grad_tiles[0].shape[1]
    cols_all = tiles * tile_cols
    chunk = width // (quads * pieces)

    def body(*refs):
        x_ref, gain_ref, shift_ref, refs = refs[0], refs[1], refs[2], refs[3:]
        dq_refs, (*dw_refs, low_t, part_ref) = refs[:tiles], refs[tiles:]
        _, part, quad = place(pieces)

        @pl.loop(0, total // ROWS)
        def _(i):
            rows = pl.ds(pl.multiple_of(i * ROWS, ROWS), ROWS)
            normed, _ = norm_rows(x_ref[rows, :].astype(F32))
            low_t[:, rows] = (normed * gain_ref[...] + shift_ref[...]).T.astype(BF16)

        for t in range(tiles):
            cols = slice(t * tile_cols, (t + 1) * tile_cols)
            part_ref[...] = dot(low_t[...], dq_refs[t][...]).astype(BF16)
            if not packed:
                dw_refs[0][:, cols] = part_ref[...]
                continue
            for c in range(pieces):

                @pl.when(part == c)
                def _(c=c, cols=cols):
                    for q in range(quads):
                        for e in range(pieces):
                            at = (q * pieces + (c + e) % pieces) * chunk
                            dw_refs[e][q ^ quad, :, cols] = part_ref[at : at + chunk, :]

    if packed:
        grads = [sds((quads, chunk, cols_all), BF16)] * pieces
    else:
        grads = [sds((width, cols_all), BF16)]
    return run(
        body,
        [rows_all, gain, shift, *grad_tiles],
        after,
        out_shape=grads,
        scratch_shapes=[pltpu.VMEM((width, total), BF16), pltpu.VMEM((width, tile_cols), BF16)],
        vmem=12,
        cost_estimate=cost(2 * total * width * cols_all, 6 * 1024 * 1024),
        name="project_weights",
    )


def project_rows(
    rows_all, weight, grad_tiles, sums_mid, up_sums, pieces, quads, packed, real, after
):
    total, width = rows_all.shape
    piece_rows = total // pieces
    cols_all = weight.shape[1]
    tiles = len(grad_tiles)
    tile_cols = cols_all // tiles

    def body(*refs):
        x_ref, w_ref, mid_ref, refs = *refs[:3], refs[3:]
        ups_refs, refs = refs[: len(up_sums)], refs[len(up_sums) :]
        dq_refs, refs = refs[:tiles], refs[tiles:]
        own_ref, refs = refs[0], refs[1:]
        send_refs, (sums_ref, bias_ref) = refs[: pieces - 1], refs[pieces - 1 :]
        _, part, _ = place(pieces)
        sums_ref[...] = jnp.zeros_like(sums_ref)
        bias_ref[...] = jnp.zeros_like(bias_ref)
        for h in range(pieces):

            @pl.loop(0, piece_rows // ROWS)
            def _(i, h=h):
                at = pl.multiple_of(i * ROWS, ROWS)
                src = pl.ds(at, ROWS)
                rows = pl.ds(h * piece_rows + at, ROWS)
                normed, _ = norm_rows(x_ref[rows, :].astype(F32))
                grad = jnp.zeros((ROWS, width), F32)
                for t in range(tiles):
                    grad_rows = dq_refs[t][rows, :]
                    cols = slice(t * tile_cols, (t + 1) * tile_cols)
                    grad = grad + dot_nt(grad_rows, w_ref[:, cols])
                    bias_ref[0:1, cols] += jnp.sum(grad_rows.astype(F32), axis=0, keepdims=True)
                if h == 0:
                    own_ref[src, :] = grad
                else:
                    send_refs[h - 1][src, :] = grad.astype(BF16)
                sums_ref[0:1, :] += jnp.sum(grad * normed, axis=0, keepdims=True)
                sums_ref[1:2, :] += jnp.sum(grad, axis=0, keepdims=True)

        if not packed:
            return
        for row, src in ((4, 2), (5, 0), (6, 1), (15, 3)):
            sums_ref[row : row + 1, :] = mid_ref[src : src + 1, :]
        for c in range(pieces):

            @pl.when(part == c)
            def _(c=c):
                for row, p in ((2, 0), (3, 2)):
                    mine = jnp.concatenate(
                        [
                            bias_ref[0:1, (3 * t + p) * LANES :][:, : min(LANES, real - t * LANES)]
                            for t in range(tiles)
                        ],
                        axis=1,
                    )
                    sums_ref[row : row + 1, c * real : (c + 1) * real] = mine
                for n in range(quads):
                    row = 7 + n * pieces + c
                    start = 0
                    for ref in ups_refs:
                        size = ref.shape[1] // quads
                        here = ref[0:1, n * size : (n + 1) * size]
                        sums_ref[row : row + 1, start : start + size] = here
                        start += size

    return run(
        body,
        [rows_all, weight, sums_mid, *up_sums, *grad_tiles],
        after,
        out_shape=[sds((piece_rows, width), F32)]
        + [sds((piece_rows, width), BF16)] * (pieces - 1)
        + [sds((16, width), F32), sds((8, cols_all), F32)],
        vmem=12,
        cost_estimate=cost(2 * total * width * cols_all, 8 * 1024 * 1024),
        name="project_rows",
    )


def finish_rows(rows_all, gain, grad_mid, grad_own, received, count, after):
    rows, width = grad_mid.shape
    others = len(received)
    piece = rows // count
    per_step = ROWS // piece

    def body(*refs):
        x_ref, gain_ref, gm_ref, own_ref, refs = refs[0], refs[1], refs[2], refs[3], refs[4:]
        recv_refs, out_refs = refs[:others], refs[others:]
        for n in range(rows // ROWS):
            at = slice(n * ROWS, (n + 1) * ROWS)
            normed, inv_std = norm_rows(x_ref[at, :].astype(F32))
            grad = own_ref[at, :]
            for ref in recv_refs:
                grad = grad + ref[at, :].astype(F32)
            done = gm_ref[at, :] + norm_back(grad * gain_ref[...], normed, inv_std)
            for e in range(per_step):
                out_refs[n * per_step + e][...] = done[e * piece : (e + 1) * piece, :].astype(BF16)

    return run(
        body,
        [rows_all, gain, grad_mid, grad_own, *received],
        after,
        out_shape=[sds((piece, width), BF16)] * count,
        vmem=12,
        cost_estimate=cost(20 * rows * width, 6 * 1024 * 1024),
        name="finish_rows",
    )


def finish_result(own, received, count):
    rows, width = own.shape
    others = len(received)
    piece = rows // count

    def body(*refs):
        out_refs = refs[1 + others :]
        for n in range(count):
            at = slice(n * piece, (n + 1) * piece)
            total = refs[0][at, :]
            for ref in refs[1 : 1 + others]:
                total = total + ref[at, :].astype(F32)
            out_refs[n % 2][n // 2] = total.astype(BF16)

    return run(
        body,
        [far(own), *received],
        out_shape=[sds((count // 2, piece, width), BF16)] * 2,
        vmem=8,
        cost_estimate=cost(2 * rows * width, 3 * 1024 * 1024),
        name="finish_result",
    )


def pass_on(keep, received, after):
    def body(keep_ref, recv_ref, out_ref):
        out_ref[0] = keep_ref[1]
        out_ref[1] = recv_ref[1]

    return run(
        body,
        [keep, received],
        after,
        out_shape=sds(keep.shape, keep.dtype),
        vmem=6,
        cost_estimate=cost(0, 4 * keep.size),
        name="pass_on",
    )


def collect_halves(keep, near, far, group, after):
    _, rows, width = keep.shape

    def body(keep_ref, near_ref, far_ref, out_ref):
        _, _, quad = place(group)
        out_ref[quad] = keep_ref[0]
        out_ref[quad ^ 1] = near_ref[0]
        out_ref[quad ^ 2] = far_ref[0]
        out_ref[quad ^ 3] = far_ref[1]

    return run(
        body,
        [keep, near, far],
        after,
        out_shape=sds((4, rows, width), keep.dtype),
        vmem=6,
        cost_estimate=cost(0, 16 * rows * width),
        name="collect_halves",
    )


def two_parts(item):
    first = item.astype(BF16)
    return first, (item - first.astype(F32)).astype(BF16)


def pack_attention(
    qkv_keep, qkv_recv, out_keep, out_recv, small, small_recv, real, blocks, after
):
    quads, chunk, cols_all = qkv_keep.shape
    wide = cols_all // 3
    tiles = wide // LANES
    width = out_keep.shape[2]
    qkv_lanes = 6 * real // blocks
    out_lanes = width // blocks
    lanes = qkv_lanes + out_lanes
    halves = quads // 2
    slot = halves * chunk
    small_rows = small.shape[0]

    def body(qk_ref, qr_ref, ok_ref, or_ref, small_ref, srecv_ref, *out_refs):
        _, part, quad = place(2)
        mine = lax.axis_index("batch")
        slots = out_refs[4]

        def heads_of(rows, p):
            return [
                rows[:, (3 * t + p) * LANES : (3 * t + p) * LANES + min(LANES, real - t * LANES)]
                for t in range(tiles)
            ]

        for c in range(2):

            @pl.when(part == c)
            def _(c=c):
                for q in range(quads):
                    pair = (qk_ref[q], qr_ref[q])
                    if c == 1:
                        pair = pair[::-1]
                    parts = []
                    for p in range(3):
                        parts += heads_of(pair[0], p) + heads_of(pair[1], p)
                    row = jnp.concatenate(parts, axis=1)
                    for b in range(blocks):
                        slots[b ^ mine, q, :, 0:qkv_lanes] = row[
                            :, b * qkv_lanes : (b + 1) * qkv_lanes
                        ]
                for e, ref in enumerate((ok_ref, or_ref)):
                    for n in range(halves):
                        q = ((c + e) % 2) * halves + n
                        for b in range(blocks):
                            slots[b ^ mine, q ^ quad, :, qkv_lanes:lanes] = ref[
                                n, :, b * out_lanes : (b + 1) * out_lanes
                            ]

        for n, order in enumerate(((0, 2), (1, 3), (0, 1), (2, 3))):
            for e in range(2):
                for f in range(halves):
                    at = e * slot + f * chunk
                    src = f if n < 2 else halves + f
                    out_refs[n][at : at + chunk, :] = slots[order[e], src]
        parts = two_parts(small_ref[...] + srecv_ref[...])
        for n in range(2):
            for e in range(2):
                at = 2 * slot + e * small_rows
                out_refs[n][at : at + small_rows, :] = parts[e]

    first = sds((2 * slot + 2 * small_rows, lanes), BF16)
    other = sds((2 * slot, lanes), BF16)
    return run(
        body,
        [qkv_keep, qkv_recv, out_keep, out_recv, small, small_recv],
        after,
        out_shape=[first, first, other, other],
        scratch_shapes=[pltpu.VMEM((blocks, quads, chunk, lanes), BF16)],
        vmem=12,
        cost_estimate=cost(0, 4 * 1024 * 1024),
        name="pack_attention",
    )


def sum_first(keeps, received, after=()):
    count = len(keeps)
    shape = keeps[0].shape[1:]

    def body(*refs):
        for n in range(count):
            for e in range(2):
                total = refs[n][e].astype(F32) + refs[count + n][e].astype(F32)
                refs[2 * count + 2 * n + e][...] = total.astype(BF16)

    return run(
        body,
        [*keeps, *received],
        after,
        out_shape=[pltpu.HBM(shape, BF16), sds(shape, BF16)] * count,
        vmem=12,
        cost_estimate=cost(0, 6 * count * keeps[0].size),
        name="sum_first",
    )


def sum_second(keeps, received, after=()):
    quads, rows, width = keeps[0].shape

    def body(ka, kb, ra, rb, keep_ref, send_ref):
        for d in range(quads):
            ref = send_ref if d % 2 else keep_ref
            for e, (keep, recv) in enumerate(((ka, ra), (kb, rb))):
                total = keep[d].astype(F32) + recv[d].astype(F32)
                ref[d // 2, e] = total.astype(BF16)

    return run(
        body,
        [*keeps, *received],
        after,
        out_shape=[pltpu.HBM((quads // 2, 2, rows, width), BF16)] * 2,
        vmem=10,
        cost_estimate=cost(0, 12 * keeps[0].size),
        name="sum_second",
    )


def sum_third(keep, received, after=()):
    def body(keep_ref, recv_ref, stay_ref, pass_ref):
        for ref, e in ((stay_ref, 0), (pass_ref, 1)):
            ref[...] = (keep_ref[e].astype(F32) + recv_ref[e].astype(F32)).astype(BF16)

    return run(
        body,
        [keep, received],
        after,
        out_shape=[sds(keep.shape[1:], BF16)] * 2,
        vmem=6,
        cost_estimate=cost(0, 6 * keep.size),
        name="sum_third",
    )


def small_sum(refs, rows, count):
    total = None
    for ref in refs:
        for e in range(2):
            item = ref[rows + e * count : rows + (e + 1) * count, :].astype(F32)
            total = item if total is None else total + item
    return total


def sum_first_attention(keeps, received, slot, small_rows, after):
    lanes = keeps[0].shape[1]

    def body(ka, kb, ra, rb, stay_a, pass_a, stay_b, pass_b):
        parts = two_parts(small_sum((ka, ra), 2 * slot, small_rows))
        for keep, recv, stay, on in ((ka, ra, stay_a, pass_a), (kb, rb, stay_b, pass_b)):
            for e, ref in enumerate((stay, on)):
                at = slice(e * slot, (e + 1) * slot)
                ref[0:slot, :] = (keep[at, :].astype(F32) + recv[at, :].astype(F32)).astype(BF16)
        for ref in (stay_a, pass_a):
            for e in range(2):
                ref[slot + e * small_rows : slot + (e + 1) * small_rows, :] = parts[e]

    first = sds((slot + 2 * small_rows, lanes), BF16)
    other = sds((slot, lanes), BF16)
    return run(
        body,
        [*keeps, *received],
        after,
        out_shape=[first, first, other, other],
        vmem=8,
        cost_estimate=cost(0, 3 * 1024 * 1024),
        name="sum_first_attention",
    )


def sum_second_attention(keeps, received, chunk, quads, small_rows, after):
    lanes = keeps[0].shape[1]
    halves = quads // 2
    slot = halves * chunk

    def body(ka, kb, ra, rb, *out_refs):
        parts = two_parts(small_sum((ka, ra), slot, small_rows))
        for d in range(quads):
            keep, recv = ((ka, ra), (kb, rb))[d // halves]
            at = slice(d % halves * chunk, (d % halves + 1) * chunk)
            total = keep[at, :].astype(F32) + recv[at, :].astype(F32)
            out_refs[d][0:chunk, :] = total.astype(BF16)
            for e in range(2):
                at = chunk + e * small_rows
                out_refs[d][at : at + small_rows, :] = parts[e]

    return run(
        body,
        [*keeps, *received],
        after,
        out_shape=[sds((chunk + 2 * small_rows, lanes), BF16)] * quads,
        vmem=8,
        cost_estimate=cost(0, 2 * 1024 * 1024),
        name="sum_second_attention",
    )


def final_attention(pieces, chunk, qkv_lanes, small_rows):
    lanes = pieces[0].shape[1]
    count = len(pieces)

    def body(*refs):
        total = refs[0][0:chunk, :].astype(F32)
        for ref in refs[1:count]:
            total = total + ref[0:chunk, :].astype(F32)
        refs[count][...] = total[:, :qkv_lanes]
        refs[count + 1][...] = total[:, qkv_lanes:]
        refs[count + 2][...] = small_sum(refs[:count], chunk, small_rows)

    return run(
        body,
        pieces,
        out_shape=[
            sds((chunk, qkv_lanes), F32),
            sds((chunk, lanes - qkv_lanes), F32),
            sds((small_rows, lanes), F32),
        ],
        vmem=6,
        cost_estimate=cost(0, 1024 * 1024),
        name="final_attention",
    )


def final_units(first, second, after):
    high = first[0].shape[1]
    sizes = [first[0].shape[2], second[0].shape[2]]
    unit_block = sum(sizes)
    count = len(first)
    half = high // 2

    def body(*refs):
        _, part, _ = place(2)
        keep_ref, send_ref, down_ref = refs[2 * count :]
        for h in range(2):
            pieces = refs[h * count : (h + 1) * count]
            up, down = pieces[0][0].astype(F32), pieces[0][1].astype(F32)
            for ref in pieces[1:]:
                up = up + ref[0].astype(F32)
                down = down + ref[1].astype(F32)
            here = slice(h * sizes[0], h * sizes[0] + sizes[h])
            down_ref[here, :] = down.T
            for c in range(2):

                @pl.when(part == c)
                def _(up=up, here=here, c=c):
                    keep_ref[:, here] = up[c * half : (c + 1) * half, :]
                    send_ref[:, here] = up[(1 - c) * half : (2 - c) * half, :].astype(BF16)

    return run(
        body,
        [*first, *second],
        after,
        out_shape=[
            sds((half, unit_block), F32),
            sds((half, unit_block), BF16),
            sds((unit_block, high), F32),
        ],
        vmem=10,
        cost_estimate=cost(0, 4 * 1024 * 1024),
        name="final_units",
    )


def final_join(keep, recv):
    chunk, unit_block = keep.shape

    def body(keep_ref, recv_ref, out_ref):
        _, part, _ = place(2)
        for c in range(2):

            @pl.when(part == c)
            def _(c=c):
                out_ref[:, c * unit_block : (c + 1) * unit_block] = keep_ref[...]
                out_ref[:, (1 - c) * unit_block : (2 - c) * unit_block] = recv_ref[...].astype(F32)

    return run(
        body,
        [keep, recv],
        out_shape=sds((chunk, 2 * unit_block), F32),
        vmem=5,
        cost_estimate=cost(0, 1024 * 1024),
        name="final_join",
    )


def on_device(
    tokens,
    mask,
    cotangent,
    ln1_gain,
    ln1_bias,
    qkv_weight,
    q_bias,
    v_bias,
    out_weight,
    out_bias,
    ln2_gain,
    ln2_bias,
    up_weight,
    up_bias,
    down_weight,
    down_bias,
):
    seq_size = lax.axis_size("seq")
    batch_size = lax.axis_size("batch")
    micro_count, seq_count, local_len, width = tokens.shape
    sequences = micro_count * seq_count
    group = seq_size // sequences
    units = up_weight.shape[1]
    head_dim = width // HEADS
    heads = HEADS // group
    real = heads * head_dim
    wide = -(-real // LANES) * LANES
    full_len = local_len * seq_size
    block_len = local_len // group
    rows = seq_size * block_len
    own_units = units // group
    part = lax.axis_index("seq") % group
    aligned = (
        seq_size == batch_size * group
        and group == 2
        and batch_size == 4
        and wide == 3 * LANES
        and (seq_size // group) % group == 0
        and units % (batch_size * group * LANES) == 0
        and own_units // batch_size == width
    )

    def from_part(item, ahead):
        if ahead % group == 0:
            return item
        pairs = [
            (q * group + (c + ahead) % group, q * group + c)
            for q in range(sequences)
            for c in range(group)
        ]
        return lax.ppermute(item, "seq", pairs)

    def gather_parts(item):
        return [from_part(item, n) for n in range(group)]

    def row_of(item):
        return item.astype(F32)[None, :]

    def blocks_of(item):
        return item.reshape(sequences, local_len, width)

    x_own = over_quads(deal(blocks_of(tokens), group), group)
    x_pieces = [from_part(item, n) for n in range(group) for item in x_own]

    count_rows = jnp.sum(mask, axis=2).reshape(sequences).astype(BF16)
    cot_low = jnp.where(mask[..., None] != 0, cotangent, jnp.zeros_like(cotangent))
    cot_send = jnp.concatenate(
        [blocks_of(cot_low), jnp.broadcast_to(count_rows[:, None, None], (sequences, 16, width))],
        axis=1,
    )
    cot_own = over_quads(deal(cot_send, group, x_pieces[sequences:]), group)

    qkv_w, qkv_b, *out_w = pick_weights(
        qkv_weight,
        jnp.concatenate([q_bias, jnp.zeros_like(q_bias), v_bias])[None, :],
        out_weight,
        group,
        real,
        wide,
    )
    if aligned:
        up_own, up_b, down_own = up_weight, up_bias[None, :], down_weight
    else:

        def own_columns(matrix, blocks):
            split = matrix.reshape(matrix.shape[0], blocks, group, -1)
            return lax.dynamic_index_in_dim(split, part, 2, keepdims=False)

        up_own = own_columns(up_weight, batch_size).reshape(width, own_units)
        up_b = own_columns(up_bias[None, :], batch_size).reshape(1, own_units)
        down_own = lax.dynamic_index_in_dim(
            down_weight.reshape(batch_size, group, -1, width), part, 1, keepdims=False
        ).reshape(own_units, width)

    tiles = wide // LANES
    x_all, qkv, att_first, logs_first = attend_first(
        x_pieces, row_of(ln1_gain), row_of(ln1_bias), qkv_w, qkv_b, tiles - 1, heads, head_dim
    )
    cot_stack = stack(cot_own, [logs_first])
    att_last, logs_last = attend_last(qkv, tiles - 1, heads, head_dim, [cot_stack])
    cot_pieces = cot_own + [
        item[d]
        for item in gather_parts(cot_stack)[1:]
        for d in range(sequences)
    ]
    blocks = batch_size if aligned else 1
    unit_block = own_units // blocks
    size = unit_block * 2 // 5
    shape = (group, sequences if aligned else None, width // sequences)
    calls = [
        Units(unit_block, blocks, 0, size, *shape),
        Units(unit_block, blocks, size, unit_block - size, *shape),
    ]
    mid, second, second_t, grad_rows, grad_t, result_own, grad_second, *found = feed_first(
        x_all,
        gather_parts(att_first),
        gather_parts(att_last),
        cot_pieces,
        out_w,
        row_of(out_bias),
        row_of(ln2_gain),
        row_of(ln2_bias),
        up_own,
        up_b,
        down_own,
        row_of(down_bias),
        calls[0],
    )
    up_sums, ff_grads = [found[0]], [found[group:]]
    result_own, grad_second, *found = feed_second(
        second,
        second_t,
        grad_rows,
        grad_t,
        result_own,
        grad_second,
        found[1:group],
        up_own,
        up_b,
        down_own,
        calls[1],
    )
    up_sums.append(found[0])
    result_send = found[1:group]
    ff_grads.append(found[group:])

    def begin_sum(e, sends, after):
        moved = [swap(sends[0], "batch", batch_size, 1), swap(sends[1], "batch", batch_size, 2)]
        stay_a, pass_a, stay_b, pass_b = sum_first(
            [ff_grads[e][0], ff_grads[e][2]], moved, after
        )
        moved = [swap(pass_a, "batch", batch_size, 2), swap(pass_b, "batch", batch_size, 1)]
        return [stay_a, stay_b], moved

    if aligned:
        waiting = begin_sum(0, [ff_grads[0][1], ff_grads[0][3]], [])
        (grad_second,) = gate([grad_second], waiting[0][:1])
    second_send = grad_second
    second_recv = [from_part(second_send, n) for n in range(1, group)]
    result_recv = [from_part(result_send[group - n - 1], n) for n in range(1, group)]
    result_keep, result_pass = finish_result(result_own, result_recv, sequences)

    def quad_swap(item, distance):
        return swap(item, "seq", seq_size, distance * group)

    result_near = quad_swap(result_pass, 1)

    chunk = width // seq_size
    grad_mid, grad_att, sums_mid, *out_grad = mid_back(
        mid,
        grad_second,
        second_recv,
        grad_rows,
        row_of(ln2_gain),
        out_w[0],
        att_first,
        att_last,
        chunk if aligned else 0,
    )

    def tile_back(t, after, cost_part=1):
        last = t == tiles - 1
        return attend_backward(
            qkv,
            grad_att,
            att_last if last else att_first,
            0 if last else t,
            logs_last if last else logs_first,
            0 if last else t * (LANES // head_dim),
            t,
            heads,
            head_dim,
            after,
            cost_part,
        )

    grad_tiles = [None] * tiles
    after = [result_keep]
    if aligned:
        keep, send = sum_second(*waiting, [grad_mid])
        moved = quad_swap(send, 1)
        sends = gate([ff_grads[1][1], ff_grads[1][3]], [keep])
        after = [result_keep, keep]
    grad_tiles[0] = tile_back(0, after, 64)
    result_pass = pass_on(result_keep, result_near, grad_tiles[:1])
    result_far = quad_swap(result_pass, 2)
    after = [result_pass]
    if aligned:
        unit_first = list(sum_third(keep, moved, [grad_tiles[0]]))
        unit_first[1] = quad_swap(unit_first[1], 2)
        waiting = begin_sum(1, sends, [grad_tiles[0]])
        after = [result_pass, unit_first[0], waiting[0][0]]
    for t in range(1, tiles - 1):
        grad_tiles[t] = tile_back(t, after)
    after = [grad_tiles[-2], result_far]
    if aligned:
        out_recv = from_part(out_grad[1], 1)
        keep, send = sum_second(*waiting, [grad_tiles[-2]])
        moved = quad_swap(send, 1)
        after = [keep, result_far, unit_first[1]]
    grad_tiles[-1] = tile_back(tiles - 1, after)
    after = []
    if aligned:
        after = [out_recv]
    qkv_grad = project_weights(
        x_all,
        row_of(ln1_gain),
        row_of(ln1_bias),
        grad_tiles,
        group,
        sequences,
        aligned,
        after,
    )
    after = qkv_grad[:1]
    if aligned:
        unit_second = list(sum_third(keep, moved, qkv_grad[:1]))
        unit_second[1] = quad_swap(unit_second[1], 2)
        after = unit_second[:1]
    first_own, *found = project_rows(
        x_all,
        qkv_w,
        grad_tiles,
        sums_mid,
        up_sums,
        group,
        sequences,
        aligned,
        real,
        after,
    )
    first_send, (small, bias_sums) = found[: group - 1], found[group - 1 :]
    first_recv = [from_part(first_send[group - n - 1], n) for n in range(1, group)]
    after = []
    if aligned:
        small_rows = small.shape[0]
        packed = pack_attention(
            qkv_grad[0],
            from_part(qkv_grad[1], 1),
            out_grad[0],
            out_recv,
            small,
            from_part(small, 1),
            real,
            batch_size,
            [],
        )
        after = packed[:1]
    row_parts = finish_rows(
        x_all, row_of(ln1_gain), grad_mid, first_own, first_recv, sequences, after
    )
    row_moved = over_quads(row_parts, group)
    if aligned:
        stay_a, pass_a, stay_b, pass_b = sum_first_attention(
            [packed[0], packed[2]],
            [swap(packed[1], "batch", batch_size, 1), swap(packed[3], "batch", batch_size, 2)],
            sequences // 2 * chunk,
            small_rows,
            [row_parts[0], *row_moved[1::2]],
        )
        summed = sum_second_attention(
            [stay_a, stay_b],
            [swap(pass_a, "batch", batch_size, 2), swap(pass_b, "batch", batch_size, 1)],
            chunk,
            sequences,
            small_rows,
            [],
        )
        after = summed[:1]
        up_keep, up_send, down_grad = final_units(unit_first, unit_second, after)
        up_grad = final_join(up_keep, from_part(up_send, 1))
        qkv_final, out_final, small = final_attention(
            over_quads(summed, group), chunk, qkv_weight.shape[1] // batch_size, small_rows
        )
        small = small.reshape(-1)
    result = collect_halves(result_keep, result_near, result_far, group, after)
    result = result.reshape(tokens.shape)
    grad_in = collect(row_moved, group, after).reshape(tokens.shape)
    if not aligned:

        def spread(item, blocks):
            split = item.reshape(blocks, 1, -1)
            empty = jnp.zeros((blocks, group, split.shape[2]), F32)
            return lax.dynamic_update_slice(empty, split, (0, part, 0)).reshape(-1)

        bias_sums = bias_sums[0].reshape(tiles, 3, LANES).transpose(1, 0, 2)
        bias_sums = bias_sums.reshape(3, wide)[:, :real]
        small = jnp.concatenate(
            [
                small[0],
                small[1],
                spread(bias_sums[0], 1),
                spread(bias_sums[2], 1),
                sums_mid[2],
                sums_mid[0],
                sums_mid[1],
                spread(jnp.concatenate([item[0] for item in up_sums]), batch_size),
                sums_mid[3],
            ]
        )

        def scattered(item):
            item = lax.psum_scatter(item.astype(BF16), "seq", scatter_dimension=0, tiled=True)
            return lax.psum_scatter(item, "batch", scatter_dimension=1, tiled=True).astype(F32)

        def spread_columns(item, blocks):
            split = item.reshape(item.shape[0], blocks, 1, -1)
            empty = jnp.zeros((item.shape[0], blocks, group, split.shape[3]), item.dtype)
            filled = lax.dynamic_update_slice(empty, split, (0, 0, part, 0))
            return filled.reshape(item.shape[0], -1)

        up_full, down_full = [
            jnp.concatenate([item[e] for item in ff_grads], axis=1) for e in range(2)
        ]
        up_grad = scattered(spread_columns(up_full, batch_size))
        down_grad = scattered(spread_columns(down_full, batch_size).T)
        rows_full = qkv_grad[0].reshape(width, tiles, 3, LANES).transpose(0, 2, 1, 3)
        rows_full = rows_full.reshape(width, 3, wide)[..., :real]
        qkv_final = scattered(spread_columns(rows_full.reshape(width, -1), 3))
        out_final = scattered(spread_columns(out_grad[0][:real].T, 1).T)
        small = lax.psum(small, ("seq", "batch"))

    edges = [width] * 7 + [units, width]
    pieces, start = [], 0
    for size in edges:
        pieces.append(small[start : start + size])
        start += size
    return (
        result,
        grad_in,
        pieces[0],
        pieces[1],
        qkv_final,
        pieces[2],
        pieces[3],
        out_final,
        pieces[4],
        pieces[5],
        pieces[6],
        up_grad,
        pieces[7],
        down_grad,
        pieces[8],
    )


def solution(mesh):
    rows = P(None, "batch", "seq", None)
    split = P("seq", "batch")
    in_specs = (rows, P(None, "batch", "seq"), rows) + (P(),) * 13
    out_specs = (
        rows,
        rows,
        P(),
        P(),
        split,
        P(),
        P(),
        split,
        P(),
        P(),
        P(),
        split,
        P(),
        split,
        P(),
    )
    return jax.shard_map(
        on_device, mesh=mesh, in_specs=in_specs, out_specs=out_specs, check_vma=False
    )
```

profile of v0, /device:TPU:9, one launch (start us, length us, event | category | flops | bytes accessed | tf_op | source)
XLA Modules:
  0.0 218.9 jit_solution(7693909849209329072)
XLA Ops:
  0.7 1.2 copy-done.17
  2.0 2.5 %collective-permute-start.1 = (bf16[128,640]{1,0:T(8,128)(2,1)S(1)}, bf16[128,640]{1,0:T(8,128)(2,1)S(1)}, u32[]{:S(2)}, u32[]{:S(2)}) collective-permute-start(bf16[128,640]{1,0:T(8,128)(2,1)S(1)} %get-tuple-element.108), channel_id=1, source_target_pairs={{0,16},{4,20},{8,24},{12,28},{16,0},{20,4},{24,8},{28,12},{1,17},{... | collective-permute-start | bytes 491528 | tf_op jit(solution)/shard_map/ppermute | solution.py:161
  4.6 1.5 collective-permute-start.3
  6.8 1.2 broadcast_select_fusion
  8.1 1.6 collective-permute-start.4
  9.7 1.9 collective-permute-done.1.refs_2_
  11.6 5.6 %collective-permute-start.5 = (bf16[128,640]{1,0:T(8,128)(2,1)S(1)}, bf16[128,640]{1,0:T(8,128)(2,1)S(1)}, u32[]{:S(2)}, u32[]{:S(2)}) collective-permute-start(bf16[128,640]{1,0:T(8,128)(2,1)S(1)} %collective-permute-done.1.refs_2_), channel_id=1, source_target_pairs={{4,0},{0,4},{12,8},{8,12},{20,16},{16,20},{28,24},{24,28},{5,1},{1... | collective-permute-start | bytes 491528 | tf_op jit(solution)/shard_map/ppermute | solution.py:1391
  17.2 1.4 collective-permute-done.2.refs_3_
  18.5 1.8 collective-permute-start.6
  20.7 1.7 copy-done.2
  23.8 2.5 %collective-permute-start.8 = (bf16[144,640]{1,0:T(8,128)(2,1)S(1)}, bf16[144,640]{1,0:T(8,128)(2,1)S(1)}, u32[]{:S(2)}, u32[]{:S(2)}) collective-permute-start(bf16[144,640]{1,0:T(8,128)(2,1)S(1)} %get-tuple-element.117), channel_id=1, source_target_pairs={{0,16},{4,20},{8,24},{12,28},{16,0},{20,4},{24,8},{28,12},{1,17},{... | collective-permute-start | bytes 552968 | tf_op jit(solution)/shard_map/ppermute | solution.py:161
  26.4 15.8 %attend_first.1 = (bf16[1024,640]{1,0:T(8,128)(2,1)S(1)}, bf16[1024,1152]{1,0:T(8,128)(2,1)S(1)}, bf16[1024,256]{1,0:T(8,128)(2,1)S(1)}, f32[1024,128]{1,0:T(8,128)S(1)}) custom-call(bf16[128,640]{1,0:T(8,128)(2,1)S(1)} %get-tuple-element.106.refs_0_, bf16[128,640]{1,0:T(8,128)(2,1)S(1)} %collective-permute-done.refs_1_, ...), custom_call_target="tpu_custom_call" | custom-call | flops 12247367680 | bytes 8388608 | tf_op jit(solution)/shard_map/attend_first/pallas_call | solution.py:70
  44.1 3.1 %attend_last.1 = (bf16[1024,128]{1,0:T(8,128)(2,1)S(1)}, f32[1024,128]{1,0:T(8,128)S(1)}) custom-call(bf16[1024,1152]{1,0:T(8,128)(2,1)S(1)} %get-tuple-element.114.refs_0_, bf16[4,144,640]{2,1,0:T(8,128)(2,1)S(1)} %stack.1.refs_1_), custom_call_target="tpu_custom_call" | custom-call | flops 2147483648 | bytes 2097152 | tf_op jit(solution)/shard_map/attend_last/pallas_call | solution.py:70
  49.7 17.2 %feed_first.1 = (f32[1024,640]{1,0:T(8,128)}, bf16[1024,640]{1,0:T(8,128)(2,1)S(1)}, bf16[640,1024]{1,0:T(8,128)(2,1)S(1)}, bf16[1024,640]{1,0:T(8,128)(2,1)S(1)...) custom-call(bf16[1024,640]{1,0:T(8,128)(2,1)S(1)} %get-tuple-element, ...), custom_call_target="tpu_custom_call" | custom-call | flops 8053063680 | bytes 25165824 | tf_op jit(solution)/shard_map/feed_first/pallas_call | solution.py:70
  67.5 1.2 collective-permute-start.15
  68.7 1.2 collective-permute-start.16
  69.9 22.8 %feed_second.1 = (f32[512,640]{1,0:T(8,128)S(1)}, bf16[1024,640]{1,0:T(8,128)(2,1)S(1)}, f32[8,1536]{1,0:T(8,128)S(1)}, bf16[512,640]{1,0:T(8,128)(2,1)}, bf16[2...) custom-call(bf16[1024,640]{1,0:T(8,128)(2,1)S(1)} %get-tuple-element, ...), custom_call_target="tpu_custom_call" | custom-call | flops 12079595520 | bytes 25165824 | tf_op jit(solution)/shard_map/feed_second/pallas_call | solution.py:70
  92.8 1.6 sum_first.2
  96.7 1.8 collective-permute-done.17.refs_2_
  98.5 7.0 %mid_back.1 = (f32[512,640]{1,0:T(8,128)S(1)}, bf16[1024,384]{1,0:T(8,128)(2,1)S(1)}, f32[8,640]{1,0:T(8,128)S(1)}, bf16[2,80,640]{2,1,0:T(8,128)(2,1)}, bf16[2,80,640]{2,1,0:T(8,128)(2,1)}) custom-call(f32[1024,640]{1,0:T(8,128)} %get-tuple-element.134.refs_0_, bf16[1024,640]{1,0:T(8,128)(2,1)} %gate.2.refs_1_, ...), custom_call_target="tpu_custom_call" | custom-call | flops 1006632960 | bytes 14680064 | tf_op jit(solution)/shard_map/mid_back/pallas_call | solution.py:70
  107.6 1.6 finish_result.1
  109.3 1.4 collective-permute-start.21
  110.8 1.7 copy-done.4
  112.4 12.1 %attend_backward.3.refs_2_.refs_4_.refs_3_.refs_5_ = bf16[1024,384]{1,0:T(8,128)(2,1)S(1)} custom-call(bf16[1024,1152]{1,0:T(8,128)(2,1)S(1)} %copy-done.4, bf16[1024,384]{1,0:T(8,128)(2,1)S(1)} %get-tuple-element.141.refs_1_, bf16[1024,256]{1,0:T(8,128)(2,1)S(1)} %copy-done.6, f32[1024,128]{1,0:T(8,128)S(1)} %get-tuple-element.119.refs_4_.refs_3_, ...), custom_call_target="tpu_custom_call" | custom-call | flops 167772160 | bytes 49152 | tf_op jit(solution)/shard_map/attend_backward/pallas_call | solution.py:70
  124.6 1.2 collective-permute-start.20
  125.8 2.2 %collective-permute-start.27 = (bf16[2,80,640]{2,1,0:T(8,128)(2,1)S(1)}, bf16[2,80,640]{2,1,0:T(8,128)(2,1)S(1)}, u32[]{:S(2)}, u32[]{:S(2)}) collective-permute-start(bf16[2,80,640]{2,1,0:T(8,128)(2,1)S(1)} %copy-done.46), channel_id=1, source_target_pairs={{4,0},{0,4},{12,8},{8,12},{20,16},{16,20},{28,24},{24,28},{5,1},{1... | collective-permute-start | bytes 614408 | tf_op jit(solution)/shard_map/ppermute | solution.py:1391
  128.1 1.6 collective-permute-start.26
  129.7 1.1 sum_first.3
  131.1 1.2 collective-permute-start.25
  133.3 12.4 %attend_backward.4.refs_4_.refs_6_ = bf16[1024,384]{1,0:T(8,128)(2,1)S(1)} custom-call(bf16[1024,1152]{1,0:T(8,128)(2,1)S(1)} %copy-done.4, bf16[1024,384]{1,0:T(8,128)(2,1)S(1)} %get-tuple-element.141.refs_1_, bf16[1024,256]{1,0:T(8,128)(2,1)S(1)} %copy-done.6, f32[1024,128]{1,0:T(8,128)S(1)} %get-tuple-element.119.refs_4_.refs_3_, ...), custom_call_target="tpu_custom_call" | custom-call | flops 10737418240 | bytes 3145728 | tf_op jit(solution)/shard_map/attend_backward/pallas_call | solution.py:70
  145.7 1.1 sum_second.3
  147.0 1.1 copy-done.22
  148.2 6.5 %attend_backward.5.refs_5_.refs_7_ = bf16[1024,384]{1,0:T(8,128)(2,1)S(1)} custom-call(bf16[1024,1152]{1,0:T(8,128)(2,1)S(1)} %copy-done.4, bf16[1024,384]{1,0:T(8,128)(2,1)S(1)} %get-tuple-element.141.refs_1_, bf16[1024,128]{1,0:T(8,128)(2,1)S(1)} %copy-done.27, f32[1024,128]{1,0:T(8,128)S(1)} %copy-done.35, bf16[2,2,160,384]{3,2,1,0:T(8,128)(2,1)S(1)} %copy-done.22, ...), custom_call_target="tpu_custom_call" | custom-call | flops 5368709120 | bytes 3145728 | tf_op jit(solution)/shard_map/attend_backward/pallas_call | solution.py:70
  154.8 4.2 %project_weights.1 = (bf16[4,80,1152]{2,1,0:T(8,128)(2,1)S(1)}, bf16[4,80,1152]{2,1,0:T(8,128)(2,1)S(1)}) custom-call(bf16[1024,640]{1,0:T(8,128)(2,1)S(1)} %copy-done.9, f32[1,640]{1,0:T(1,128)S(1)} %broadcast_in_dim.49.refs_8_.refs_1_, f32[1,640]{1,0:T(1,128)S(1)} %broadcast_in_dim.50.refs_9_.refs_2_, ...), custom_call_target="tpu_custom_call" | custom-call | flops 1509949440 | bytes 6291456 | tf_op jit(solution)/shard_map/project_weights/pallas_call | solution.py:70
  159.0 2.5 %collective-permute-start.28 = (bf16[4,80,1152]{2,1,0:T(8,128)(2,1)S(1)}, bf16[4,80,1152]{2,1,0:T(8,128)(2,1)S(1)}, u32[]{:S(2)}, u32[]{:S(2)}) collective-permute-start(bf16[4,80,1152]{2,1,0:T(8,128)(2,1)S(1)} %get-tuple-element.164), channel_id=1, source_target_pairs={{4,0},{0,4},{12,8},{8,12},{20,16},{16,20},{28,24},{24,28},{5,1},{1... | collective-permute-start | bytes 2211848 | tf_op jit(solution)/shard_map/ppermute | solution.py:1391
  161.6 4.2 %project_rows.1 = (f32[512,640]{1,0:T(8,128)S(1)}, bf16[512,640]{1,0:T(8,128)(2,1)S(1)}, f32[16,640]{1,0:T(8,128)S(1)}, f32[8,1152]{1,0:T(8,128)}) custom-call(bf16[1024,640]{1,0:T(8,128)(2,1)S(1)} %copy-done.9, bf16[640,1152]{1,0:T(8,128)(2,1)S(1)} %copy-done.30, f32[8,640]{1,0:T(8,128)S(1)} %get-tuple-element.166.refs_2_, f32[8,1024]{1,0:T(8,128)S(1)} %copy-done.33, ...), custom_call_target="tpu_custom_call" | custom-call | flops 1509949440 | bytes 8388608 | tf_op jit(solution)/shard_map/project_rows/pallas_call | solution.py:70
  166.8 1.8 collective-permute-done.30.refs_5_
  170.6 1.5 finish_rows.1
  172.2 1.7 collective-permute-start.34
  173.9 1.3 collective-permute-start.35
  175.2 5.1 %collective-permute-done.32.refs_3_ = bf16[320,640]{1,0:T(8,128)(2,1)S(1)} collective-permute-done((bf16[320,640]{1,0:T(8,128)(2,1)S(1)}, bf16[320,640]{1,0:T(8,128)(2,1)S(1)}, u32[]{:S(2)}, u32[]{:S(2)}) %collective-permute-start.32) | collective-permute-done | bytes 409632 | tf_op jit(solution)/shard_map/ppermute | solution.py:161
  182.5 2.9 %collective-permute-start.42 = (bf16[2,160,384]{2,1,0:T(8,128)(2,1)S(1)}, bf16[2,160,384]{2,1,0:T(8,128)(2,1)S(1)}, u32[]{:S(2)}, u32[]{:S(2)}) collective-permute-start(bf16[2,160,384]{2,1,0:T(8,128)(2,1)S(1)} %get-tuple-element.193), channel_id=1, source_target_pairs={{0,16},{4,20},{8,24},{12,28},{16,0},{20,4},{24,8},{28,12},{1,17},{... | collective-permute-start | bytes 737288 | tf_op jit(solution)/shard_map/ppermute | solution.py:161
  185.5 1.4 collective-permute-done.37.refs_3_
  187.6 2.6 %collective-permute-start.39 = (bf16[112,640]{1,0:T(8,128)(2,1)}, bf16[112,640]{1,0:T(8,128)(2,1)S(1)}, u32[]{:S(2)}, u32[]{:S(2)}) collective-permute-start(bf16[112,640]{1,0:T(8,128)(2,1)} %get-tuple-element.187), channel_id=1, source_target_pairs={{0,8},{4,12},{8,0},{12,4},{16,24},{20,28},{24,16},{28,20},{1,9},{5... | collective-permute-start | bytes 430088 | tf_op jit(solution)/shard_map/ppermute | solution.py:161
  190.2 1.4 collective-permute-start.40
  191.6 8.2 %collective-permute-done.42.refs_3_ = bf16[2,160,384]{2,1,0:T(8,128)(2,1)S(1)} collective-permute-done((bf16[2,160,384]{2,1,0:T(8,128)(2,1)S(1)}, bf16[2,160,384]{2,1,0:T(8,128)(2,1)S(1)}, u32[]{:S(2)}, u32[]{:S(2)}) %collective-permute-start.42) | collective-permute-done | bytes 245792 | tf_op jit(solution)/shard_map/ppermute | solution.py:161
  200.2 8.3 %collective-permute-start.43 = (bf16[80,640]{1,0:T(8,128)(2,1)S(1)}, bf16[80,640]{1,0:T(8,128)(2,1)S(1)}, u32[]{:S(2)}, u32[]{:S(2)}) collective-permute-start(bf16[80,640]{1,0:T(8,128)(2,1)S(1)} %get-tuple-element.195), channel_id=1, source_target_pairs={{4,0},{0,4},{12,8},{8,12},{20,16},{16,20},{28,24},{24,28},{5,1},{1... | collective-permute-start | bytes 307208 | tf_op jit(solution)/shard_map/ppermute | solution.py:1391
  212.1 4.4 %collective-permute-done.41.refs_3_ = bf16[112,640]{1,0:T(8,128)(2,1)S(1)} collective-permute-done((bf16[112,640]{1,0:T(8,128)(2,1)S(1)}, bf16[112,640]{1,0:T(8,128)(2,1)S(1)}, u32[]{:S(2)}, u32[]{:S(2)}) %collective-permute-start.41) | collective-permute-done | bytes 143392 | tf_op jit(solution)/shard_map/ppermute | solution.py:161
  (188 shorter events, 25.7 us)
Async XLA Ops:
  1.9 6.2 %collective-permute-start = (bf16[128,640]{1,0:T(8,128)(2,1)S(1)}, bf16[128,640]{1,0:T(8,128)(2,1)S(1)}, u32[]{:S(2)}, u32[]{:S(2)}) collective-permute-start(bf16[128,640]{1,0:T(8,128)(2,1)S(1)} %get-tuple-element.107), channel_id=1, source_target_pairs={{0,8},{4,12},{8,0},{12,4},{16,24},{20,28},{24,16},{28,20},{1,9},{5... | collective-permute-start | bytes 491528 | tf_op jit(solution)/shard_map/ppermute | solution.py:161
  2.0 9.6 %collective-permute-start.1 = (bf16[128,640]{1,0:T(8,128)(2,1)S(1)}, bf16[128,640]{1,0:T(8,128)(2,1)S(1)}, u32[]{:S(2)}, u32[]{:S(2)}) collective-permute-start(bf16[128,640]{1,0:T(8,128)(2,1)S(1)} %get-tuple-element.108), channel_id=1, source_target_pairs={{0,16},{4,20},{8,24},{12,28},{16,0},{20,4},{24,8},{28,12},{1,17},{... | collective-permute-start | bytes 491528 | tf_op jit(solution)/shard_map/ppermute | solution.py:161
  4.5 14.1 %collective-permute-start.2 = (bf16[128,640]{1,0:T(8,128)(2,1)S(1)}, bf16[128,640]{1,0:T(8,128)(2,1)S(1)}, u32[]{:S(2)}, u32[]{:S(2)}) collective-permute-start(bf16[128,640]{1,0:T(8,128)(2,1)S(1)} %get-tuple-element.109), channel_id=1, source_target_pairs={{0,24},{4,28},{8,16},{12,20},{16,8},{20,12},{24,0},{28,4},{1,25},{... | collective-permute-start | bytes 491528 | tf_op jit(solution)/shard_map/ppermute | solution.py:161
  4.6 18.9 %collective-permute-start.3 = (bf16[128,640]{1,0:T(8,128)(2,1)S(1)}, bf16[128,640]{1,0:T(8,128)(2,1)S(1)}, u32[]{:S(2)}, u32[]{:S(2)}) collective-permute-start(bf16[128,640]{1,0:T(8,128)(2,1)S(1)} %get-tuple-element.106.refs_0_), channel_id=1, source_target_pairs={{4,0},{0,4},{12,8},{8,12},{20,16},{16,20},{28,24},{24,28},{5,1},{1... | collective-permute-start | bytes 491528 | tf_op jit(solution)/shard_map/ppermute | solution.py:1391
  8.1 15.5 %collective-permute-start.4 = (bf16[128,640]{1,0:T(8,128)(2,1)S(1)}, bf16[128,640]{1,0:T(8,128)(2,1)S(1)}, u32[]{:S(2)}, u32[]{:S(2)}) collective-permute-start(bf16[128,640]{1,0:T(8,128)(2,1)S(1)} %collective-permute-done.refs_1_), channel_id=1, source_target_pairs={{4,0},{0,4},{12,8},{8,12},{20,16},{16,20},{28,24},{24,28},{5,1},{1... | collective-permute-start | bytes 491528 | tf_op jit(solution)/shard_map/ppermute | solution.py:1391
  11.6 11.9 %collective-permute-start.5 = (bf16[128,640]{1,0:T(8,128)(2,1)S(1)}, bf16[128,640]{1,0:T(8,128)(2,1)S(1)}, u32[]{:S(2)}, u32[]{:S(2)}) collective-permute-start(bf16[128,640]{1,0:T(8,128)(2,1)S(1)} %collective-permute-done.1.refs_2_), channel_id=1, source_target_pairs={{4,0},{0,4},{12,8},{8,12},{20,16},{16,20},{28,24},{24,28},{5,1},{1... | collective-permute-start | bytes 491528 | tf_op jit(solution)/shard_map/ppermute | solution.py:1391
  18.5 5.0 %collective-permute-start.6 = (bf16[128,640]{1,0:T(8,128)(2,1)S(1)}, bf16[128,640]{1,0:T(8,128)(2,1)S(1)}, u32[]{:S(2)}, u32[]{:S(2)}) collective-permute-start(bf16[128,640]{1,0:T(8,128)(2,1)S(1)} %collective-permute-done.2.refs_3_), channel_id=1, source_target_pairs={{4,0},{0,4},{12,8},{8,12},{20,16},{16,20},{28,24},{24,28},{5,1},{1... | collective-permute-start | bytes 491528 | tf_op jit(solution)/shard_map/ppermute | solution.py:1391
  23.4 26.2 %copy-start.18 = (bf16[384,640]{1,0:T(8,128)(2,1)}, bf16[384,640]{1,0:T(8,128)(2,1)S(1)}, u32[]{:S(2)}) copy-start(bf16[384,640]{1,0:T(8,128)(2,1)S(1)} %get-tuple-element.121.refs_13_.refs_5_) | copy-start | bytes 1474564
  23.7 18.6 %collective-permute-start.7 = (bf16[144,640]{1,0:T(8,128)(2,1)S(1)}, bf16[144,640]{1,0:T(8,128)(2,1)S(1)}, u32[]{:S(2)}, u32[]{:S(2)}) collective-permute-start(bf16[144,640]{1,0:T(8,128)(2,1)S(1)} %get-tuple-element.116), channel_id=1, source_target_pairs={{0,8},{4,12},{8,0},{12,4},{16,24},{20,28},{24,16},{28,20},{1,9},{5... | collective-permute-start | bytes 552968 | tf_op jit(solution)/shard_map/ppermute | solution.py:161
  23.8 18.5 %collective-permute-start.8 = (bf16[144,640]{1,0:T(8,128)(2,1)S(1)}, bf16[144,640]{1,0:T(8,128)(2,1)S(1)}, u32[]{:S(2)}, u32[]{:S(2)}) collective-permute-start(bf16[144,640]{1,0:T(8,128)(2,1)S(1)} %get-tuple-element.117), channel_id=1, source_target_pairs={{0,16},{4,20},{8,24},{12,28},{16,0},{20,4},{24,8},{28,12},{1,17},{... | collective-permute-start | bytes 552968 | tf_op jit(solution)/shard_map/ppermute | solution.py:161
  26.2 17.0 %collective-permute-start.9 = (bf16[144,640]{1,0:T(8,128)(2,1)S(1)}, bf16[144,640]{1,0:T(8,128)(2,1)S(1)}, u32[]{:S(2)}, u32[]{:S(2)}) collective-permute-start(bf16[144,640]{1,0:T(8,128)(2,1)S(1)} %get-tuple-element.118), channel_id=1, source_target_pairs={{0,24},{4,28},{8,16},{12,20},{16,8},{20,12},{24,0},{28,4},{1,25},{... | collective-permute-start | bytes 552968 | tf_op jit(solution)/shard_map/ppermute | solution.py:161
  43.3 5.2 %collective-permute-start.12 = (bf16[4,144,640]{2,1,0:T(8,128)(2,1)S(1)}, bf16[4,144,640]{2,1,0:T(8,128)(2,1)S(1)}, u32[]{:S(2)}, u32[]{:S(2)}) collective-permute-start(bf16[4,144,640]{2,1,0:T(8,128)(2,1)S(1)} %stack.1.refs_1_), channel_id=1, source_target_pairs={{4,0},{0,4},{12,8},{8,12},{20,16},{16,20},{28,24},{24,28},{5,1},{1... | collective-permute-start | bytes 2211848 | tf_op jit(solution)/shard_map/ppermute | solution.py:1391
  44.0 5.6 %collective-permute-start.10 = (bf16[1024,256]{1,0:T(8,128)(2,1)S(1)}, bf16[1024,256]{1,0:T(8,128)(2,1)S(1)}, u32[]{:S(2)}, u32[]{:S(2)}) collective-permute-start(bf16[1024,256]{1,0:T(8,128)(2,1)S(1)} %get-tuple-element.113.refs_1_.refs_6_.refs_2_), channel_id=1, source_target_pairs={{4,0},{0,4},{12,8},{8,12},{20,16},{16,20},{28,24},{24,28},{5,1},{1... | collective-permute-start | bytes 1572872 | tf_op jit(solution)/shard_map/ppermute | solution.py:1391
  48.0 1.6 collective-permute-start.11
  67.5 25.3 %copy-start.10 = (bf16[1024,640]{1,0:T(8,128)(2,1)}, bf16[1024,640]{1,0:T(8,128)(2,1)S(1)}, u32[]{:S(2)}) copy-start(bf16[1024,640]{1,0:T(8,128)(2,1)S(1)} %get-tuple-element.125.refs_2_.refs_3_) | copy-start | bytes 3932164
  67.5 25.3 %collective-permute-start.15 = (bf16[2,4,160,256]{3,2,1,0:T(8,128)(2,1)}, bf16[2,4,160,256]{3,2,1,0:T(8,128)(2,1)S(1)}, u32[]{:S(2)}, u32[]{:S(2)}) collective-permute-start(bf16[2,4,160,256]{3,2,1,0:T(8,128)(2,1)} %get-tuple-element.138), channel_id=1, source_target_pairs={{0,1},{1,0},{2,3},{3,2},{4,5},{5,4},{6,7},{7,6},{8,9},{9,8},{10,11... | collective-permute-start | bytes 1966088 | tf_op jit(solution)/shard_map/ppermute | solution.py:161
  68.7 24.1 %collective-permute-start.16 = (bf16[2,4,160,256]{3,2,1,0:T(8,128)(2,1)}, bf16[2,4,160,256]{3,2,1,0:T(8,128)(2,1)S(1)}, u32[]{:S(2)}, u32[]{:S(2)}) collective-permute-start(bf16[2,4,160,256]{3,2,1,0:T(8,128)(2,1)} %get-tuple-element.139), channel_id=1, source_target_pairs={{0,2},{1,3},{2,0},{3,1},{4,6},{5,7},{6,4},{7,5},{8,10},{9,11},{10,... | collective-permute-start | bytes 1966088 | tf_op jit(solution)/shard_map/ppermute | solution.py:161
  69.9 22.9 %copy-start.15 = (bf16[2,4,160,256]{3,2,1,0:T(8,128)(2,1)S(1)}, bf16[2,4,160,256]{3,2,1,0:T(8,128)(2,1)}, u32[]{:S(2)}) copy-start(bf16[2,4,160,256]{3,2,1,0:T(8,128)(2,1)} %get-tuple-element.136.refs_0_) | copy-start | bytes 1966084
  69.9 22.9 %copy-start.16 = (bf16[2,4,160,256]{3,2,1,0:T(8,128)(2,1)S(1)}, bf16[2,4,160,256]{3,2,1,0:T(8,128)(2,1)}, u32[]{:S(2)}) copy-start(bf16[2,4,160,256]{3,2,1,0:T(8,128)(2,1)} %get-tuple-element.137.refs_1_) | copy-start | bytes 1966084
  94.7 3.8 %collective-permute-start.17 = (bf16[1024,640]{1,0:T(8,128)(2,1)}, bf16[1024,640]{1,0:T(8,128)(2,1)S(1)}, u32[]{:S(2)}, u32[]{:S(2)}) collective-permute-start(bf16[1024,640]{1,0:T(8,128)(2,1)} %gate.2.refs_1_), channel_id=1, source_target_pairs={{4,0},{0,4},{12,8},{8,12},{20,16},{16,20},{28,24},{24,28},{5,1},{1... | collective-permute-start | bytes 3932168 | tf_op jit(solution)/shard_map/ppermute | solution.py:1391
  95.6 9.9 %collective-permute-start.18 = (bf16[4,160,256]{2,1,0:T(8,128)(2,1)}, bf16[4,160,256]{2,1,0:T(8,128)(2,1)S(1)}, u32[]{:S(2)}, u32[]{:S(2)}) collective-permute-start(bf16[4,160,256]{2,1,0:T(8,128)(2,1)} %get-tuple-element.143), channel_id=1, source_target_pairs={{0,2},{1,3},{2,0},{3,1},{4,6},{5,7},{6,4},{7,5},{8,10},{9,11},{10,... | collective-permute-start | bytes 983048 | tf_op jit(solution)/shard_map/ppermute | solution.py:161
  95.9 9.7 %collective-permute-start.19 = (bf16[4,160,256]{2,1,0:T(8,128)(2,1)}, bf16[4,160,256]{2,1,0:T(8,128)(2,1)S(1)}, u32[]{:S(2)}, u32[]{:S(2)}) collective-permute-start(bf16[4,160,256]{2,1,0:T(8,128)(2,1)} %get-tuple-element.144), channel_id=1, source_target_pairs={{0,1},{1,0},{2,3},{3,2},{4,5},{5,4},{6,7},{7,6},{8,9},{9,8},{10,11... | collective-permute-start | bytes 983048 | tf_op jit(solution)/shard_map/ppermute | solution.py:161
  96.1 11.5 %collective-permute-start.13 = (bf16[512,640]{1,0:T(8,128)(2,1)}, bf16[512,640]{1,0:T(8,128)(2,1)}, u32[]{:S(2)}, u32[]{:S(2)}) collective-permute-start(bf16[512,640]{1,0:T(8,128)(2,1)} %get-tuple-element.131), channel_id=1, source_target_pairs={{4,0},{0,4},{12,8},{8,12},{20,16},{16,20},{28,24},{24,28},{5,1},{1... | collective-permute-start | bytes 1966088 | tf_op jit(solution)/shard_map/ppermute | solution.py:1391
  106.5 23.2 %collective-permute-start.22 = (bf16[2,4,160,384]{3,2,1,0:T(8,128)(2,1)}, bf16[2,4,160,384]{3,2,1,0:T(8,128)(2,1)S(1)}, u32[]{:S(2)}, u32[]{:S(2)}) collective-permute-start(bf16[2,4,160,384]{3,2,1,0:T(8,128)(2,1)} %get-tuple-element.153), channel_id=1, source_target_pairs={{0,1},{1,0},{2,3},{3,2},{4,5},{5,4},{6,7},{7,6},{8,9},{9,8},{10,11... | collective-permute-start | bytes 2949128 | tf_op jit(solution)/shard_map/ppermute | solution.py:161
  106.8 22.9 %collective-permute-start.23 = (bf16[2,4,160,384]{3,2,1,0:T(8,128)(2,1)}, bf16[2,4,160,384]{3,2,1,0:T(8,128)(2,1)S(1)}, u32[]{:S(2)}, u32[]{:S(2)}) collective-permute-start(bf16[2,4,160,384]{3,2,1,0:T(8,128)(2,1)} %get-tuple-element.154), channel_id=1, source_target_pairs={{0,2},{1,3},{2,0},{3,1},{4,6},{5,7},{6,4},{7,5},{8,10},{9,11},{10,... | collective-permute-start | bytes 2949128 | tf_op jit(solution)/shard_map/ppermute | solution.py:161
  109.2 15.3 %collective-permute-start.14 = (bf16[2,128,640]{2,1,0:T(8,128)(2,1)S(1)}, bf16[2,128,640]{2,1,0:T(8,128)(2,1)S(1)}, u32[]{:S(2)}, u32[]{:S(2)}) collective-permute-start(bf16[2,128,640]{2,1,0:T(8,128)(2,1)S(1)} %get-tuple-element.133), channel_id=1, source_target_pairs={{0,8},{4,12},{8,0},{12,4},{16,24},{20,28},{24,16},{28,20},{1,9},{5... | collective-permute-start | bytes 983048 | tf_op jit(solution)/shard_map/ppermute | solution.py:161
  109.3 18.7 %collective-permute-start.21 = (bf16[2,2,160,256]{3,2,1,0:T(8,128)(2,1)S(1)}, bf16[2,2,160,256]{3,2,1,0:T(8,128)(2,1)S(1)}, u32[]{:S(2)}, u32[]{:S(2)}) collective-permute-start(bf16[2,2,160,256]{3,2,1,0:T(8,128)(2,1)S(1)} %copy-done.45), channel_id=1, source_target_pairs={{0,8},{4,12},{8,0},{12,4},{16,24},{20,28},{24,16},{28,20},{1,9},{5... | collective-permute-start | bytes 983048 | tf_op jit(solution)/shard_map/ppermute | solution.py:161
  124.6 22.4 %collective-permute-start.20 = (bf16[2,128,640]{2,1,0:T(8,128)(2,1)S(1)}, bf16[2,128,640]{2,1,0:T(8,128)(2,1)S(1)}, u32[]{:S(2)}, u32[]{:S(2)}) collective-permute-start(bf16[2,128,640]{2,1,0:T(8,128)(2,1)S(1)} %pass_on.1.refs_4_), channel_id=1, source_target_pairs={{0,16},{4,20},{8,24},{12,28},{16,0},{20,4},{24,8},{28,12},{1,17},{... | collective-permute-start | bytes 983048 | tf_op jit(solution)/shard_map/ppermute | solution.py:161
  125.8 29.0 %collective-permute-start.27 = (bf16[2,80,640]{2,1,0:T(8,128)(2,1)S(1)}, bf16[2,80,640]{2,1,0:T(8,128)(2,1)S(1)}, u32[]{:S(2)}, u32[]{:S(2)}) collective-permute-start(bf16[2,80,640]{2,1,0:T(8,128)(2,1)S(1)} %copy-done.46), channel_id=1, source_target_pairs={{4,0},{0,4},{12,8},{8,12},{20,16},{16,20},{28,24},{24,28},{5,1},{1... | collective-permute-start | bytes 614408 | tf_op jit(solution)/shard_map/ppermute | solution.py:1391
  128.1 18.9 %collective-permute-start.26 = (bf16[2,160,256]{2,1,0:T(8,128)(2,1)S(1)}, bf16[2,160,256]{2,1,0:T(8,128)(2,1)S(1)}, u32[]{:S(2)}, u32[]{:S(2)}) collective-permute-start(bf16[2,160,256]{2,1,0:T(8,128)(2,1)S(1)} %get-tuple-element.161), channel_id=1, source_target_pairs={{0,16},{4,20},{8,24},{12,28},{16,0},{20,4},{24,8},{28,12},{1,17},{... | collective-permute-start | bytes 491528 | tf_op jit(solution)/shard_map/ppermute | solution.py:161
  130.8 14.8 %collective-permute-start.24 = (bf16[4,160,384]{2,1,0:T(8,128)(2,1)S(1)}, bf16[4,160,384]{2,1,0:T(8,128)(2,1)S(1)}, u32[]{:S(2)}, u32[]{:S(2)}) collective-permute-start(bf16[4,160,384]{2,1,0:T(8,128)(2,1)S(1)} %get-tuple-element.158), channel_id=1, source_target_pairs={{0,2},{1,3},{2,0},{3,1},{4,6},{5,7},{6,4},{7,5},{8,10},{9,11},{10,... | collective-permute-start | bytes 1474568 | tf_op jit(solution)/shard_map/ppermute | solution.py:161
  131.1 14.6 %collective-permute-start.25 = (bf16[4,160,384]{2,1,0:T(8,128)(2,1)S(1)}, bf16[4,160,384]{2,1,0:T(8,128)(2,1)S(1)}, u32[]{:S(2)}, u32[]{:S(2)}) collective-permute-start(bf16[4,160,384]{2,1,0:T(8,128)(2,1)S(1)} %get-tuple-element.159), channel_id=1, source_target_pairs={{0,1},{1,0},{2,3},{3,2},{4,5},{5,4},{6,7},{7,6},{8,9},{9,8},{10,11... | collective-permute-start | bytes 1474568 | tf_op jit(solution)/shard_map/ppermute | solution.py:161
  146.9 14.6 %collective-permute-start.29 = (bf16[2,2,160,384]{3,2,1,0:T(8,128)(2,1)}, bf16[2,2,160,384]{3,2,1,0:T(8,128)(2,1)S(1)}, u32[]{:S(2)}, u32[]{:S(2)}) collective-permute-start(bf16[2,2,160,384]{3,2,1,0:T(8,128)(2,1)} %get-tuple-element.169), channel_id=1, source_target_pairs={{0,8},{4,12},{8,0},{12,4},{16,24},{20,28},{24,16},{28,20},{1,9},{5... | collective-permute-start | bytes 1474568 | tf_op jit(solution)/shard_map/ppermute | solution.py:161
  159.0 9.6 %collective-permute-start.28 = (bf16[4,80,1152]{2,1,0:T(8,128)(2,1)S(1)}, bf16[4,80,1152]{2,1,0:T(8,128)(2,1)S(1)}, u32[]{:S(2)}, u32[]{:S(2)}) collective-permute-start(bf16[4,80,1152]{2,1,0:T(8,128)(2,1)S(1)} %get-tuple-element.164), channel_id=1, source_target_pairs={{4,0},{0,4},{12,8},{8,12},{20,16},{16,20},{28,24},{24,28},{5,1},{1... | collective-permute-start | bytes 2211848 | tf_op jit(solution)/shard_map/ppermute | solution.py:1391
  165.8 4.9 %collective-permute-start.33 = (bf16[512,640]{1,0:T(8,128)(2,1)S(1)}, bf16[512,640]{1,0:T(8,128)(2,1)S(1)}, u32[]{:S(2)}, u32[]{:S(2)}) collective-permute-start(bf16[512,640]{1,0:T(8,128)(2,1)S(1)} %get-tuple-element.177), channel_id=1, source_target_pairs={{4,0},{0,4},{12,8},{8,12},{20,16},{16,20},{28,24},{24,28},{5,1},{1... | collective-permute-start | bytes 1966088 | tf_op jit(solution)/shard_map/ppermute | solution.py:1391
  166.8 1.8 collective-permute-start.30
  169.6 11.6 %collective-permute-start.31 = (bf16[352,640]{1,0:T(8,128)(2,1)S(1)}, bf16[352,640]{1,0:T(8,128)(2,1)S(1)}, u32[]{:S(2)}, u32[]{:S(2)}) collective-permute-start(bf16[352,640]{1,0:T(8,128)(2,1)S(1)} %get-tuple-element.174), channel_id=1, source_target_pairs={{0,1},{1,0},{2,3},{3,2},{4,5},{5,4},{6,7},{7,6},{8,9},{9,8},{10,11... | collective-permute-start | bytes 1351688 | tf_op jit(solution)/shard_map/ppermute | solution.py:161
  169.9 10.4 %collective-permute-start.32 = (bf16[320,640]{1,0:T(8,128)(2,1)S(1)}, bf16[320,640]{1,0:T(8,128)(2,1)S(1)}, u32[]{:S(2)}, u32[]{:S(2)}) collective-permute-start(bf16[320,640]{1,0:T(8,128)(2,1)S(1)} %get-tuple-element.175), channel_id=1, source_target_pairs={{0,2},{1,3},{2,0},{3,1},{4,6},{5,7},{6,4},{7,5},{8,10},{9,11},{10,... | collective-permute-start | bytes 1228808 | tf_op jit(solution)/shard_map/ppermute | solution.py:161
  172.2 9.1 %collective-permute-start.34 = (bf16[128,640]{1,0:T(8,128)(2,1)S(1)}, bf16[128,640]{1,0:T(8,128)(2,1)S(1)}, u32[]{:S(2)}, u32[]{:S(2)}) collective-permute-start(bf16[128,640]{1,0:T(8,128)(2,1)S(1)} %get-tuple-element.179), channel_id=1, source_target_pairs={{0,8},{4,12},{8,0},{12,4},{16,24},{20,28},{24,16},{28,20},{1,9},{5... | collective-permute-start | bytes 491528 | tf_op jit(solution)/shard_map/ppermute | solution.py:161
  173.9 7.4 %collective-permute-start.35 = (bf16[128,640]{1,0:T(8,128)(2,1)S(1)}, bf16[128,640]{1,0:T(8,128)(2,1)S(1)}, u32[]{:S(2)}, u32[]{:S(2)}) collective-permute-start(bf16[128,640]{1,0:T(8,128)(2,1)S(1)} %get-tuple-element.180), channel_id=1, source_target_pairs={{0,24},{4,28},{8,16},{12,20},{16,8},{20,12},{24,0},{28,4},{1,25},{... | collective-permute-start | bytes 491528 | tf_op jit(solution)/shard_map/ppermute | solution.py:161
  181.5 5.4 %collective-permute-start.36 = (bf16[192,640]{1,0:T(8,128)(2,1)S(1)}, bf16[192,640]{1,0:T(8,128)(2,1)S(1)}, u32[]{:S(2)}, u32[]{:S(2)}) collective-permute-start(bf16[192,640]{1,0:T(8,128)(2,1)S(1)} %get-tuple-element.183), channel_id=1, source_target_pairs={{0,2},{1,3},{2,0},{3,1},{4,6},{5,7},{6,4},{7,5},{8,10},{9,11},{10,... | collective-permute-start | bytes 737288 | tf_op jit(solution)/shard_map/ppermute | solution.py:161
  182.2 4.6 %collective-permute-start.37 = (bf16[160,640]{1,0:T(8,128)(2,1)S(1)}, bf16[160,640]{1,0:T(8,128)(2,1)S(1)}, u32[]{:S(2)}, u32[]{:S(2)}) collective-permute-start(bf16[160,640]{1,0:T(8,128)(2,1)S(1)} %get-tuple-element.184), channel_id=1, source_target_pairs={{0,1},{1,0},{2,3},{3,2},{4,5},{5,4},{6,7},{7,6},{8,9},{9,8},{10,11... | collective-permute-start | bytes 614408 | tf_op jit(solution)/shard_map/ppermute | solution.py:161
  182.5 17.3 %collective-permute-start.42 = (bf16[2,160,384]{2,1,0:T(8,128)(2,1)S(1)}, bf16[2,160,384]{2,1,0:T(8,128)(2,1)S(1)}, u32[]{:S(2)}, u32[]{:S(2)}) collective-permute-start(bf16[2,160,384]{2,1,0:T(8,128)(2,1)S(1)} %get-tuple-element.193), channel_id=1, source_target_pairs={{0,16},{4,20},{8,24},{12,28},{16,0},{20,4},{24,8},{28,12},{1,17},{... | collective-permute-start | bytes 737288 | tf_op jit(solution)/shard_map/ppermute | solution.py:161
  185.4 24.9 %collective-permute-start.38 = (bf16[128,640]{1,0:T(8,128)(2,1)}, bf16[128,640]{1,0:T(8,128)(2,1)S(1)}, u32[]{:S(2)}, u32[]{:S(2)}) collective-permute-start(bf16[128,640]{1,0:T(8,128)(2,1)} %get-tuple-element.186), channel_id=1, source_target_pairs={{0,16},{4,20},{8,24},{12,28},{16,0},{20,4},{24,8},{28,12},{1,17},{... | collective-permute-start | bytes 491528 | tf_op jit(solution)/shard_map/ppermute | solution.py:161
  187.6 24.4 %collective-permute-start.39 = (bf16[112,640]{1,0:T(8,128)(2,1)}, bf16[112,640]{1,0:T(8,128)(2,1)S(1)}, u32[]{:S(2)}, u32[]{:S(2)}) collective-permute-start(bf16[112,640]{1,0:T(8,128)(2,1)} %get-tuple-element.187), channel_id=1, source_target_pairs={{0,8},{4,12},{8,0},{12,4},{16,24},{20,28},{24,16},{28,20},{1,9},{5... | collective-permute-start | bytes 430088 | tf_op jit(solution)/shard_map/ppermute | solution.py:161
  190.2 21.9 %collective-permute-start.40 = (bf16[112,640]{1,0:T(8,128)(2,1)}, bf16[112,640]{1,0:T(8,128)(2,1)S(1)}, u32[]{:S(2)}, u32[]{:S(2)}) collective-permute-start(bf16[112,640]{1,0:T(8,128)(2,1)} %get-tuple-element.188), channel_id=1, source_target_pairs={{0,16},{4,20},{8,24},{12,28},{16,0},{20,4},{24,8},{28,12},{1,17},{... | collective-permute-start | bytes 430088 | tf_op jit(solution)/shard_map/ppermute | solution.py:161
  191.6 24.8 %collective-permute-start.41 = (bf16[112,640]{1,0:T(8,128)(2,1)S(1)}, bf16[112,640]{1,0:T(8,128)(2,1)S(1)}, u32[]{:S(2)}, u32[]{:S(2)}) collective-permute-start(bf16[112,640]{1,0:T(8,128)(2,1)S(1)} %get-tuple-element.189), channel_id=1, source_target_pairs={{0,24},{4,28},{8,16},{12,20},{16,8},{20,12},{24,0},{28,4},{1,25},{... | collective-permute-start | bytes 430088 | tf_op jit(solution)/shard_map/ppermute | solution.py:161
  200.2 11.1 %collective-permute-start.43 = (bf16[80,640]{1,0:T(8,128)(2,1)S(1)}, bf16[80,640]{1,0:T(8,128)(2,1)S(1)}, u32[]{:S(2)}, u32[]{:S(2)}) collective-permute-start(bf16[80,640]{1,0:T(8,128)(2,1)S(1)} %get-tuple-element.195), channel_id=1, source_target_pairs={{4,0},{0,4},{12,8},{8,12},{20,16},{16,20},{28,24},{24,28},{5,1},{1... | collective-permute-start | bytes 307208 | tf_op jit(solution)/shard_map/ppermute | solution.py:1391
  (43 other events, 302.4 us)
where the time goes:
time: 222 us; the launch traced here: 219 us
  Pallas kernels  120 us (54%)
  starting transfers between devices  54.7 us (25%)
  waiting for transfers between devices  28.8 us (13%)
  local copies, waits for them, and re-layouts  11 us (5%)
    pallas_call x30, Pallas kernels, run(): pl.pallas_call(inner, in_specs=specs + [ANY] * extra, out_specs=out_specs...  119 us
    ppermute x30, starting transfers between devices, swap(): return lax.ppermute(item, axis, [(i, i ^ distance) for i in range(size)])  27.3 us
    ppermute x14, starting transfers between devices, from_part(): return lax.ppermute(item, 'seq', pairs)  27.3 us
    ppermute x30, waiting for transfers between devices, swap(): return lax.ppermute(item, axis, [(i, i ^ distance) for i in range(size)])  24.2 us
    unnamed x95, local copies, waits for them, and re-layouts  9.52 us
    ppermute x14, waiting for transfers between devices, from_part(): return lax.ppermute(item, 'seq', pairs)  4.64 us
  transfers between devices with their start and end apart: 44, of which 11 were waited for; matrix products, arithmetic and copies ran while one was open for 2% of the time, Pallas kernels for 46%

commit v1 on v0

--- a/solution.py
+++ b/solution.py
@@ -405,7 +405,7 @@
             pltpu.SemaphoreType.DMA((2 * self.blocks,)),
         ]
 
-    def compute(self, part, second, second_t, grad, grad_t, acc, gs, ubg, scratch, outs):
+    def compute(self, second, second_t, grad, grad_t, ubg, scratch, outs, give):
         up_slots, down_slots, out_sem, acts, grad_pres, up_ref, down_ref, bias_ref, _ = scratch
         if not self.packed:
             up_slots, down_slots = outs
@@ -449,8 +449,7 @@
             acts[rows, :] = act
             grad_pres[rows, :] = grad_pre
             ubg[0:1, :] += jnp.sum(grad_pre.astype(F32), axis=0, keepdims=True)
-            acc[rows, :] += dot(act, down_ref[...])
-            gs[rows, :] += dot_nt(grad_pre, up_ref[...])
+            give(i, rows, dot(act, down_ref[...]), dot_nt(grad_pre, up_ref[...]))
             ready = ahead
         for n in range(self.count // self.chunk):
             weights(n)
@@ -487,7 +486,7 @@
         mid_ref, second, second_t, grad, grad_t, own_ref, low_ref, ubg, refs = *refs[7:15], refs[15:]
         send_refs, refs = refs[: pieces - 1], refs[pieces - 1 :]
         outs, refs = refs[: len(grads)], refs[len(grads) :]
-        acc, gs, mid_rows, mid_sem, *scratch = refs
+        mid_rows, mid_sem, *scratch = refs
         _, part, _ = place(pieces)
         loads = units.loads(part, up_hbm, down_hbm, ub_ref, *scratch[5:])
         for load in loads:
@@ -517,25 +516,27 @@
                 normed, _ = norm_rows(mid)
                 low = normed * gain_ref[...] + shift_ref[...]
                 second[dst, :] = low.astype(BF16)
-                second_t[:, dst] = low.T.astype(BF16)
-                grad_t[:, dst] = grad[dst, :].astype(F32).T.astype(BF16)
-                acc[dst, :] = mid + db_ref[...] if h == 0 else jnp.zeros((ROWS, width), F32)
-                gs[dst, :] = jnp.zeros((ROWS, width), F32)
+                second_t[:, dst] = low.astype(BF16).T
+                grad_t[:, dst] = grad[dst, :].T
 
         keep_mid = pltpu.make_async_copy(mid_rows, mid_ref, mid_sem)
         keep_mid.start()
         for load in loads:
             load.wait()
-        stores = units.compute(
-            part, second, second_t, grad, grad_t, acc, gs, ubg, scratch, outs
-        )
+
+        def give(i, rows, result, grad_second):
+            low_ref[rows, :] = grad_second.astype(BF16)
+            h = i * ROWS // piece_rows
+            at = slice(rows.start - h * piece_rows, rows.stop - h * piece_rows)
+            if h == 0:
+                own_ref[at, :] = mid_rows[rows, :] + db_ref[...] + result
+            else:
+                send_refs[h - 1][at, :] = result.astype(BF16)
+
+        stores = units.compute(second, second_t, grad, grad_t, ubg, scratch, outs, give)
         for store in stores:
             store.start()
         keep_mid.wait()
-        own_ref[...] = acc[0:piece_rows, :]
-        low_ref[...] = gs[...].astype(BF16)
-        for h in range(1, pieces):
-            send_refs[h - 1][...] = acc[h * piece_rows : (h + 1) * piece_rows, :].astype(BF16)
         for store in stores:
             store.wait()
 
@@ -563,10 +564,10 @@
         out_shape=[pltpu.HBM((total, width), F32), flat, turned, flat, turned, half, flat, sds((8, units.count), F32)]
         + [sds((piece_rows, width), BF16)] * (pieces - 1)
         + grads,
-        scratch_shapes=[pltpu.VMEM((total, width), F32)] * 3
+        scratch_shapes=[pltpu.VMEM((total, width), F32)]
         + [pltpu.SemaphoreType.DMA]
         + units.scratch(total, width),
-        vmem=26,
+        vmem=22,
         cost_estimate=cost(12 * total * width * units.count, 24 * 1024 * 1024, total * units.count),
         name="feed_first",
     )
@@ -586,26 +587,27 @@
         send_ins, refs = refs[: pieces - 1], refs[pieces - 1 :]
         own_ref, low_ref, ubg, refs = refs[0], refs[1], refs[2], refs[3:]
         send_refs, refs = refs[: pieces - 1], refs[pieces - 1 :]
-        outs, (acc, gs), scratch = refs[: len(grads)], refs[len(grads) :][:2], refs[len(grads) + 2 :]
+        outs, scratch = refs[: len(grads)], refs[len(grads) :]
         _, part, _ = place(pieces)
         loads = units.loads(part, up_hbm, down_hbm, ub_ref, *scratch[5:])
         for load in loads:
             load.start()
         ubg[...] = jnp.zeros_like(ubg)
-        acc[...] = jnp.zeros_like(acc)
-        gs[...] = jnp.zeros_like(gs)
         for load in loads:
             load.wait()
-        stores = units.compute(
-            part, second, second_t, grad, grad_t, acc, gs, ubg, scratch, outs
-        )
+
+        def give(i, rows, result, grad_second):
+            low_ref[rows, :] = (grad_second + low_in[rows, :].astype(F32)).astype(BF16)
+            h = i * ROWS // piece_rows
+            at = slice(rows.start - h * piece_rows, rows.stop - h * piece_rows)
+            if h == 0:
+                own_ref[at, :] = own_in[at, :] + result
+            else:
+                send_refs[h - 1][at, :] = (result + send_ins[h - 1][at, :].astype(F32)).astype(BF16)
+
+        stores = units.compute(second, second_t, grad, grad_t, ubg, scratch, outs, give)
         for store in stores:
             store.start()
-        low_ref[...] = (gs[...] + low_in[...].astype(F32)).astype(BF16)
-        own_ref[...] = acc[0:piece_rows, :] + own_in[...]
-        for h in range(1, pieces):
-            item = acc[h * piece_rows : (h + 1) * piece_rows, :] + send_ins[h - 1][...].astype(F32)
-            send_refs[h - 1][...] = item.astype(BF16)
         for store in stores:
             store.wait()
 
@@ -632,8 +634,8 @@
         ]
         + [sds((piece_rows, width), BF16)] * (pieces - 1)
         + grads,
-        scratch_shapes=[pltpu.VMEM((total, width), F32)] * 2 + units.scratch(total, width),
-        vmem=30,
+        scratch_shapes=units.scratch(total, width),
+        vmem=26,
         cost_estimate=cost(12 * total * width * units.count, 24 * 1024 * 1024, total * units.count),
         name="feed_second",
     )
@@ -1616,7 +1618,7 @@
             [swap(packed[1], "batch", batch_size, 1), swap(packed[3], "batch", batch_size, 2)],
             sequences // 2 * chunk,
             small_rows,
-            [row_parts[0], *row_moved[1::2]],
+            [row_parts[0], row_moved[1], unit_second[1]],
         )
         summed = sum_second_attention(
             [stay_a, stay_b],
@@ -1624,7 +1626,7 @@
             chunk,
             sequences,
             small_rows,
-            [],
+            row_moved[3:],
         )
         after = summed[:1]
         up_keep, up_send, down_grad = final_units(unit_first, unit_second, after)

time: 222 us -> 219 us (0.986)
  waiting for transfers between devices: 28.8 us -> 25.2 us
    ppermute x30, waiting for transfers between devices: 24.2 us -> 20.7 us  [swap(): return lax.ppermute(item, axis, [(i, i ^ distance) for i in range(size)])]
    ppermute x30, starting transfers between devices: 27.3 us -> 30.8 us  [swap(): return lax.ppermute(item, axis, [(i, i ^ distance) for i in range(size)])]
where the time goes in v1:
time: 219 us; the launch traced here: 216 us
  Pallas kernels  120 us (55%)
  starting transfers between devices  56.8 us (26%)
  waiting for transfers between devices  25.2 us (12%)
  local copies, waits for them, and re-layouts  10.7 us (5%)
    pallas_call x30, Pallas kernels, run(): pl.pallas_call(inner, in_specs=specs + [ANY] * extra, out_specs=out_specs...  119 us
    ppermute x30, starting transfers between devices, swap(): return lax.ppermute(item, axis, [(i, i ^ distance) for i in range(size)])  30.8 us
    ppermute x14, starting transfers between devices, from_part(): return lax.ppermute(item, 'seq', pairs)  25.9 us
    ppermute x30, waiting for transfers between devices, swap(): return lax.ppermute(item, axis, [(i, i ^ distance) for i in range(size)])  20.7 us
    unnamed x95, local copies, waits for them, and re-layouts  9.21 us
    ppermute x14, waiting for transfers between devices, from_part(): return lax.ppermute(item, 'seq', pairs)  4.56 us
  transfers between devices with their start and end apart: 44, of which 11 were waited for; matrix products, arithmetic and copies ran while one was open for 2% of the time, Pallas kernels for 46%

profile of v1, /device:TPU:9, one launch (start us, length us, event | category | flops | bytes accessed | tf_op | source)
XLA Modules:
  0.0 216.4 jit_solution(4922574260278021718)
XLA Ops:
  0.7 1.2 copy-done.17
  2.0 2.5 %collective-permute-start.1 = (bf16[128,640]{1,0:T(8,128)(2,1)S(1)}, bf16[128,640]{1,0:T(8,128)(2,1)S(1)}, u32[]{:S(2)}, u32[]{:S(2)}) collective-permute-start(bf16[128,640]{1,0:T(8,128)(2,1)S(1)} %get-tuple-element.108), channel_id=1, source_target_pairs={{0,16},{4,20},{8,24},{12,28},{16,0},{20,4},{24,8},{28,12},{1,17},{... | collective-permute-start | bytes 491528 | tf_op jit(solution)/shard_map/ppermute | solution.py:161
  4.6 1.5 collective-permute-start.3
  6.8 1.2 broadcast_select_fusion
  8.1 1.6 collective-permute-start.4
  9.7 1.9 collective-permute-done.1.refs_2_
  11.6 5.6 %collective-permute-start.5 = (bf16[128,640]{1,0:T(8,128)(2,1)S(1)}, bf16[128,640]{1,0:T(8,128)(2,1)S(1)}, u32[]{:S(2)}, u32[]{:S(2)}) collective-permute-start(bf16[128,640]{1,0:T(8,128)(2,1)S(1)} %collective-permute-done.1.refs_2_), channel_id=1, source_target_pairs={{4,0},{0,4},{12,8},{8,12},{20,16},{16,20},{28,24},{24,28},{5,1},{1... | collective-permute-start | bytes 491528 | tf_op jit(solution)/shard_map/ppermute | solution.py:1393
  17.2 1.4 collective-permute-done.2.refs_3_
  18.5 1.8 collective-permute-start.6
  20.7 1.7 copy-done.2
  23.7 2.5 %collective-permute-start.8 = (bf16[144,640]{1,0:T(8,128)(2,1)S(1)}, bf16[144,640]{1,0:T(8,128)(2,1)S(1)}, u32[]{:S(2)}, u32[]{:S(2)}) collective-permute-start(bf16[144,640]{1,0:T(8,128)(2,1)S(1)} %get-tuple-element.117), channel_id=1, source_target_pairs={{0,16},{4,20},{8,24},{12,28},{16,0},{20,4},{24,8},{28,12},{1,17},{... | collective-permute-start | bytes 552968 | tf_op jit(solution)/shard_map/ppermute | solution.py:161
  26.4 15.9 %attend_first.1 = (bf16[1024,640]{1,0:T(8,128)(2,1)S(1)}, bf16[1024,1152]{1,0:T(8,128)(2,1)S(1)}, bf16[1024,256]{1,0:T(8,128)(2,1)S(1)}, f32[1024,128]{1,0:T(8,128)S(1)}) custom-call(bf16[128,640]{1,0:T(8,128)(2,1)S(1)} %get-tuple-element.106.refs_0_, bf16[128,640]{1,0:T(8,128)(2,1)S(1)} %collective-permute-done.refs_1_, ...), custom_call_target="tpu_custom_call" | custom-call | flops 12247367680 | bytes 8388608 | tf_op jit(solution)/shard_map/attend_first/pallas_call | solution.py:70
  44.1 3.1 %attend_last.1 = (bf16[1024,128]{1,0:T(8,128)(2,1)S(1)}, f32[1024,128]{1,0:T(8,128)S(1)}) custom-call(bf16[1024,1152]{1,0:T(8,128)(2,1)S(1)} %get-tuple-element.114.refs_0_, bf16[4,144,640]{2,1,0:T(8,128)(2,1)S(1)} %stack.1.refs_1_), custom_call_target="tpu_custom_call" | custom-call | flops 2147483648 | bytes 2097152 | tf_op jit(solution)/shard_map/attend_last/pallas_call | solution.py:70
  49.7 16.8 %feed_first.1 = (f32[1024,640]{1,0:T(8,128)}, bf16[1024,640]{1,0:T(8,128)(2,1)S(1)}, bf16[640,1024]{1,0:T(8,128)(2,1)S(1)}, bf16[1024,640]{1,0:T(8,128)(2,1)S(1)...) custom-call(bf16[1024,640]{1,0:T(8,128)(2,1)S(1)} %get-tuple-element, ...), custom_call_target="tpu_custom_call" | custom-call | flops 8053063680 | bytes 25165824 | tf_op jit(solution)/shard_map/feed_first/pallas_call | solution.py:70
  67.1 1.2 collective-permute-start.15
  68.3 1.2 collective-permute-start.16
  69.6 22.2 %feed_second.1 = (f32[512,640]{1,0:T(8,128)S(1)}, bf16[1024,640]{1,0:T(8,128)(2,1)S(1)}, f32[8,1536]{1,0:T(8,128)S(1)}, bf16[512,640]{1,0:T(8,128)(2,1)}, bf16[2...) custom-call(bf16[1024,640]{1,0:T(8,128)(2,1)S(1)} %get-tuple-element, ...), custom_call_target="tpu_custom_call" | custom-call | flops 12079595520 | bytes 25165824 | tf_op jit(solution)/shard_map/feed_second/pallas_call | solution.py:70
  91.9 1.8 sum_first.2
  93.8 1.0 collective-permute-start.17
  95.9 1.7 collective-permute-done.17.refs_2_
  97.7 7.0 %mid_back.1 = (f32[512,640]{1,0:T(8,128)S(1)}, bf16[1024,384]{1,0:T(8,128)(2,1)S(1)}, f32[8,640]{1,0:T(8,128)S(1)}, bf16[2,80,640]{2,1,0:T(8,128)(2,1)}, bf16[2,80,640]{2,1,0:T(8,128)(2,1)}) custom-call(f32[1024,640]{1,0:T(8,128)} %get-tuple-element.134.refs_0_, bf16[1024,640]{1,0:T(8,128)(2,1)} %gate.2.refs_1_, ...), custom_call_target="tpu_custom_call" | custom-call | flops 1006632960 | bytes 14680064 | tf_op jit(solution)/shard_map/mid_back/pallas_call | solution.py:70
  106.7 1.6 finish_result.1
  108.4 1.4 collective-permute-start.21
  109.9 1.7 copy-done.4
  111.5 12.1 %attend_backward.3.refs_2_.refs_4_.refs_3_.refs_5_ = bf16[1024,384]{1,0:T(8,128)(2,1)S(1)} custom-call(bf16[1024,1152]{1,0:T(8,128)(2,1)S(1)} %copy-done.4, bf16[1024,384]{1,0:T(8,128)(2,1)S(1)} %get-tuple-element.141.refs_1_, bf16[1024,256]{1,0:T(8,128)(2,1)S(1)} %copy-done.6, f32[1024,128]{1,0:T(8,128)S(1)} %get-tuple-element.119.refs_4_.refs_3_, ...), custom_call_target="tpu_custom_call" | custom-call | flops 167772160 | bytes 49152 | tf_op jit(solution)/shard_map/attend_backward/pallas_call | solution.py:70
  123.7 1.2 collective-permute-start.20
  124.9 2.3 %collective-permute-start.27 = (bf16[2,80,640]{2,1,0:T(8,128)(2,1)S(1)}, bf16[2,80,640]{2,1,0:T(8,128)(2,1)S(1)}, u32[]{:S(2)}, u32[]{:S(2)}) collective-permute-start(bf16[2,80,640]{2,1,0:T(8,128)(2,1)S(1)} %copy-done.46), channel_id=1, source_target_pairs={{4,0},{0,4},{12,8},{8,12},{20,16},{16,20},{28,24},{24,28},{5,1},{1... | collective-permute-start | bytes 614408 | tf_op jit(solution)/shard_map/ppermute | solution.py:1393
  127.2 1.6 collective-permute-start.26
  128.9 1.1 sum_first.3
  130.2 1.2 collective-permute-start.25
  131.4 1.0 copy-done.20
  132.5 12.4 %attend_backward.4.refs_4_.refs_6_ = bf16[1024,384]{1,0:T(8,128)(2,1)S(1)} custom-call(bf16[1024,1152]{1,0:T(8,128)(2,1)S(1)} %copy-done.4, bf16[1024,384]{1,0:T(8,128)(2,1)S(1)} %get-tuple-element.141.refs_1_, bf16[1024,256]{1,0:T(8,128)(2,1)S(1)} %copy-done.6, f32[1024,128]{1,0:T(8,128)S(1)} %get-tuple-element.119.refs_4_.refs_3_, ...), custom_call_target="tpu_custom_call" | custom-call | flops 10737418240 | bytes 3145728 | tf_op jit(solution)/shard_map/attend_backward/pallas_call | solution.py:70
  144.9 1.1 sum_second.3
  146.2 1.1 copy-done.22
  147.3 6.5 %attend_backward.5.refs_5_.refs_7_ = bf16[1024,384]{1,0:T(8,128)(2,1)S(1)} custom-call(bf16[1024,1152]{1,0:T(8,128)(2,1)S(1)} %copy-done.4, bf16[1024,384]{1,0:T(8,128)(2,1)S(1)} %get-tuple-element.141.refs_1_, bf16[1024,128]{1,0:T(8,128)(2,1)S(1)} %copy-done.27, f32[1024,128]{1,0:T(8,128)S(1)} %copy-done.35, bf16[2,2,160,384]{3,2,1,0:T(8,128)(2,1)S(1)} %copy-done.22, ...), custom_call_target="tpu_custom_call" | custom-call | flops 5368709120 | bytes 3145728 | tf_op jit(solution)/shard_map/attend_backward/pallas_call | solution.py:70
  153.9 4.2 %project_weights.1 = (bf16[4,80,1152]{2,1,0:T(8,128)(2,1)S(1)}, bf16[4,80,1152]{2,1,0:T(8,128)(2,1)S(1)}) custom-call(bf16[1024,640]{1,0:T(8,128)(2,1)S(1)} %copy-done.9, f32[1,640]{1,0:T(1,128)S(1)} %broadcast_in_dim.49.refs_8_.refs_1_, f32[1,640]{1,0:T(1,128)S(1)} %broadcast_in_dim.50.refs_9_.refs_2_, ...), custom_call_target="tpu_custom_call" | custom-call | flops 1509949440 | bytes 6291456 | tf_op jit(solution)/shard_map/project_weights/pallas_call | solution.py:70
  158.1 2.4 %collective-permute-start.28 = (bf16[4,80,1152]{2,1,0:T(8,128)(2,1)S(1)}, bf16[4,80,1152]{2,1,0:T(8,128)(2,1)S(1)}, u32[]{:S(2)}, u32[]{:S(2)}) collective-permute-start(bf16[4,80,1152]{2,1,0:T(8,128)(2,1)S(1)} %get-tuple-element.164), channel_id=1, source_target_pairs={{4,0},{0,4},{12,8},{8,12},{20,16},{16,20},{28,24},{24,28},{5,1},{1... | collective-permute-start | bytes 2211848 | tf_op jit(solution)/shard_map/ppermute | solution.py:1393
  160.7 4.2 %project_rows.1 = (f32[512,640]{1,0:T(8,128)S(1)}, bf16[512,640]{1,0:T(8,128)(2,1)S(1)}, f32[16,640]{1,0:T(8,128)S(1)}, f32[8,1152]{1,0:T(8,128)}) custom-call(bf16[1024,640]{1,0:T(8,128)(2,1)S(1)} %copy-done.9, bf16[640,1152]{1,0:T(8,128)(2,1)S(1)} %copy-done.30, f32[8,640]{1,0:T(8,128)S(1)} %get-tuple-element.166.refs_2_, f32[8,1024]{1,0:T(8,128)S(1)} %copy-done.33, ...), custom_call_target="tpu_custom_call" | custom-call | flops 1509949440 | bytes 8388608 | tf_op jit(solution)/shard_map/project_rows/pallas_call | solution.py:70
  164.9 1.1 collective-permute-start.33
  165.9 1.8 collective-permute-done.30.refs_5_
  169.8 2.7 %collective-permute-start.35 = (bf16[2,160,384]{2,1,0:T(8,128)(2,1)S(1)}, bf16[2,160,384]{2,1,0:T(8,128)(2,1)S(1)}, u32[]{:S(2)}, u32[]{:S(2)}) collective-permute-start(bf16[2,160,384]{2,1,0:T(8,128)(2,1)S(1)} %get-tuple-element.180), channel_id=1, source_target_pairs={{0,16},{4,20},{8,24},{12,28},{16,0},{20,4},{24,8},{28,12},{1,17},{... | collective-permute-start | bytes 737288 | tf_op jit(solution)/shard_map/ppermute | solution.py:161
  173.5 9.4 %collective-permute-done.35.refs_6_.refs_3_ = bf16[2,160,384]{2,1,0:T(8,128)(2,1)S(1)} collective-permute-done((bf16[2,160,384]{2,1,0:T(8,128)(2,1)S(1)}, bf16[2,160,384]{2,1,0:T(8,128)(2,1)S(1)}, u32[]{:S(2)}, u32[]{:S(2)}) %collective-permute-start.35) | collective-permute-done | bytes 245792 | tf_op jit(solution)/shard_map/ppermute | solution.py:161
  183.9 1.2 collective-permute-start.37
  185.7 4.0 %collective-permute-start.39 = (bf16[128,640]{1,0:T(8,128)(2,1)S(1)}, bf16[128,640]{1,0:T(8,128)(2,1)S(1)}, u32[]{:S(2)}, u32[]{:S(2)}) collective-permute-start(bf16[128,640]{1,0:T(8,128)(2,1)S(1)} %get-tuple-element.187), channel_id=1, source_target_pairs={{0,16},{4,20},{8,24},{12,28},{16,0},{20,4},{24,8},{28,12},{1,17},{... | collective-permute-start | bytes 491528 | tf_op jit(solution)/shard_map/ppermute | solution.py:161
  191.0 3.9 %collective-permute-start.40 = (bf16[112,640]{1,0:T(8,128)(2,1)}, bf16[112,640]{1,0:T(8,128)(2,1)S(1)}, u32[]{:S(2)}, u32[]{:S(2)}) collective-permute-start(bf16[112,640]{1,0:T(8,128)(2,1)} %get-tuple-element.188), channel_id=1, source_target_pairs={{0,8},{4,12},{8,0},{12,4},{16,24},{20,28},{24,16},{28,20},{1,9},{5... | collective-permute-start | bytes 430088 | tf_op jit(solution)/shard_map/ppermute | solution.py:161
  197.1 6.8 %collective-permute-start.43 = (bf16[80,640]{1,0:T(8,128)(2,1)}, bf16[80,640]{1,0:T(8,128)(2,1)S(1)}, u32[]{:S(2)}, u32[]{:S(2)}) collective-permute-start(bf16[80,640]{1,0:T(8,128)(2,1)} %get-tuple-element.195), channel_id=1, source_target_pairs={{4,0},{0,4},{12,8},{8,12},{20,16},{16,20},{28,24},{24,28},{5,1},{1... | collective-permute-start | bytes 307208 | tf_op jit(solution)/shard_map/ppermute | solution.py:1393
  207.4 2.2 %collective-permute-done.41.refs_2_ = bf16[112,640]{1,0:T(8,128)(2,1)S(1)} collective-permute-done((bf16[112,640]{1,0:T(8,128)(2,1)}, bf16[112,640]{1,0:T(8,128)(2,1)S(1)}, u32[]{:S(2)}, u32[]{:S(2)}) %collective-permute-start.41) | collective-permute-done | bytes 143392 | tf_op jit(solution)/shard_map/ppermute | solution.py:161
  209.6 4.4 %collective-permute-done.42.refs_3_ = bf16[112,640]{1,0:T(8,128)(2,1)S(1)} collective-permute-done((bf16[112,640]{1,0:T(8,128)(2,1)S(1)}, bf16[112,640]{1,0:T(8,128)(2,1)S(1)}, u32[]{:S(2)}, u32[]{:S(2)}) %collective-permute-start.42) | collective-permute-done | bytes 143392 | tf_op jit(solution)/shard_map/ppermute | solution.py:161
  (188 shorter events, 25.0 us)
Async XLA Ops:
  1.9 6.2 %collective-permute-start = (bf16[128,640]{1,0:T(8,128)(2,1)S(1)}, bf16[128,640]{1,0:T(8,128)(2,1)S(1)}, u32[]{:S(2)}, u32[]{:S(2)}) collective-permute-start(bf16[128,640]{1,0:T(8,128)(2,1)S(1)} %get-tuple-element.107), channel_id=1, source_target_pairs={{0,8},{4,12},{8,0},{12,4},{16,24},{20,28},{24,16},{28,20},{1,9},{5... | collective-permute-start | bytes 491528 | tf_op jit(solution)/shard_map/ppermute | solution.py:161
  2.0 9.6 %collective-permute-start.1 = (bf16[128,640]{1,0:T(8,128)(2,1)S(1)}, bf16[128,640]{1,0:T(8,128)(2,1)S(1)}, u32[]{:S(2)}, u32[]{:S(2)}) collective-permute-start(bf16[128,640]{1,0:T(8,128)(2,1)S(1)} %get-tuple-element.108), channel_id=1, source_target_pairs={{0,16},{4,20},{8,24},{12,28},{16,0},{20,4},{24,8},{28,12},{1,17},{... | collective-permute-start | bytes 491528 | tf_op jit(solution)/shard_map/ppermute | solution.py:161
  4.5 14.1 %collective-permute-start.2 = (bf16[128,640]{1,0:T(8,128)(2,1)S(1)}, bf16[128,640]{1,0:T(8,128)(2,1)S(1)}, u32[]{:S(2)}, u32[]{:S(2)}) collective-permute-start(bf16[128,640]{1,0:T(8,128)(2,1)S(1)} %get-tuple-element.109), channel_id=1, source_target_pairs={{0,24},{4,28},{8,16},{12,20},{16,8},{20,12},{24,0},{28,4},{1,25},{... | collective-permute-start | bytes 491528 | tf_op jit(solution)/shard_map/ppermute | solution.py:161
  4.6 18.9 %collective-permute-start.3 = (bf16[128,640]{1,0:T(8,128)(2,1)S(1)}, bf16[128,640]{1,0:T(8,128)(2,1)S(1)}, u32[]{:S(2)}, u32[]{:S(2)}) collective-permute-start(bf16[128,640]{1,0:T(8,128)(2,1)S(1)} %get-tuple-element.106.refs_0_), channel_id=1, source_target_pairs={{4,0},{0,4},{12,8},{8,12},{20,16},{16,20},{28,24},{24,28},{5,1},{1... | collective-permute-start | bytes 491528 | tf_op jit(solution)/shard_map/ppermute | solution.py:1393
  8.1 15.5 %collective-permute-start.4 = (bf16[128,640]{1,0:T(8,128)(2,1)S(1)}, bf16[128,640]{1,0:T(8,128)(2,1)S(1)}, u32[]{:S(2)}, u32[]{:S(2)}) collective-permute-start(bf16[128,640]{1,0:T(8,128)(2,1)S(1)} %collective-permute-done.refs_1_), channel_id=1, source_target_pairs={{4,0},{0,4},{12,8},{8,12},{20,16},{16,20},{28,24},{24,28},{5,1},{1... | collective-permute-start | bytes 491528 | tf_op jit(solution)/shard_map/ppermute | solution.py:1393
  11.6 11.9 %collective-permute-start.5 = (bf16[128,640]{1,0:T(8,128)(2,1)S(1)}, bf16[128,640]{1,0:T(8,128)(2,1)S(1)}, u32[]{:S(2)}, u32[]{:S(2)}) collective-permute-start(bf16[128,640]{1,0:T(8,128)(2,1)S(1)} %collective-permute-done.1.refs_2_), channel_id=1, source_target_pairs={{4,0},{0,4},{12,8},{8,12},{20,16},{16,20},{28,24},{24,28},{5,1},{1... | collective-permute-start | bytes 491528 | tf_op jit(solution)/shard_map/ppermute | solution.py:1393
  18.5 5.0 %collective-permute-start.6 = (bf16[128,640]{1,0:T(8,128)(2,1)S(1)}, bf16[128,640]{1,0:T(8,128)(2,1)S(1)}, u32[]{:S(2)}, u32[]{:S(2)}) collective-permute-start(bf16[128,640]{1,0:T(8,128)(2,1)S(1)} %collective-permute-done.2.refs_3_), channel_id=1, source_target_pairs={{4,0},{0,4},{12,8},{8,12},{20,16},{16,20},{28,24},{24,28},{5,1},{1... | collective-permute-start | bytes 491528 | tf_op jit(solution)/shard_map/ppermute | solution.py:1393
  23.4 26.2 %copy-start.18 = (bf16[384,640]{1,0:T(8,128)(2,1)}, bf16[384,640]{1,0:T(8,128)(2,1)S(1)}, u32[]{:S(2)}) copy-start(bf16[384,640]{1,0:T(8,128)(2,1)S(1)} %get-tuple-element.121.refs_13_.refs_5_) | copy-start | bytes 1474564
  23.7 18.6 %collective-permute-start.7 = (bf16[144,640]{1,0:T(8,128)(2,1)S(1)}, bf16[144,640]{1,0:T(8,128)(2,1)S(1)}, u32[]{:S(2)}, u32[]{:S(2)}) collective-permute-start(bf16[144,640]{1,0:T(8,128)(2,1)S(1)} %get-tuple-element.116), channel_id=1, source_target_pairs={{0,8},{4,12},{8,0},{12,4},{16,24},{20,28},{24,16},{28,20},{1,9},{5... | collective-permute-start | bytes 552968 | tf_op jit(solution)/shard_map/ppermute | solution.py:161
  23.7 18.6 %collective-permute-start.8 = (bf16[144,640]{1,0:T(8,128)(2,1)S(1)}, bf16[144,640]{1,0:T(8,128)(2,1)S(1)}, u32[]{:S(2)}, u32[]{:S(2)}) collective-permute-start(bf16[144,640]{1,0:T(8,128)(2,1)S(1)} %get-tuple-element.117), channel_id=1, source_target_pairs={{0,16},{4,20},{8,24},{12,28},{16,0},{20,4},{24,8},{28,12},{1,17},{... | collective-permute-start | bytes 552968 | tf_op jit(solution)/shard_map/ppermute | solution.py:161
  26.2 17.0 %collective-permute-start.9 = (bf16[144,640]{1,0:T(8,128)(2,1)S(1)}, bf16[144,640]{1,0:T(8,128)(2,1)S(1)}, u32[]{:S(2)}, u32[]{:S(2)}) collective-permute-start(bf16[144,640]{1,0:T(8,128)(2,1)S(1)} %get-tuple-element.118), channel_id=1, source_target_pairs={{0,24},{4,28},{8,16},{12,20},{16,8},{20,12},{24,0},{28,4},{1,25},{... | collective-permute-start | bytes 552968 | tf_op jit(solution)/shard_map/ppermute | solution.py:161
  43.3 5.2 %collective-permute-start.12 = (bf16[4,144,640]{2,1,0:T(8,128)(2,1)S(1)}, bf16[4,144,640]{2,1,0:T(8,128)(2,1)S(1)}, u32[]{:S(2)}, u32[]{:S(2)}) collective-permute-start(bf16[4,144,640]{2,1,0:T(8,128)(2,1)S(1)} %stack.1.refs_1_), channel_id=1, source_target_pairs={{4,0},{0,4},{12,8},{8,12},{20,16},{16,20},{28,24},{24,28},{5,1},{1... | collective-permute-start | bytes 2211848 | tf_op jit(solution)/shard_map/ppermute | solution.py:1393
  44.0 5.6 %collective-permute-start.10 = (bf16[1024,256]{1,0:T(8,128)(2,1)S(1)}, bf16[1024,256]{1,0:T(8,128)(2,1)S(1)}, u32[]{:S(2)}, u32[]{:S(2)}) collective-permute-start(bf16[1024,256]{1,0:T(8,128)(2,1)S(1)} %get-tuple-element.113.refs_1_.refs_6_.refs_2_), channel_id=1, source_target_pairs={{4,0},{0,4},{12,8},{8,12},{20,16},{16,20},{28,24},{24,28},{5,1},{1... | collective-permute-start | bytes 1572872 | tf_op jit(solution)/shard_map/ppermute | solution.py:1393
  48.0 1.6 collective-permute-start.11
  67.1 24.7 %copy-start.10 = (bf16[1024,640]{1,0:T(8,128)(2,1)}, bf16[1024,640]{1,0:T(8,128)(2,1)S(1)}, u32[]{:S(2)}) copy-start(bf16[1024,640]{1,0:T(8,128)(2,1)S(1)} %get-tuple-element.125.refs_2_.refs_3_) | copy-start | bytes 3932164
  67.1 24.7 %collective-permute-start.15 = (bf16[2,4,160,256]{3,2,1,0:T(8,128)(2,1)}, bf16[2,4,160,256]{3,2,1,0:T(8,128)(2,1)S(1)}, u32[]{:S(2)}, u32[]{:S(2)}) collective-permute-start(bf16[2,4,160,256]{3,2,1,0:T(8,128)(2,1)} %get-tuple-element.138), channel_id=1, source_target_pairs={{0,1},{1,0},{2,3},{3,2},{4,5},{5,4},{6,7},{7,6},{8,9},{9,8},{10,11... | collective-permute-start | bytes 1966088 | tf_op jit(solution)/shard_map/ppermute | solution.py:161
  68.3 23.5 %collective-permute-start.16 = (bf16[2,4,160,256]{3,2,1,0:T(8,128)(2,1)}, bf16[2,4,160,256]{3,2,1,0:T(8,128)(2,1)S(1)}, u32[]{:S(2)}, u32[]{:S(2)}) collective-permute-start(bf16[2,4,160,256]{3,2,1,0:T(8,128)(2,1)} %get-tuple-element.139), channel_id=1, source_target_pairs={{0,2},{1,3},{2,0},{3,1},{4,6},{5,7},{6,4},{7,5},{8,10},{9,11},{10,... | collective-permute-start | bytes 1966088 | tf_op jit(solution)/shard_map/ppermute | solution.py:161
  69.6 22.3 %copy-start.15 = (bf16[2,4,160,256]{3,2,1,0:T(8,128)(2,1)S(1)}, bf16[2,4,160,256]{3,2,1,0:T(8,128)(2,1)}, u32[]{:S(2)}) copy-start(bf16[2,4,160,256]{3,2,1,0:T(8,128)(2,1)} %get-tuple-element.136.refs_0_) | copy-start | bytes 1966084
  69.6 22.3 %copy-start.16 = (bf16[2,4,160,256]{3,2,1,0:T(8,128)(2,1)S(1)}, bf16[2,4,160,256]{3,2,1,0:T(8,128)(2,1)}, u32[]{:S(2)}) copy-start(bf16[2,4,160,256]{3,2,1,0:T(8,128)(2,1)} %get-tuple-element.137.refs_1_) | copy-start | bytes 1966084
  93.8 3.9 %collective-permute-start.17 = (bf16[1024,640]{1,0:T(8,128)(2,1)}, bf16[1024,640]{1,0:T(8,128)(2,1)S(1)}, u32[]{:S(2)}, u32[]{:S(2)}) collective-permute-start(bf16[1024,640]{1,0:T(8,128)(2,1)} %gate.2.refs_1_), channel_id=1, source_target_pairs={{4,0},{0,4},{12,8},{8,12},{20,16},{16,20},{28,24},{24,28},{5,1},{1... | collective-permute-start | bytes 3932168 | tf_op jit(solution)/shard_map/ppermute | solution.py:1393
  94.8 9.9 %collective-permute-start.18 = (bf16[4,160,256]{2,1,0:T(8,128)(2,1)}, bf16[4,160,256]{2,1,0:T(8,128)(2,1)S(1)}, u32[]{:S(2)}, u32[]{:S(2)}) collective-permute-start(bf16[4,160,256]{2,1,0:T(8,128)(2,1)} %get-tuple-element.143), channel_id=1, source_target_pairs={{0,2},{1,3},{2,0},{3,1},{4,6},{5,7},{6,4},{7,5},{8,10},{9,11},{10,... | collective-permute-start | bytes 983048 | tf_op jit(solution)/shard_map/ppermute | solution.py:161
  95.0 9.7 %collective-permute-start.19 = (bf16[4,160,256]{2,1,0:T(8,128)(2,1)}, bf16[4,160,256]{2,1,0:T(8,128)(2,1)S(1)}, u32[]{:S(2)}, u32[]{:S(2)}) collective-permute-start(bf16[4,160,256]{2,1,0:T(8,128)(2,1)} %get-tuple-element.144), channel_id=1, source_target_pairs={{0,1},{1,0},{2,3},{3,2},{4,5},{5,4},{6,7},{7,6},{8,9},{9,8},{10,11... | collective-permute-start | bytes 983048 | tf_op jit(solution)/shard_map/ppermute | solution.py:161
  95.3 11.4 %collective-permute-start.13 = (bf16[512,640]{1,0:T(8,128)(2,1)}, bf16[512,640]{1,0:T(8,128)(2,1)}, u32[]{:S(2)}, u32[]{:S(2)}) collective-permute-start(bf16[512,640]{1,0:T(8,128)(2,1)} %get-tuple-element.131), channel_id=1, source_target_pairs={{4,0},{0,4},{12,8},{8,12},{20,16},{16,20},{28,24},{24,28},{5,1},{1... | collective-permute-start | bytes 1966088 | tf_op jit(solution)/shard_map/ppermute | solution.py:1393
  105.7 23.2 %collective-permute-start.22 = (bf16[2,4,160,384]{3,2,1,0:T(8,128)(2,1)}, bf16[2,4,160,384]{3,2,1,0:T(8,128)(2,1)S(1)}, u32[]{:S(2)}, u32[]{:S(2)}) collective-permute-start(bf16[2,4,160,384]{3,2,1,0:T(8,128)(2,1)} %get-tuple-element.153), channel_id=1, source_target_pairs={{0,1},{1,0},{2,3},{3,2},{4,5},{5,4},{6,7},{7,6},{8,9},{9,8},{10,11... | collective-permute-start | bytes 2949128 | tf_op jit(solution)/shard_map/ppermute | solution.py:161
  106.0 22.9 %collective-permute-start.23 = (bf16[2,4,160,384]{3,2,1,0:T(8,128)(2,1)}, bf16[2,4,160,384]{3,2,1,0:T(8,128)(2,1)S(1)}, u32[]{:S(2)}, u32[]{:S(2)}) collective-permute-start(bf16[2,4,160,384]{3,2,1,0:T(8,128)(2,1)} %get-tuple-element.154), channel_id=1, source_target_pairs={{0,2},{1,3},{2,0},{3,1},{4,6},{5,7},{6,4},{7,5},{8,10},{9,11},{10,... | collective-permute-start | bytes 2949128 | tf_op jit(solution)/shard_map/ppermute | solution.py:161
  108.3 15.3 %collective-permute-start.14 = (bf16[2,128,640]{2,1,0:T(8,128)(2,1)S(1)}, bf16[2,128,640]{2,1,0:T(8,128)(2,1)S(1)}, u32[]{:S(2)}, u32[]{:S(2)}) collective-permute-start(bf16[2,128,640]{2,1,0:T(8,128)(2,1)S(1)} %get-tuple-element.133), channel_id=1, source_target_pairs={{0,8},{4,12},{8,0},{12,4},{16,24},{20,28},{24,16},{28,20},{1,9},{5... | collective-permute-start | bytes 983048 | tf_op jit(solution)/shard_map/ppermute | solution.py:161
  108.4 18.7 %collective-permute-start.21 = (bf16[2,2,160,256]{3,2,1,0:T(8,128)(2,1)S(1)}, bf16[2,2,160,256]{3,2,1,0:T(8,128)(2,1)S(1)}, u32[]{:S(2)}, u32[]{:S(2)}) collective-permute-start(bf16[2,2,160,256]{3,2,1,0:T(8,128)(2,1)S(1)} %copy-done.45), channel_id=1, source_target_pairs={{0,8},{4,12},{8,0},{12,4},{16,24},{20,28},{24,16},{28,20},{1,9},{5... | collective-permute-start | bytes 983048 | tf_op jit(solution)/shard_map/ppermute | solution.py:161
  123.7 22.5 %collective-permute-start.20 = (bf16[2,128,640]{2,1,0:T(8,128)(2,1)S(1)}, bf16[2,128,640]{2,1,0:T(8,128)(2,1)S(1)}, u32[]{:S(2)}, u32[]{:S(2)}) collective-permute-start(bf16[2,128,640]{2,1,0:T(8,128)(2,1)S(1)} %pass_on.1.refs_4_), channel_id=1, source_target_pairs={{0,16},{4,20},{8,24},{12,28},{16,0},{20,4},{24,8},{28,12},{1,17},{... | collective-permute-start | bytes 983048 | tf_op jit(solution)/shard_map/ppermute | solution.py:161
  124.9 29.0 %collective-permute-start.27 = (bf16[2,80,640]{2,1,0:T(8,128)(2,1)S(1)}, bf16[2,80,640]{2,1,0:T(8,128)(2,1)S(1)}, u32[]{:S(2)}, u32[]{:S(2)}) collective-permute-start(bf16[2,80,640]{2,1,0:T(8,128)(2,1)S(1)} %copy-done.46), channel_id=1, source_target_pairs={{4,0},{0,4},{12,8},{8,12},{20,16},{16,20},{28,24},{24,28},{5,1},{1... | collective-permute-start | bytes 614408 | tf_op jit(solution)/shard_map/ppermute | solution.py:1393
  127.2 18.9 %collective-permute-start.26 = (bf16[2,160,256]{2,1,0:T(8,128)(2,1)S(1)}, bf16[2,160,256]{2,1,0:T(8,128)(2,1)S(1)}, u32[]{:S(2)}, u32[]{:S(2)}) collective-permute-start(bf16[2,160,256]{2,1,0:T(8,128)(2,1)S(1)} %get-tuple-element.161), channel_id=1, source_target_pairs={{0,16},{4,20},{8,24},{12,28},{16,0},{20,4},{24,8},{28,12},{1,17},{... | collective-permute-start | bytes 491528 | tf_op jit(solution)/shard_map/ppermute | solution.py:161
  130.0 14.8 %collective-permute-start.24 = (bf16[4,160,384]{2,1,0:T(8,128)(2,1)S(1)}, bf16[4,160,384]{2,1,0:T(8,128)(2,1)S(1)}, u32[]{:S(2)}, u32[]{:S(2)}) collective-permute-start(bf16[4,160,384]{2,1,0:T(8,128)(2,1)S(1)} %get-tuple-element.158), channel_id=1, source_target_pairs={{0,2},{1,3},{2,0},{3,1},{4,6},{5,7},{6,4},{7,5},{8,10},{9,11},{10,... | collective-permute-start | bytes 1474568 | tf_op jit(solution)/shard_map/ppermute | solution.py:161
  130.2 14.6 %collective-permute-start.25 = (bf16[4,160,384]{2,1,0:T(8,128)(2,1)S(1)}, bf16[4,160,384]{2,1,0:T(8,128)(2,1)S(1)}, u32[]{:S(2)}, u32[]{:S(2)}) collective-permute-start(bf16[4,160,384]{2,1,0:T(8,128)(2,1)S(1)} %get-tuple-element.159), channel_id=1, source_target_pairs={{0,1},{1,0},{2,3},{3,2},{4,5},{5,4},{6,7},{7,6},{8,9},{9,8},{10,11... | collective-permute-start | bytes 1474568 | tf_op jit(solution)/shard_map/ppermute | solution.py:161
  146.0 14.5 %collective-permute-start.29 = (bf16[2,2,160,384]{3,2,1,0:T(8,128)(2,1)}, bf16[2,2,160,384]{3,2,1,0:T(8,128)(2,1)S(1)}, u32[]{:S(2)}, u32[]{:S(2)}) collective-permute-start(bf16[2,2,160,384]{3,2,1,0:T(8,128)(2,1)} %get-tuple-element.169), channel_id=1, source_target_pairs={{0,8},{4,12},{8,0},{12,4},{16,24},{20,28},{24,16},{28,20},{1,9},{5... | collective-permute-start | bytes 1474568 | tf_op jit(solution)/shard_map/ppermute | solution.py:161
  158.1 9.6 %collective-permute-start.28 = (bf16[4,80,1152]{2,1,0:T(8,128)(2,1)S(1)}, bf16[4,80,1152]{2,1,0:T(8,128)(2,1)S(1)}, u32[]{:S(2)}, u32[]{:S(2)}) collective-permute-start(bf16[4,80,1152]{2,1,0:T(8,128)(2,1)S(1)} %get-tuple-element.164), channel_id=1, source_target_pairs={{4,0},{0,4},{12,8},{8,12},{20,16},{16,20},{28,24},{24,28},{5,1},{1... | collective-permute-start | bytes 2211848 | tf_op jit(solution)/shard_map/ppermute | solution.py:1393
  164.9 7.7 %collective-permute-start.33 = (bf16[512,640]{1,0:T(8,128)(2,1)S(1)}, bf16[512,640]{1,0:T(8,128)(2,1)S(1)}, u32[]{:S(2)}, u32[]{:S(2)}) collective-permute-start(bf16[512,640]{1,0:T(8,128)(2,1)S(1)} %get-tuple-element.177), channel_id=1, source_target_pairs={{4,0},{0,4},{12,8},{8,12},{20,16},{16,20},{28,24},{24,28},{5,1},{1... | collective-permute-start | bytes 1966088 | tf_op jit(solution)/shard_map/ppermute | solution.py:1393
  165.9 1.8 collective-permute-start.30
  168.7 14.2 %collective-permute-start.31 = (bf16[352,640]{1,0:T(8,128)(2,1)S(1)}, bf16[352,640]{1,0:T(8,128)(2,1)S(1)}, u32[]{:S(2)}, u32[]{:S(2)}) collective-permute-start(bf16[352,640]{1,0:T(8,128)(2,1)S(1)} %get-tuple-element.174), channel_id=1, source_target_pairs={{0,1},{1,0},{2,3},{3,2},{4,5},{5,4},{6,7},{7,6},{8,9},{9,8},{10,11... | collective-permute-start | bytes 1351688 | tf_op jit(solution)/shard_map/ppermute | solution.py:161
  169.0 13.9 %collective-permute-start.32 = (bf16[320,640]{1,0:T(8,128)(2,1)S(1)}, bf16[320,640]{1,0:T(8,128)(2,1)S(1)}, u32[]{:S(2)}, u32[]{:S(2)}) collective-permute-start(bf16[320,640]{1,0:T(8,128)(2,1)S(1)} %get-tuple-element.175), channel_id=1, source_target_pairs={{0,2},{1,3},{2,0},{3,1},{4,6},{5,7},{6,4},{7,5},{8,10},{9,11},{10,... | collective-permute-start | bytes 1228808 | tf_op jit(solution)/shard_map/ppermute | solution.py:161
  169.8 13.1 %collective-permute-start.35 = (bf16[2,160,384]{2,1,0:T(8,128)(2,1)S(1)}, bf16[2,160,384]{2,1,0:T(8,128)(2,1)S(1)}, u32[]{:S(2)}, u32[]{:S(2)}) collective-permute-start(bf16[2,160,384]{2,1,0:T(8,128)(2,1)S(1)} %get-tuple-element.180), channel_id=1, source_target_pairs={{0,16},{4,20},{8,24},{12,28},{16,0},{20,4},{24,8},{28,12},{1,17},{... | collective-permute-start | bytes 737288 | tf_op jit(solution)/shard_map/ppermute | solution.py:161
  173.4 9.5 %collective-permute-start.34 = (bf16[128,640]{1,0:T(8,128)(2,1)S(1)}, bf16[128,640]{1,0:T(8,128)(2,1)S(1)}, u32[]{:S(2)}, u32[]{:S(2)}) collective-permute-start(bf16[128,640]{1,0:T(8,128)(2,1)S(1)} %get-tuple-element.179), channel_id=1, source_target_pairs={{0,8},{4,12},{8,0},{12,4},{16,24},{20,28},{24,16},{28,20},{1,9},{5... | collective-permute-start | bytes 491528 | tf_op jit(solution)/shard_map/ppermute | solution.py:161
  183.2 7.1 %collective-permute-start.36 = (bf16[192,640]{1,0:T(8,128)(2,1)S(1)}, bf16[192,640]{1,0:T(8,128)(2,1)S(1)}, u32[]{:S(2)}, u32[]{:S(2)}) collective-permute-start(bf16[192,640]{1,0:T(8,128)(2,1)S(1)} %get-tuple-element.183), channel_id=1, source_target_pairs={{0,2},{1,3},{2,0},{3,1},{4,6},{5,7},{6,4},{7,5},{8,10},{9,11},{10,... | collective-permute-start | bytes 737288 | tf_op jit(solution)/shard_map/ppermute | solution.py:161
  183.9 5.9 %collective-permute-start.37 = (bf16[160,640]{1,0:T(8,128)(2,1)S(1)}, bf16[160,640]{1,0:T(8,128)(2,1)S(1)}, u32[]{:S(2)}, u32[]{:S(2)}) collective-permute-start(bf16[160,640]{1,0:T(8,128)(2,1)S(1)} %get-tuple-element.184), channel_id=1, source_target_pairs={{0,1},{1,0},{2,3},{3,2},{4,5},{5,4},{6,7},{7,6},{8,9},{9,8},{10,11... | collective-permute-start | bytes 614408 | tf_op jit(solution)/shard_map/ppermute | solution.py:161
  185.1 4.6 %collective-permute-start.38 = (bf16[128,640]{1,0:T(8,128)(2,1)S(1)}, bf16[128,640]{1,0:T(8,128)(2,1)S(1)}, u32[]{:S(2)}, u32[]{:S(2)}) collective-permute-start(bf16[128,640]{1,0:T(8,128)(2,1)S(1)} %get-tuple-element.185), channel_id=1, source_target_pairs={{0,24},{4,28},{8,16},{12,20},{16,8},{20,12},{24,0},{28,4},{1,25},{... | collective-permute-start | bytes 491528 | tf_op jit(solution)/shard_map/ppermute | solution.py:161
  185.7 20.0 %collective-permute-start.39 = (bf16[128,640]{1,0:T(8,128)(2,1)S(1)}, bf16[128,640]{1,0:T(8,128)(2,1)S(1)}, u32[]{:S(2)}, u32[]{:S(2)}) collective-permute-start(bf16[128,640]{1,0:T(8,128)(2,1)S(1)} %get-tuple-element.187), channel_id=1, source_target_pairs={{0,16},{4,20},{8,24},{12,28},{16,0},{20,4},{24,8},{28,12},{1,17},{... | collective-permute-start | bytes 491528 | tf_op jit(solution)/shard_map/ppermute | solution.py:161
  191.0 16.4 %collective-permute-start.40 = (bf16[112,640]{1,0:T(8,128)(2,1)}, bf16[112,640]{1,0:T(8,128)(2,1)S(1)}, u32[]{:S(2)}, u32[]{:S(2)}) collective-permute-start(bf16[112,640]{1,0:T(8,128)(2,1)} %get-tuple-element.188), channel_id=1, source_target_pairs={{0,8},{4,12},{8,0},{12,4},{16,24},{20,28},{24,16},{28,20},{1,9},{5... | collective-permute-start | bytes 430088 | tf_op jit(solution)/shard_map/ppermute | solution.py:161
  194.9 14.7 %collective-permute-start.41 = (bf16[112,640]{1,0:T(8,128)(2,1)}, bf16[112,640]{1,0:T(8,128)(2,1)S(1)}, u32[]{:S(2)}, u32[]{:S(2)}) collective-permute-start(bf16[112,640]{1,0:T(8,128)(2,1)} %get-tuple-element.189), channel_id=1, source_target_pairs={{0,16},{4,20},{8,24},{12,28},{16,0},{20,4},{24,8},{28,12},{1,17},{... | collective-permute-start | bytes 430088 | tf_op jit(solution)/shard_map/ppermute | solution.py:161
  195.5 18.5 %collective-permute-start.42 = (bf16[112,640]{1,0:T(8,128)(2,1)S(1)}, bf16[112,640]{1,0:T(8,128)(2,1)S(1)}, u32[]{:S(2)}, u32[]{:S(2)}) collective-permute-start(bf16[112,640]{1,0:T(8,128)(2,1)S(1)} %get-tuple-element.190), channel_id=1, source_target_pairs={{0,24},{4,28},{8,16},{12,20},{16,8},{20,12},{24,0},{28,4},{1,25},{... | collective-permute-start | bytes 430088 | tf_op jit(solution)/shard_map/ppermute | solution.py:161
  197.1 9.6 %collective-permute-start.43 = (bf16[80,640]{1,0:T(8,128)(2,1)}, bf16[80,640]{1,0:T(8,128)(2,1)S(1)}, u32[]{:S(2)}, u32[]{:S(2)}) collective-permute-start(bf16[80,640]{1,0:T(8,128)(2,1)} %get-tuple-element.195), channel_id=1, source_target_pairs={{4,0},{0,4},{12,8},{8,12},{20,16},{16,20},{28,24},{24,28},{5,1},{1... | collective-permute-start | bytes 307208 | tf_op jit(solution)/shard_map/ppermute | solution.py:1393
  (43 other events, 294.1 us)

commit v2 on v1

--- a/solution.py
+++ b/solution.py
@@ -669,8 +669,8 @@
         grad_mid = go + norm_back(grad * gain_ref[...], normed, inv_std)
         low = grad_mid.astype(BF16)
         do_ref[...] = dot_nt(low, wo_ref[...]).astype(BF16)
-        acc[0:split, :] += dot(att_ref[...].astype(F32).T.astype(BF16), low)
-        acc[split:, :] += dot(last_ref[...].astype(F32).T.astype(BF16), low)
+        acc[0:split, :] += dot(att_ref[...].T, low)
+        acc[split:, :] += dot(last_ref[...].T, low)
 
         @pl.when(i < per_piece)
         def _():
@@ -768,9 +768,9 @@
             mean_t[j : j + 1, :] = jnp.sum(
                 both_t[j * head_dim : (j + 1) * head_dim, :], axis=0, keepdims=True
             )
-        query_t[...] = query.T.astype(BF16)
-        do_t[...] = upstream.T.astype(BF16)
-        key_t[...] = key.T.astype(BF16)
+        query_t[...] = qkv_ref[:, 0:LANES].T
+        do_t[...] = do_ref[...].T
+        key_t[...] = qkv_ref[:, LANES : 2 * LANES].T
         for j in range(live):
             mine = lane // head_dim == j
             km[j] = jnp.where(mine, key, 0.0).astype(BF16)
@@ -849,7 +849,7 @@
         def _(i):
             rows = pl.ds(pl.multiple_of(i * ROWS, ROWS), ROWS)
             normed, _ = norm_rows(x_ref[rows, :].astype(F32))
-            low_t[:, rows] = (normed * gain_ref[...] + shift_ref[...]).T.astype(BF16)
+            low_t[:, rows] = (normed * gain_ref[...] + shift_ref[...]).astype(BF16).T
 
         for t in range(tiles):
             cols = slice(t * tile_cols, (t + 1) * tile_cols)

time: 219 us -> 219 us (level)
  no operation moved by 1% of the time
where the time goes in v2:
time: 219 us; the launch traced here: 216 us
  Pallas kernels  120 us (55%)
  starting transfers between devices  56.7 us (26%)
  waiting for transfers between devices  25.3 us (12%)
  local copies, waits for them, and re-layouts  10.7 us (5%)
    pallas_call x30, Pallas kernels, run(): pl.pallas_call(inner, in_specs=specs + [ANY] * extra, out_specs=out_specs...  119 us
    ppermute x30, starting transfers between devices, swap(): return lax.ppermute(item, axis, [(i, i ^ distance) for i in range(size)])  30.7 us
    ppermute x14, starting transfers between devices, from_part(): return lax.ppermute(item, 'seq', pairs)  26 us
    ppermute x30, waiting for transfers between devices, swap(): return lax.ppermute(item, axis, [(i, i ^ distance) for i in range(size)])  20.7 us
    unnamed x95, local copies, waits for them, and re-layouts  9.21 us
    ppermute x14, waiting for transfers between devices, from_part(): return lax.ppermute(item, 'seq', pairs)  4.56 us
  transfers between devices with their start and end apart: 44, of which 11 were waited for; matrix products, arithmetic and copies ran while one was open for 2% of the time, Pallas kernels for 46%

profile of v2, /device:TPU:9, one launch (start us, length us, event | category | flops | bytes accessed | tf_op | source)
XLA Modules:
  0.0 216.3 jit_solution(13883701763093536324)
XLA Ops:
  0.7 1.2 copy-done.17
  2.0 2.5 %collective-permute-start.1 = (bf16[128,640]{1,0:T(8,128)(2,1)S(1)}, bf16[128,640]{1,0:T(8,128)(2,1)S(1)}, u32[]{:S(2)}, u32[]{:S(2)}) collective-permute-start(bf16[128,640]{1,0:T(8,128)(2,1)S(1)} %get-tuple-element.108), channel_id=1, source_target_pairs={{0,16},{4,20},{8,24},{12,28},{16,0},{20,4},{24,8},{28,12},{1,17},{... | collective-permute-start | bytes 491528 | tf_op jit(solution)/shard_map/ppermute | solution.py:161
  4.6 1.5 collective-permute-start.3
  6.8 1.2 broadcast_select_fusion
  8.1 1.6 collective-permute-start.4
  9.7 1.9 collective-permute-done.1.refs_2_
  11.6 5.6 %collective-permute-start.5 = (bf16[128,640]{1,0:T(8,128)(2,1)S(1)}, bf16[128,640]{1,0:T(8,128)(2,1)S(1)}, u32[]{:S(2)}, u32[]{:S(2)}) collective-permute-start(bf16[128,640]{1,0:T(8,128)(2,1)S(1)} %collective-permute-done.1.refs_2_), channel_id=1, source_target_pairs={{4,0},{0,4},{12,8},{8,12},{20,16},{16,20},{28,24},{24,28},{5,1},{1... | collective-permute-start | bytes 491528 | tf_op jit(solution)/shard_map/ppermute | solution.py:1393
  17.2 1.4 collective-permute-done.2.refs_3_
  18.5 1.8 collective-permute-start.6
  20.7 1.7 copy-done.2
  23.7 2.5 %collective-permute-start.8 = (bf16[144,640]{1,0:T(8,128)(2,1)S(1)}, bf16[144,640]{1,0:T(8,128)(2,1)S(1)}, u32[]{:S(2)}, u32[]{:S(2)}) collective-permute-start(bf16[144,640]{1,0:T(8,128)(2,1)S(1)} %get-tuple-element.117), channel_id=1, source_target_pairs={{0,16},{4,20},{8,24},{12,28},{16,0},{20,4},{24,8},{28,12},{1,17},{... | collective-permute-start | bytes 552968 | tf_op jit(solution)/shard_map/ppermute | solution.py:161
  26.4 15.9 %attend_first.1 = (bf16[1024,640]{1,0:T(8,128)(2,1)S(1)}, bf16[1024,1152]{1,0:T(8,128)(2,1)S(1)}, bf16[1024,256]{1,0:T(8,128)(2,1)S(1)}, f32[1024,128]{1,0:T(8,128)S(1)}) custom-call(bf16[128,640]{1,0:T(8,128)(2,1)S(1)} %get-tuple-element.106.refs_0_, bf16[128,640]{1,0:T(8,128)(2,1)S(1)} %collective-permute-done.refs_1_, ...), custom_call_target="tpu_custom_call" | custom-call | flops 12247367680 | bytes 8388608 | tf_op jit(solution)/shard_map/attend_first/pallas_call | solution.py:70
  44.1 3.1 %attend_last.1 = (bf16[1024,128]{1,0:T(8,128)(2,1)S(1)}, f32[1024,128]{1,0:T(8,128)S(1)}) custom-call(bf16[1024,1152]{1,0:T(8,128)(2,1)S(1)} %get-tuple-element.114.refs_0_, bf16[4,144,640]{2,1,0:T(8,128)(2,1)S(1)} %stack.1.refs_1_), custom_call_target="tpu_custom_call" | custom-call | flops 2147483648 | bytes 2097152 | tf_op jit(solution)/shard_map/attend_last/pallas_call | solution.py:70
  49.7 16.8 %feed_first.1 = (f32[1024,640]{1,0:T(8,128)}, bf16[1024,640]{1,0:T(8,128)(2,1)S(1)}, bf16[640,1024]{1,0:T(8,128)(2,1)S(1)}, bf16[1024,640]{1,0:T(8,128)(2,1)S(1)...) custom-call(bf16[1024,640]{1,0:T(8,128)(2,1)S(1)} %get-tuple-element, ...), custom_call_target="tpu_custom_call" | custom-call | flops 8053063680 | bytes 25165824 | tf_op jit(solution)/shard_map/feed_first/pallas_call | solution.py:70
  67.1 1.2 collective-permute-start.15
  68.3 1.2 collective-permute-start.16
  69.6 22.2 %feed_second.1 = (f32[512,640]{1,0:T(8,128)S(1)}, bf16[1024,640]{1,0:T(8,128)(2,1)S(1)}, f32[8,1536]{1,0:T(8,128)S(1)}, bf16[512,640]{1,0:T(8,128)(2,1)}, bf16[2...) custom-call(bf16[1024,640]{1,0:T(8,128)(2,1)S(1)} %get-tuple-element, ...), custom_call_target="tpu_custom_call" | custom-call | flops 12079595520 | bytes 25165824 | tf_op jit(solution)/shard_map/feed_second/pallas_call | solution.py:70
  91.9 1.8 sum_first.2
  93.8 1.0 collective-permute-start.17
  95.9 1.7 collective-permute-done.17.refs_2_
  97.7 7.1 %mid_back.1 = (f32[512,640]{1,0:T(8,128)S(1)}, bf16[1024,384]{1,0:T(8,128)(2,1)S(1)}, f32[8,640]{1,0:T(8,128)S(1)}, bf16[2,80,640]{2,1,0:T(8,128)(2,1)}, bf16[2,80,640]{2,1,0:T(8,128)(2,1)}) custom-call(f32[1024,640]{1,0:T(8,128)} %get-tuple-element.134.refs_0_, bf16[1024,640]{1,0:T(8,128)(2,1)} %gate.2.refs_1_, ...), custom_call_target="tpu_custom_call" | custom-call | flops 1006632960 | bytes 14680064 | tf_op jit(solution)/shard_map/mid_back/pallas_call | solution.py:70
  106.7 1.6 finish_result.1
  108.4 1.4 collective-permute-start.21
  109.9 1.7 copy-done.4
  111.5 12.1 %attend_backward.3.refs_2_.refs_4_.refs_3_.refs_5_ = bf16[1024,384]{1,0:T(8,128)(2,1)S(1)} custom-call(bf16[1024,1152]{1,0:T(8,128)(2,1)S(1)} %copy-done.4, bf16[1024,384]{1,0:T(8,128)(2,1)S(1)} %get-tuple-element.141.refs_1_, bf16[1024,256]{1,0:T(8,128)(2,1)S(1)} %copy-done.6, f32[1024,128]{1,0:T(8,128)S(1)} %get-tuple-element.119.refs_4_.refs_3_, ...), custom_call_target="tpu_custom_call" | custom-call | flops 167772160 | bytes 49152 | tf_op jit(solution)/shard_map/attend_backward/pallas_call | solution.py:70
  123.7 1.2 collective-permute-start.20
  124.8 2.3 %collective-permute-start.27 = (bf16[2,80,640]{2,1,0:T(8,128)(2,1)S(1)}, bf16[2,80,640]{2,1,0:T(8,128)(2,1)S(1)}, u32[]{:S(2)}, u32[]{:S(2)}) collective-permute-start(bf16[2,80,640]{2,1,0:T(8,128)(2,1)S(1)} %copy-done.46), channel_id=1, source_target_pairs={{4,0},{0,4},{12,8},{8,12},{20,16},{16,20},{28,24},{24,28},{5,1},{1... | collective-permute-start | bytes 614408 | tf_op jit(solution)/shard_map/ppermute | solution.py:1393
  127.2 1.6 collective-permute-start.26
  128.8 1.1 sum_first.3
  130.2 1.2 collective-permute-start.25
  131.4 1.0 copy-done.20
  132.4 12.3 %attend_backward.4.refs_4_.refs_6_ = bf16[1024,384]{1,0:T(8,128)(2,1)S(1)} custom-call(bf16[1024,1152]{1,0:T(8,128)(2,1)S(1)} %copy-done.4, bf16[1024,384]{1,0:T(8,128)(2,1)S(1)} %get-tuple-element.141.refs_1_, bf16[1024,256]{1,0:T(8,128)(2,1)S(1)} %copy-done.6, f32[1024,128]{1,0:T(8,128)S(1)} %get-tuple-element.119.refs_4_.refs_3_, ...), custom_call_target="tpu_custom_call" | custom-call | flops 10737418240 | bytes 3145728 | tf_op jit(solution)/shard_map/attend_backward/pallas_call | solution.py:70
  144.8 1.1 sum_second.3
  146.1 1.1 copy-done.22
  147.2 6.5 %attend_backward.5.refs_5_.refs_7_ = bf16[1024,384]{1,0:T(8,128)(2,1)S(1)} custom-call(bf16[1024,1152]{1,0:T(8,128)(2,1)S(1)} %copy-done.4, bf16[1024,384]{1,0:T(8,128)(2,1)S(1)} %get-tuple-element.141.refs_1_, bf16[1024,128]{1,0:T(8,128)(2,1)S(1)} %copy-done.27, f32[1024,128]{1,0:T(8,128)S(1)} %copy-done.35, bf16[2,2,160,384]{3,2,1,0:T(8,128)(2,1)S(1)} %copy-done.22, ...), custom_call_target="tpu_custom_call" | custom-call | flops 5368709120 | bytes 3145728 | tf_op jit(solution)/shard_map/attend_backward/pallas_call | solution.py:70
  153.8 4.1 %project_weights.1 = (bf16[4,80,1152]{2,1,0:T(8,128)(2,1)S(1)}, bf16[4,80,1152]{2,1,0:T(8,128)(2,1)S(1)}) custom-call(bf16[1024,640]{1,0:T(8,128)(2,1)S(1)} %copy-done.9, f32[1,640]{1,0:T(1,128)S(1)} %broadcast_in_dim.49.refs_8_.refs_1_, f32[1,640]{1,0:T(1,128)S(1)} %broadcast_in_dim.50.refs_9_.refs_2_, ...), custom_call_target="tpu_custom_call" | custom-call | flops 1509949440 | bytes 6291456 | tf_op jit(solution)/shard_map/project_weights/pallas_call | solution.py:70
  158.0 2.5 %collective-permute-start.28 = (bf16[4,80,1152]{2,1,0:T(8,128)(2,1)S(1)}, bf16[4,80,1152]{2,1,0:T(8,128)(2,1)S(1)}, u32[]{:S(2)}, u32[]{:S(2)}) collective-permute-start(bf16[4,80,1152]{2,1,0:T(8,128)(2,1)S(1)} %get-tuple-element.164), channel_id=1, source_target_pairs={{4,0},{0,4},{12,8},{8,12},{20,16},{16,20},{28,24},{24,28},{5,1},{1... | collective-permute-start | bytes 2211848 | tf_op jit(solution)/shard_map/ppermute | solution.py:1393
  160.6 4.2 %project_rows.1 = (f32[512,640]{1,0:T(8,128)S(1)}, bf16[512,640]{1,0:T(8,128)(2,1)S(1)}, f32[16,640]{1,0:T(8,128)S(1)}, f32[8,1152]{1,0:T(8,128)}) custom-call(bf16[1024,640]{1,0:T(8,128)(2,1)S(1)} %copy-done.9, bf16[640,1152]{1,0:T(8,128)(2,1)S(1)} %copy-done.30, f32[8,640]{1,0:T(8,128)S(1)} %get-tuple-element.166.refs_2_, f32[8,1024]{1,0:T(8,128)S(1)} %copy-done.33, ...), custom_call_target="tpu_custom_call" | custom-call | flops 1509949440 | bytes 8388608 | tf_op jit(solution)/shard_map/project_rows/pallas_call | solution.py:70
  164.8 1.1 collective-permute-start.33
  165.8 1.8 collective-permute-done.30.refs_5_
  169.7 2.7 %collective-permute-start.35 = (bf16[2,160,384]{2,1,0:T(8,128)(2,1)S(1)}, bf16[2,160,384]{2,1,0:T(8,128)(2,1)S(1)}, u32[]{:S(2)}, u32[]{:S(2)}) collective-permute-start(bf16[2,160,384]{2,1,0:T(8,128)(2,1)S(1)} %get-tuple-element.180), channel_id=1, source_target_pairs={{0,16},{4,20},{8,24},{12,28},{16,0},{20,4},{24,8},{28,12},{1,17},{... | collective-permute-start | bytes 737288 | tf_op jit(solution)/shard_map/ppermute | solution.py:161
  173.5 9.4 %collective-permute-done.35.refs_6_.refs_3_ = bf16[2,160,384]{2,1,0:T(8,128)(2,1)S(1)} collective-permute-done((bf16[2,160,384]{2,1,0:T(8,128)(2,1)S(1)}, bf16[2,160,384]{2,1,0:T(8,128)(2,1)S(1)}, u32[]{:S(2)}, u32[]{:S(2)}) %collective-permute-start.35) | collective-permute-done | bytes 245792 | tf_op jit(solution)/shard_map/ppermute | solution.py:161
  183.8 1.2 collective-permute-start.37
  185.6 4.0 %collective-permute-start.39 = (bf16[128,640]{1,0:T(8,128)(2,1)S(1)}, bf16[128,640]{1,0:T(8,128)(2,1)S(1)}, u32[]{:S(2)}, u32[]{:S(2)}) collective-permute-start(bf16[128,640]{1,0:T(8,128)(2,1)S(1)} %get-tuple-element.187), channel_id=1, source_target_pairs={{0,16},{4,20},{8,24},{12,28},{16,0},{20,4},{24,8},{28,12},{1,17},{... | collective-permute-start | bytes 491528 | tf_op jit(solution)/shard_map/ppermute | solution.py:161
  190.9 3.9 %collective-permute-start.40 = (bf16[112,640]{1,0:T(8,128)(2,1)}, bf16[112,640]{1,0:T(8,128)(2,1)S(1)}, u32[]{:S(2)}, u32[]{:S(2)}) collective-permute-start(bf16[112,640]{1,0:T(8,128)(2,1)} %get-tuple-element.188), channel_id=1, source_target_pairs={{0,8},{4,12},{8,0},{12,4},{16,24},{20,28},{24,16},{28,20},{1,9},{5... | collective-permute-start | bytes 430088 | tf_op jit(solution)/shard_map/ppermute | solution.py:161
  197.0 6.8 %collective-permute-start.43 = (bf16[80,640]{1,0:T(8,128)(2,1)}, bf16[80,640]{1,0:T(8,128)(2,1)S(1)}, u32[]{:S(2)}, u32[]{:S(2)}) collective-permute-start(bf16[80,640]{1,0:T(8,128)(2,1)} %get-tuple-element.195), channel_id=1, source_target_pairs={{4,0},{0,4},{12,8},{8,12},{20,16},{16,20},{28,24},{24,28},{5,1},{1... | collective-permute-start | bytes 307208 | tf_op jit(solution)/shard_map/ppermute | solution.py:1393
  207.3 2.2 %collective-permute-done.41.refs_2_ = bf16[112,640]{1,0:T(8,128)(2,1)S(1)} collective-permute-done((bf16[112,640]{1,0:T(8,128)(2,1)}, bf16[112,640]{1,0:T(8,128)(2,1)S(1)}, u32[]{:S(2)}, u32[]{:S(2)}) %collective-permute-start.41) | collective-permute-done | bytes 143392 | tf_op jit(solution)/shard_map/ppermute | solution.py:161
  209.5 4.4 %collective-permute-done.42.refs_3_ = bf16[112,640]{1,0:T(8,128)(2,1)S(1)} collective-permute-done((bf16[112,640]{1,0:T(8,128)(2,1)S(1)}, bf16[112,640]{1,0:T(8,128)(2,1)S(1)}, u32[]{:S(2)}, u32[]{:S(2)}) %collective-permute-start.42) | collective-permute-done | bytes 143392 | tf_op jit(solution)/shard_map/ppermute | solution.py:161
  (188 shorter events, 25.0 us)
Async XLA Ops:
  1.9 6.2 %collective-permute-start = (bf16[128,640]{1,0:T(8,128)(2,1)S(1)}, bf16[128,640]{1,0:T(8,128)(2,1)S(1)}, u32[]{:S(2)}, u32[]{:S(2)}) collective-permute-start(bf16[128,640]{1,0:T(8,128)(2,1)S(1)} %get-tuple-element.107), channel_id=1, source_target_pairs={{0,8},{4,12},{8,0},{12,4},{16,24},{20,28},{24,16},{28,20},{1,9},{5... | collective-permute-start | bytes 491528 | tf_op jit(solution)/shard_map/ppermute | solution.py:161
  2.0 9.6 %collective-permute-start.1 = (bf16[128,640]{1,0:T(8,128)(2,1)S(1)}, bf16[128,640]{1,0:T(8,128)(2,1)S(1)}, u32[]{:S(2)}, u32[]{:S(2)}) collective-permute-start(bf16[128,640]{1,0:T(8,128)(2,1)S(1)} %get-tuple-element.108), channel_id=1, source_target_pairs={{0,16},{4,20},{8,24},{12,28},{16,0},{20,4},{24,8},{28,12},{1,17},{... | collective-permute-start | bytes 491528 | tf_op jit(solution)/shard_map/ppermute | solution.py:161
  4.5 14.1 %collective-permute-start.2 = (bf16[128,640]{1,0:T(8,128)(2,1)S(1)}, bf16[128,640]{1,0:T(8,128)(2,1)S(1)}, u32[]{:S(2)}, u32[]{:S(2)}) collective-permute-start(bf16[128,640]{1,0:T(8,128)(2,1)S(1)} %get-tuple-element.109), channel_id=1, source_target_pairs={{0,24},{4,28},{8,16},{12,20},{16,8},{20,12},{24,0},{28,4},{1,25},{... | collective-permute-start | bytes 491528 | tf_op jit(solution)/shard_map/ppermute | solution.py:161
  4.6 18.9 %collective-permute-start.3 = (bf16[128,640]{1,0:T(8,128)(2,1)S(1)}, bf16[128,640]{1,0:T(8,128)(2,1)S(1)}, u32[]{:S(2)}, u32[]{:S(2)}) collective-permute-start(bf16[128,640]{1,0:T(8,128)(2,1)S(1)} %get-tuple-element.106.refs_0_), channel_id=1, source_target_pairs={{4,0},{0,4},{12,8},{8,12},{20,16},{16,20},{28,24},{24,28},{5,1},{1... | collective-permute-start | bytes 491528 | tf_op jit(solution)/shard_map/ppermute | solution.py:1393
  8.1 15.5 %collective-permute-start.4 = (bf16[128,640]{1,0:T(8,128)(2,1)S(1)}, bf16[128,640]{1,0:T(8,128)(2,1)S(1)}, u32[]{:S(2)}, u32[]{:S(2)}) collective-permute-start(bf16[128,640]{1,0:T(8,128)(2,1)S(1)} %collective-permute-done.refs_1_), channel_id=1, source_target_pairs={{4,0},{0,4},{12,8},{8,12},{20,16},{16,20},{28,24},{24,28},{5,1},{1... | collective-permute-start | bytes 491528 | tf_op jit(solution)/shard_map/ppermute | solution.py:1393
  11.6 11.9 %collective-permute-start.5 = (bf16[128,640]{1,0:T(8,128)(2,1)S(1)}, bf16[128,640]{1,0:T(8,128)(2,1)S(1)}, u32[]{:S(2)}, u32[]{:S(2)}) collective-permute-start(bf16[128,640]{1,0:T(8,128)(2,1)S(1)} %collective-permute-done.1.refs_2_), channel_id=1, source_target_pairs={{4,0},{0,4},{12,8},{8,12},{20,16},{16,20},{28,24},{24,28},{5,1},{1... | collective-permute-start | bytes 491528 | tf_op jit(solution)/shard_map/ppermute | solution.py:1393
  18.5 5.0 %collective-permute-start.6 = (bf16[128,640]{1,0:T(8,128)(2,1)S(1)}, bf16[128,640]{1,0:T(8,128)(2,1)S(1)}, u32[]{:S(2)}, u32[]{:S(2)}) collective-permute-start(bf16[128,640]{1,0:T(8,128)(2,1)S(1)} %collective-permute-done.2.refs_3_), channel_id=1, source_target_pairs={{4,0},{0,4},{12,8},{8,12},{20,16},{16,20},{28,24},{24,28},{5,1},{1... | collective-permute-start | bytes 491528 | tf_op jit(solution)/shard_map/ppermute | solution.py:1393
  23.4 26.2 %copy-start.18 = (bf16[384,640]{1,0:T(8,128)(2,1)}, bf16[384,640]{1,0:T(8,128)(2,1)S(1)}, u32[]{:S(2)}) copy-start(bf16[384,640]{1,0:T(8,128)(2,1)S(1)} %get-tuple-element.121.refs_13_.refs_5_) | copy-start | bytes 1474564
  23.7 18.6 %collective-permute-start.7 = (bf16[144,640]{1,0:T(8,128)(2,1)S(1)}, bf16[144,640]{1,0:T(8,128)(2,1)S(1)}, u32[]{:S(2)}, u32[]{:S(2)}) collective-permute-start(bf16[144,640]{1,0:T(8,128)(2,1)S(1)} %get-tuple-element.116), channel_id=1, source_target_pairs={{0,8},{4,12},{8,0},{12,4},{16,24},{20,28},{24,16},{28,20},{1,9},{5... | collective-permute-start | bytes 552968 | tf_op jit(solution)/shard_map/ppermute | solution.py:161
  23.7 18.6 %collective-permute-start.8 = (bf16[144,640]{1,0:T(8,128)(2,1)S(1)}, bf16[144,640]{1,0:T(8,128)(2,1)S(1)}, u32[]{:S(2)}, u32[]{:S(2)}) collective-permute-start(bf16[144,640]{1,0:T(8,128)(2,1)S(1)} %get-tuple-element.117), channel_id=1, source_target_pairs={{0,16},{4,20},{8,24},{12,28},{16,0},{20,4},{24,8},{28,12},{1,17},{... | collective-permute-start | bytes 552968 | tf_op jit(solution)/shard_map/ppermute | solution.py:161
  26.2 17.0 %collective-permute-start.9 = (bf16[144,640]{1,0:T(8,128)(2,1)S(1)}, bf16[144,640]{1,0:T(8,128)(2,1)S(1)}, u32[]{:S(2)}, u32[]{:S(2)}) collective-permute-start(bf16[144,640]{1,0:T(8,128)(2,1)S(1)} %get-tuple-element.118), channel_id=1, source_target_pairs={{0,24},{4,28},{8,16},{12,20},{16,8},{20,12},{24,0},{28,4},{1,25},{... | collective-permute-start | bytes 552968 | tf_op jit(solution)/shard_map/ppermute | solution.py:161
  43.3 5.2 %collective-permute-start.12 = (bf16[4,144,640]{2,1,0:T(8,128)(2,1)S(1)}, bf16[4,144,640]{2,1,0:T(8,128)(2,1)S(1)}, u32[]{:S(2)}, u32[]{:S(2)}) collective-permute-start(bf16[4,144,640]{2,1,0:T(8,128)(2,1)S(1)} %stack.1.refs_1_), channel_id=1, source_target_pairs={{4,0},{0,4},{12,8},{8,12},{20,16},{16,20},{28,24},{24,28},{5,1},{1... | collective-permute-start | bytes 2211848 | tf_op jit(solution)/shard_map/ppermute | solution.py:1393
  44.0 5.6 %collective-permute-start.10 = (bf16[1024,256]{1,0:T(8,128)(2,1)S(1)}, bf16[1024,256]{1,0:T(8,128)(2,1)S(1)}, u32[]{:S(2)}, u32[]{:S(2)}) collective-permute-start(bf16[1024,256]{1,0:T(8,128)(2,1)S(1)} %get-tuple-element.113.refs_1_.refs_6_.refs_2_), channel_id=1, source_target_pairs={{4,0},{0,4},{12,8},{8,12},{20,16},{16,20},{28,24},{24,28},{5,1},{1... | collective-permute-start | bytes 1572872 | tf_op jit(solution)/shard_map/ppermute | solution.py:1393
  48.0 1.6 collective-permute-start.11
  67.1 24.7 %copy-start.10 = (bf16[1024,640]{1,0:T(8,128)(2,1)}, bf16[1024,640]{1,0:T(8,128)(2,1)S(1)}, u32[]{:S(2)}) copy-start(bf16[1024,640]{1,0:T(8,128)(2,1)S(1)} %get-tuple-element.125.refs_2_.refs_3_) | copy-start | bytes 3932164
  67.1 24.7 %collective-permute-start.15 = (bf16[2,4,160,256]{3,2,1,0:T(8,128)(2,1)}, bf16[2,4,160,256]{3,2,1,0:T(8,128)(2,1)S(1)}, u32[]{:S(2)}, u32[]{:S(2)}) collective-permute-start(bf16[2,4,160,256]{3,2,1,0:T(8,128)(2,1)} %get-tuple-element.138), channel_id=1, source_target_pairs={{0,1},{1,0},{2,3},{3,2},{4,5},{5,4},{6,7},{7,6},{8,9},{9,8},{10,11... | collective-permute-start | bytes 1966088 | tf_op jit(solution)/shard_map/ppermute | solution.py:161
  68.3 23.5 %collective-permute-start.16 = (bf16[2,4,160,256]{3,2,1,0:T(8,128)(2,1)}, bf16[2,4,160,256]{3,2,1,0:T(8,128)(2,1)S(1)}, u32[]{:S(2)}, u32[]{:S(2)}) collective-permute-start(bf16[2,4,160,256]{3,2,1,0:T(8,128)(2,1)} %get-tuple-element.139), channel_id=1, source_target_pairs={{0,2},{1,3},{2,0},{3,1},{4,6},{5,7},{6,4},{7,5},{8,10},{9,11},{10,... | collective-permute-start | bytes 1966088 | tf_op jit(solution)/shard_map/ppermute | solution.py:161
  69.6 22.3 %copy-start.15 = (bf16[2,4,160,256]{3,2,1,0:T(8,128)(2,1)S(1)}, bf16[2,4,160,256]{3,2,1,0:T(8,128)(2,1)}, u32[]{:S(2)}) copy-start(bf16[2,4,160,256]{3,2,1,0:T(8,128)(2,1)} %get-tuple-element.136.refs_0_) | copy-start | bytes 1966084
  69.6 22.3 %copy-start.16 = (bf16[2,4,160,256]{3,2,1,0:T(8,128)(2,1)S(1)}, bf16[2,4,160,256]{3,2,1,0:T(8,128)(2,1)}, u32[]{:S(2)}) copy-start(bf16[2,4,160,256]{3,2,1,0:T(8,128)(2,1)} %get-tuple-element.137.refs_1_) | copy-start | bytes 1966084
  93.8 3.9 %collective-permute-start.17 = (bf16[1024,640]{1,0:T(8,128)(2,1)}, bf16[1024,640]{1,0:T(8,128)(2,1)S(1)}, u32[]{:S(2)}, u32[]{:S(2)}) collective-permute-start(bf16[1024,640]{1,0:T(8,128)(2,1)} %gate.2.refs_1_), channel_id=1, source_target_pairs={{4,0},{0,4},{12,8},{8,12},{20,16},{16,20},{28,24},{24,28},{5,1},{1... | collective-permute-start | bytes 3932168 | tf_op jit(solution)/shard_map/ppermute | solution.py:1393
  94.8 9.9 %collective-permute-start.18 = (bf16[4,160,256]{2,1,0:T(8,128)(2,1)}, bf16[4,160,256]{2,1,0:T(8,128)(2,1)S(1)}, u32[]{:S(2)}, u32[]{:S(2)}) collective-permute-start(bf16[4,160,256]{2,1,0:T(8,128)(2,1)} %get-tuple-element.143), channel_id=1, source_target_pairs={{0,2},{1,3},{2,0},{3,1},{4,6},{5,7},{6,4},{7,5},{8,10},{9,11},{10,... | collective-permute-start | bytes 983048 | tf_op jit(solution)/shard_map/ppermute | solution.py:161
  95.0 9.7 %collective-permute-start.19 = (bf16[4,160,256]{2,1,0:T(8,128)(2,1)}, bf16[4,160,256]{2,1,0:T(8,128)(2,1)S(1)}, u32[]{:S(2)}, u32[]{:S(2)}) collective-permute-start(bf16[4,160,256]{2,1,0:T(8,128)(2,1)} %get-tuple-element.144), channel_id=1, source_target_pairs={{0,1},{1,0},{2,3},{3,2},{4,5},{5,4},{6,7},{7,6},{8,9},{9,8},{10,11... | collective-permute-start | bytes 983048 | tf_op jit(solution)/shard_map/ppermute | solution.py:161
  95.3 11.4 %collective-permute-start.13 = (bf16[512,640]{1,0:T(8,128)(2,1)}, bf16[512,640]{1,0:T(8,128)(2,1)}, u32[]{:S(2)}, u32[]{:S(2)}) collective-permute-start(bf16[512,640]{1,0:T(8,128)(2,1)} %get-tuple-element.131), channel_id=1, source_target_pairs={{4,0},{0,4},{12,8},{8,12},{20,16},{16,20},{28,24},{24,28},{5,1},{1... | collective-permute-start | bytes 1966088 | tf_op jit(solution)/shard_map/ppermute | solution.py:1393
  105.7 23.1 %collective-permute-start.22 = (bf16[2,4,160,384]{3,2,1,0:T(8,128)(2,1)}, bf16[2,4,160,384]{3,2,1,0:T(8,128)(2,1)S(1)}, u32[]{:S(2)}, u32[]{:S(2)}) collective-permute-start(bf16[2,4,160,384]{3,2,1,0:T(8,128)(2,1)} %get-tuple-element.153), channel_id=1, source_target_pairs={{0,1},{1,0},{2,3},{3,2},{4,5},{5,4},{6,7},{7,6},{8,9},{9,8},{10,11... | collective-permute-start | bytes 2949128 | tf_op jit(solution)/shard_map/ppermute | solution.py:161
  106.0 22.8 %collective-permute-start.23 = (bf16[2,4,160,384]{3,2,1,0:T(8,128)(2,1)}, bf16[2,4,160,384]{3,2,1,0:T(8,128)(2,1)S(1)}, u32[]{:S(2)}, u32[]{:S(2)}) collective-permute-start(bf16[2,4,160,384]{3,2,1,0:T(8,128)(2,1)} %get-tuple-element.154), channel_id=1, source_target_pairs={{0,2},{1,3},{2,0},{3,1},{4,6},{5,7},{6,4},{7,5},{8,10},{9,11},{10,... | collective-permute-start | bytes 2949128 | tf_op jit(solution)/shard_map/ppermute | solution.py:161
  108.3 15.3 %collective-permute-start.14 = (bf16[2,128,640]{2,1,0:T(8,128)(2,1)S(1)}, bf16[2,128,640]{2,1,0:T(8,128)(2,1)S(1)}, u32[]{:S(2)}, u32[]{:S(2)}) collective-permute-start(bf16[2,128,640]{2,1,0:T(8,128)(2,1)S(1)} %get-tuple-element.133), channel_id=1, source_target_pairs={{0,8},{4,12},{8,0},{12,4},{16,24},{20,28},{24,16},{28,20},{1,9},{5... | collective-permute-start | bytes 983048 | tf_op jit(solution)/shard_map/ppermute | solution.py:161
  108.4 18.7 %collective-permute-start.21 = (bf16[2,2,160,256]{3,2,1,0:T(8,128)(2,1)S(1)}, bf16[2,2,160,256]{3,2,1,0:T(8,128)(2,1)S(1)}, u32[]{:S(2)}, u32[]{:S(2)}) collective-permute-start(bf16[2,2,160,256]{3,2,1,0:T(8,128)(2,1)S(1)} %copy-done.45), channel_id=1, source_target_pairs={{0,8},{4,12},{8,0},{12,4},{16,24},{20,28},{24,16},{28,20},{1,9},{5... | collective-permute-start | bytes 983048 | tf_op jit(solution)/shard_map/ppermute | solution.py:161
  123.7 22.4 %collective-permute-start.20 = (bf16[2,128,640]{2,1,0:T(8,128)(2,1)S(1)}, bf16[2,128,640]{2,1,0:T(8,128)(2,1)S(1)}, u32[]{:S(2)}, u32[]{:S(2)}) collective-permute-start(bf16[2,128,640]{2,1,0:T(8,128)(2,1)S(1)} %pass_on.1.refs_4_), channel_id=1, source_target_pairs={{0,16},{4,20},{8,24},{12,28},{16,0},{20,4},{24,8},{28,12},{1,17},{... | collective-permute-start | bytes 983048 | tf_op jit(solution)/shard_map/ppermute | solution.py:161
  124.8 28.9 %collective-permute-start.27 = (bf16[2,80,640]{2,1,0:T(8,128)(2,1)S(1)}, bf16[2,80,640]{2,1,0:T(8,128)(2,1)S(1)}, u32[]{:S(2)}, u32[]{:S(2)}) collective-permute-start(bf16[2,80,640]{2,1,0:T(8,128)(2,1)S(1)} %copy-done.46), channel_id=1, source_target_pairs={{4,0},{0,4},{12,8},{8,12},{20,16},{16,20},{28,24},{24,28},{5,1},{1... | collective-permute-start | bytes 614408 | tf_op jit(solution)/shard_map/ppermute | solution.py:1393
  127.2 18.9 %collective-permute-start.26 = (bf16[2,160,256]{2,1,0:T(8,128)(2,1)S(1)}, bf16[2,160,256]{2,1,0:T(8,128)(2,1)S(1)}, u32[]{:S(2)}, u32[]{:S(2)}) collective-permute-start(bf16[2,160,256]{2,1,0:T(8,128)(2,1)S(1)} %get-tuple-element.161), channel_id=1, source_target_pairs={{0,16},{4,20},{8,24},{12,28},{16,0},{20,4},{24,8},{28,12},{1,17},{... | collective-permute-start | bytes 491528 | tf_op jit(solution)/shard_map/ppermute | solution.py:161
  130.0 14.8 %collective-permute-start.24 = (bf16[4,160,384]{2,1,0:T(8,128)(2,1)S(1)}, bf16[4,160,384]{2,1,0:T(8,128)(2,1)S(1)}, u32[]{:S(2)}, u32[]{:S(2)}) collective-permute-start(bf16[4,160,384]{2,1,0:T(8,128)(2,1)S(1)} %get-tuple-element.158), channel_id=1, source_target_pairs={{0,2},{1,3},{2,0},{3,1},{4,6},{5,7},{6,4},{7,5},{8,10},{9,11},{10,... | collective-permute-start | bytes 1474568 | tf_op jit(solution)/shard_map/ppermute | solution.py:161
  130.2 14.6 %collective-permute-start.25 = (bf16[4,160,384]{2,1,0:T(8,128)(2,1)S(1)}, bf16[4,160,384]{2,1,0:T(8,128)(2,1)S(1)}, u32[]{:S(2)}, u32[]{:S(2)}) collective-permute-start(bf16[4,160,384]{2,1,0:T(8,128)(2,1)S(1)} %get-tuple-element.159), channel_id=1, source_target_pairs={{0,1},{1,0},{2,3},{3,2},{4,5},{5,4},{6,7},{7,6},{8,9},{9,8},{10,11... | collective-permute-start | bytes 1474568 | tf_op jit(solution)/shard_map/ppermute | solution.py:161
  145.9 14.5 %collective-permute-start.29 = (bf16[2,2,160,384]{3,2,1,0:T(8,128)(2,1)}, bf16[2,2,160,384]{3,2,1,0:T(8,128)(2,1)S(1)}, u32[]{:S(2)}, u32[]{:S(2)}) collective-permute-start(bf16[2,2,160,384]{3,2,1,0:T(8,128)(2,1)} %get-tuple-element.169), channel_id=1, source_target_pairs={{0,8},{4,12},{8,0},{12,4},{16,24},{20,28},{24,16},{28,20},{1,9},{5... | collective-permute-start | bytes 1474568 | tf_op jit(solution)/shard_map/ppermute | solution.py:161
  158.0 9.7 %collective-permute-start.28 = (bf16[4,80,1152]{2,1,0:T(8,128)(2,1)S(1)}, bf16[4,80,1152]{2,1,0:T(8,128)(2,1)S(1)}, u32[]{:S(2)}, u32[]{:S(2)}) collective-permute-start(bf16[4,80,1152]{2,1,0:T(8,128)(2,1)S(1)} %get-tuple-element.164), channel_id=1, source_target_pairs={{4,0},{0,4},{12,8},{8,12},{20,16},{16,20},{28,24},{24,28},{5,1},{1... | collective-permute-start | bytes 2211848 | tf_op jit(solution)/shard_map/ppermute | solution.py:1393
  164.8 7.7 %collective-permute-start.33 = (bf16[512,640]{1,0:T(8,128)(2,1)S(1)}, bf16[512,640]{1,0:T(8,128)(2,1)S(1)}, u32[]{:S(2)}, u32[]{:S(2)}) collective-permute-start(bf16[512,640]{1,0:T(8,128)(2,1)S(1)} %get-tuple-element.177), channel_id=1, source_target_pairs={{4,0},{0,4},{12,8},{8,12},{20,16},{16,20},{28,24},{24,28},{5,1},{1... | collective-permute-start | bytes 1966088 | tf_op jit(solution)/shard_map/ppermute | solution.py:1393
  165.8 1.8 collective-permute-start.30
  168.6 14.3 %collective-permute-start.31 = (bf16[352,640]{1,0:T(8,128)(2,1)S(1)}, bf16[352,640]{1,0:T(8,128)(2,1)S(1)}, u32[]{:S(2)}, u32[]{:S(2)}) collective-permute-start(bf16[352,640]{1,0:T(8,128)(2,1)S(1)} %get-tuple-element.174), channel_id=1, source_target_pairs={{0,1},{1,0},{2,3},{3,2},{4,5},{5,4},{6,7},{7,6},{8,9},{9,8},{10,11... | collective-permute-start | bytes 1351688 | tf_op jit(solution)/shard_map/ppermute | solution.py:161
  168.9 13.9 %collective-permute-start.32 = (bf16[320,640]{1,0:T(8,128)(2,1)S(1)}, bf16[320,640]{1,0:T(8,128)(2,1)S(1)}, u32[]{:S(2)}, u32[]{:S(2)}) collective-permute-start(bf16[320,640]{1,0:T(8,128)(2,1)S(1)} %get-tuple-element.175), channel_id=1, source_target_pairs={{0,2},{1,3},{2,0},{3,1},{4,6},{5,7},{6,4},{7,5},{8,10},{9,11},{10,... | collective-permute-start | bytes 1228808 | tf_op jit(solution)/shard_map/ppermute | solution.py:161
  169.7 13.1 %collective-permute-start.35 = (bf16[2,160,384]{2,1,0:T(8,128)(2,1)S(1)}, bf16[2,160,384]{2,1,0:T(8,128)(2,1)S(1)}, u32[]{:S(2)}, u32[]{:S(2)}) collective-permute-start(bf16[2,160,384]{2,1,0:T(8,128)(2,1)S(1)} %get-tuple-element.180), channel_id=1, source_target_pairs={{0,16},{4,20},{8,24},{12,28},{16,0},{20,4},{24,8},{28,12},{1,17},{... | collective-permute-start | bytes 737288 | tf_op jit(solution)/shard_map/ppermute | solution.py:161
  173.4 9.5 %collective-permute-start.34 = (bf16[128,640]{1,0:T(8,128)(2,1)S(1)}, bf16[128,640]{1,0:T(8,128)(2,1)S(1)}, u32[]{:S(2)}, u32[]{:S(2)}) collective-permute-start(bf16[128,640]{1,0:T(8,128)(2,1)S(1)} %get-tuple-element.179), channel_id=1, source_target_pairs={{0,8},{4,12},{8,0},{12,4},{16,24},{20,28},{24,16},{28,20},{1,9},{5... | collective-permute-start | bytes 491528 | tf_op jit(solution)/shard_map/ppermute | solution.py:161
  183.1 7.1 %collective-permute-start.36 = (bf16[192,640]{1,0:T(8,128)(2,1)S(1)}, bf16[192,640]{1,0:T(8,128)(2,1)S(1)}, u32[]{:S(2)}, u32[]{:S(2)}) collective-permute-start(bf16[192,640]{1,0:T(8,128)(2,1)S(1)} %get-tuple-element.183), channel_id=1, source_target_pairs={{0,2},{1,3},{2,0},{3,1},{4,6},{5,7},{6,4},{7,5},{8,10},{9,11},{10,... | collective-permute-start | bytes 737288 | tf_op jit(solution)/shard_map/ppermute | solution.py:161
  183.8 5.9 %collective-permute-start.37 = (bf16[160,640]{1,0:T(8,128)(2,1)S(1)}, bf16[160,640]{1,0:T(8,128)(2,1)S(1)}, u32[]{:S(2)}, u32[]{:S(2)}) collective-permute-start(bf16[160,640]{1,0:T(8,128)(2,1)S(1)} %get-tuple-element.184), channel_id=1, source_target_pairs={{0,1},{1,0},{2,3},{3,2},{4,5},{5,4},{6,7},{7,6},{8,9},{9,8},{10,11... | collective-permute-start | bytes 614408 | tf_op jit(solution)/shard_map/ppermute | solution.py:161
  185.1 4.6 %collective-permute-start.38 = (bf16[128,640]{1,0:T(8,128)(2,1)S(1)}, bf16[128,640]{1,0:T(8,128)(2,1)S(1)}, u32[]{:S(2)}, u32[]{:S(2)}) collective-permute-start(bf16[128,640]{1,0:T(8,128)(2,1)S(1)} %get-tuple-element.185), channel_id=1, source_target_pairs={{0,24},{4,28},{8,16},{12,20},{16,8},{20,12},{24,0},{28,4},{1,25},{... | collective-permute-start | bytes 491528 | tf_op jit(solution)/shard_map/ppermute | solution.py:161
  185.6 20.0 %collective-permute-start.39 = (bf16[128,640]{1,0:T(8,128)(2,1)S(1)}, bf16[128,640]{1,0:T(8,128)(2,1)S(1)}, u32[]{:S(2)}, u32[]{:S(2)}) collective-permute-start(bf16[128,640]{1,0:T(8,128)(2,1)S(1)} %get-tuple-element.187), channel_id=1, source_target_pairs={{0,16},{4,20},{8,24},{12,28},{16,0},{20,4},{24,8},{28,12},{1,17},{... | collective-permute-start | bytes 491528 | tf_op jit(solution)/shard_map/ppermute | solution.py:161
  190.9 16.4 %collective-permute-start.40 = (bf16[112,640]{1,0:T(8,128)(2,1)}, bf16[112,640]{1,0:T(8,128)(2,1)S(1)}, u32[]{:S(2)}, u32[]{:S(2)}) collective-permute-start(bf16[112,640]{1,0:T(8,128)(2,1)} %get-tuple-element.188), channel_id=1, source_target_pairs={{0,8},{4,12},{8,0},{12,4},{16,24},{20,28},{24,16},{28,20},{1,9},{5... | collective-permute-start | bytes 430088 | tf_op jit(solution)/shard_map/ppermute | solution.py:161
  194.8 14.7 %collective-permute-start.41 = (bf16[112,640]{1,0:T(8,128)(2,1)}, bf16[112,640]{1,0:T(8,128)(2,1)S(1)}, u32[]{:S(2)}, u32[]{:S(2)}) collective-permute-start(bf16[112,640]{1,0:T(8,128)(2,1)} %get-tuple-element.189), channel_id=1, source_target_pairs={{0,16},{4,20},{8,24},{12,28},{16,0},{20,4},{24,8},{28,12},{1,17},{... | collective-permute-start | bytes 430088 | tf_op jit(solution)/shard_map/ppermute | solution.py:161
  195.4 18.5 %collective-permute-start.42 = (bf16[112,640]{1,0:T(8,128)(2,1)S(1)}, bf16[112,640]{1,0:T(8,128)(2,1)S(1)}, u32[]{:S(2)}, u32[]{:S(2)}) collective-permute-start(bf16[112,640]{1,0:T(8,128)(2,1)S(1)} %get-tuple-element.190), channel_id=1, source_target_pairs={{0,24},{4,28},{8,16},{12,20},{16,8},{20,12},{24,0},{28,4},{1,25},{... | collective-permute-start | bytes 430088 | tf_op jit(solution)/shard_map/ppermute | solution.py:161
  197.0 9.6 %collective-permute-start.43 = (bf16[80,640]{1,0:T(8,128)(2,1)}, bf16[80,640]{1,0:T(8,128)(2,1)S(1)}, u32[]{:S(2)}, u32[]{:S(2)}) collective-permute-start(bf16[80,640]{1,0:T(8,128)(2,1)} %get-tuple-element.195), channel_id=1, source_target_pairs={{4,0},{0,4},{12,8},{8,12},{20,16},{16,20},{28,24},{24,28},{5,1},{1... | collective-permute-start | bytes 307208 | tf_op jit(solution)/shard_map/ppermute | solution.py:1393
  (43 other events, 293.9 us)
